TPU v7x, 512 devices: a whole 4x4x16 slice. The times are simulated.
512 devices in a mesh: gx: 32 (over z, core), gy: 16 (over y, x).
Axes of the slice: x: 4, y: 4, z: 16, core: 2. Of those that a mesh axis runs over, the one named last changes fastest.
Arguments:
- residual: float32 [3, 512, 256, 128], P(None, 'gx', 'gy'), may hold values from -6 to 6
- stiffness: float32 [512, 256], P('gx', 'gy'), may hold values from 0.5 to 2
- local_inverse: bfloat16 [32, 16, 1024, 1024], P('gx', 'gy'), as said below
- coarse_basis: bfloat16 [32, 16, 8, 1024], P('gx', 'gy'), may hold values from -0.5 to 0.5
- coarse_rows: bfloat16 [32, 16, 8, 4096], P('gx', 'gy'), as said below
- send_rows: int32 [32, 16, 4, 64], P('gx', 'gy'), may hold values from 0 to 767, as said below
- partition_map: int32 [512], replicated, may hold values from 0 to 511, as said below
Outputs:
- solution: float32 [3, 512, 256, 128], P(None, 'gx', 'gy')
- final: float32 [3, 512, 256, 128], P(None, 'gx', 'gy')
Inputs may be any that keep to these rules, and one draw needn't show every extreme that they name: `send_rows`: for each subdomain, the lists j = 0, 1 (lower and upper neighbour along gx) and j = 2, 3 (lower and upper neighbour along gy) each name 64 distinct owned rows, all of them in the two layers of cells nearest that neighbour. `partition_map`: A permutation of the device numbers. `coarse_rows`: with its columns put in device order through partition_map, the 4096-square matrix S is symmetric. `local_inverse`: each subdomain's block is symmetric.
All inputs are finite; a program needn't handle non-finite values.
Results may differ from a plain program's by a relative error of at most 0.0057.
Values may be sent and summed in bfloat16 or wider, within the bound.
No kernel may reach another device: no remote copies, remote signals or barrier semaphores. Data moves between devices by JAX's collectives and lax.ppermute only.
A program may use at most 64 MiB of HBM per device.

v0:
```python
import jax
import jax.numpy as jnp
from jax import lax
from jax.sharding import PartitionSpec as P


def with_halo(block, sides, width):
    for axis, dim in sides:
        count = lax.axis_size(axis)
        forward = [(i, i + 1) for i in range(count - 1)]
        backward = [(target, source) for source, target in forward]
        low = lax.ppermute(
            lax.slice_in_dim(block, block.shape[dim] - width, None, axis=dim), axis, forward
        )
        high = lax.ppermute(lax.slice_in_dim(block, 0, width, axis=dim), axis, backward)
        block = jnp.concatenate([low, block, high], axis=dim)
    return block


def trade_along_gx(pair):
    return with_halo(pair, (("gx", 0),), 1)


def trade_along_gy(pair):
    return with_halo(pair, (("gy", 0),), 1)


def operate(values, stiffness):
    padded = with_halo(values, (("gx", 1), ("gy", 2)), 1)
    beside = padded[:, 2:, 1:-1] + padded[:, :-2, 1:-1] + padded[:, 1:-1, 2:] + padded[:, 1:-1, :-2]
    return (4.0 + stiffness[None, :, :, None]) * values - beside


def coarse_solve(coarse_in, ordered):
    return jnp.dot(
        ordered,
        lax.all_gather(coarse_in, ("gx", "gy"), axis=0, tiled=True),
        preferred_element_type=jnp.float32,
    )


def precondition(values, inverse, basis_rows, row_lists, ordered):
    own_rows = values.reshape(-1, values.shape[-1])
    own_count = own_rows.shape[0]
    margin = row_lists.shape[1]
    outgoing = jnp.take(own_rows, row_lists, axis=0)
    from_gx = trade_along_gx(outgoing[0:2])
    from_gy = trade_along_gy(outgoing[2:4])
    subdomain = jnp.concatenate([own_rows, from_gx[0], from_gx[3], from_gy[0], from_gy[3]], axis=0)
    subdomain = subdomain.astype(jnp.bfloat16)
    coarse_in = jnp.dot(basis_rows, subdomain, preferred_element_type=jnp.float32).astype(
        jnp.bfloat16
    )
    coarse_out = coarse_solve(coarse_in, ordered).astype(jnp.bfloat16)
    patch = jnp.dot(inverse, subdomain, preferred_element_type=jnp.float32)
    patch = patch + lax.dot_general(
        basis_rows, coarse_out, (((0,), (0,)), ((), ())), preferred_element_type=jnp.float32
    )
    back_gx = trade_along_gx(
        jnp.stack(
            [
                patch[own_count : own_count + margin],
                patch[own_count + margin : own_count + 2 * margin],
            ]
        )
    )
    back_gy = trade_along_gy(
        jnp.stack(
            [
                patch[own_count + 2 * margin : own_count + 3 * margin],
                patch[own_count + 3 * margin :],
            ]
        )
    )
    update = patch[:own_count]
    update = update.at[row_lists[0]].add(back_gx[0])
    update = update.at[row_lists[1]].add(back_gx[3])
    update = update.at[row_lists[2]].add(back_gy[0])
    update = update.at[row_lists[3]].add(back_gy[3])
    return update.reshape(values.shape)


def per_device(
    residual, stiffness, local_inverse, coarse_basis, coarse_rows, send_rows, partition_map
):
    inverse = local_inverse[0, 0]
    basis_rows = coarse_basis[0, 0]
    row_lists = send_rows[0, 0]
    device_count = partition_map.shape[0]
    coarse_width = basis_rows.shape[0]
    stored = coarse_rows[0, 0].reshape(coarse_width, device_count, coarse_width)
    ordered = jnp.take(stored, partition_map, axis=1).reshape(
        coarse_width, device_count * coarse_width
    )
    first_pass = precondition(residual, inverse, basis_rows, row_lists, ordered)
    middle = residual - operate(first_pass, stiffness)
    second_pass = precondition(middle, inverse, basis_rows, row_lists, ordered)
    solution = first_pass + second_pass
    return (solution, residual - operate(solution, stiffness))


def solution(mesh):
    placed = (
        P(None, "gx", "gy", None),
        P("gx", "gy"),
        P("gx", "gy", None, None),
        P("gx", "gy", None, None),
        P("gx", "gy", None, None),
        P("gx", "gy", None, None),
        P(),
    )
    return jax.shard_map(
        per_device,
        mesh=mesh,
        in_specs=placed,
        out_specs=(P(None, "gx", "gy", None), P(None, "gx", "gy", None)),
        check_vma=False,
    )
```

profile of v0, /device:TPU:7, one launch (start us, length us, event | category | flops | bytes accessed | tf_op | source)
XLA Modules:
  0.0 482.3 jit_solution(15836216177516421753)
XLA Ops:
  11.4 4.1 collective-permute-start
  15.5 1.9 collective-permute-start.1
  17.4 3.1 collective-permute-start.2
  20.6 2.2 collective-permute-start.3
  23.8 3.3 collective-permute-done.3
  28.7 3.0 reshape_squeeze.3
  31.7 1.9 copy.29
  33.6 2.4 gather_fusion
  39.2 163.6 %all-gather.3.cloned.1.call-done = bf16[4096,128]{1,0:T(8,128)(2,1)} async-done(((bf16[8,128]{1,0:T(8,128)(2,1)}), bf16[4096,128]{1,0:T(8,128)(2,1)}) %all-gather.3.cloned.1.call-update) | async-done | bytes 1048592 | tf_op jit(solution)/shard_map/all_gather | solution.py:37
  206.1 3.0 collective-permute-start.4
  209.1 2.0 collective-permute-start.5
  211.0 3.2 collective-permute-start.6
  214.2 2.1 collective-permute-start.7
  218.3 4.2 collective-permute-done.7
  227.4 2.4 collective-permute-start.8
  229.8 3.7 collective-permute-start.9
  234.4 1.9 collective-permute-start.10
  236.4 5.5 %collective-permute-start.11 = (f32[3,18,1,128]{3,2,1,0:T(1,128)S(1)}, f32[3,18,1,128]{3,2,1,0:T(1,128)S(1)}, u32[]{:S(2)}, u32[]{:S(2)}) collective-permute-start(f32[3,18,1,128]{3,2,1,0:T(1,128)S(1)} %get-tuple-element.14), channel_id=1, source_target_pairs={{0,1},{1,2},{2,3},{3,4},{4,5},{5,6},{6,7},{7,8},{8,9},{9,10},{10,1... | collective-permute-start | bytes 82952 | tf_op jit(solution)/shard_map/ppermute | solution.py:12
  244.0 5.3 %collective-permute-start.12 = (bf16[1,64,128]{2,1,0:T(8,128)(2,1)S(1)}, bf16[1,64,128]{2,1,0:T(8,128)(2,1)S(1)}, u32[]{:S(2)}, u32[]{:S(2)}) collective-permute-start(bf16[1,64,128]{2,1,0:T(8,128)(2,1)S(1)} %get-tuple-element.22), channel_id=1, source_target_pairs={{0,16},{16,32},{32,48},{48,64},{64,80},{80,96},{96,112},{112,128},... | collective-permute-start | bytes 49160 | tf_op jit(solution)/shard_map/ppermute | solution.py:12
  249.4 1.9 collective-permute-start.13
  251.3 6.0 %collective-permute-start.14 = (bf16[1,64,128]{2,1,0:T(8,128)(2,1)S(1)}, bf16[1,64,128]{2,1,0:T(8,128)(2,1)S(1)}, u32[]{:S(2)}, u32[]{:S(2)}) collective-permute-start(bf16[1,64,128]{2,1,0:T(8,128)(2,1)S(1)} %get-tuple-element.20), channel_id=1, source_target_pairs={{0,1},{1,2},{2,3},{3,4},{4,5},{5,6},{6,7},{7,8},{8,9},{9,10},{10,1... | collective-permute-start | bytes 49160 | tf_op jit(solution)/shard_map/ppermute | solution.py:12
  257.4 1.9 collective-permute-start.15
  259.4 4.6 collective-permute-done.15
  265.4 168.4 %all-gather.5.cloned.1.call-done = bf16[4096,128]{1,0:T(8,128)(2,1)} async-done(((bf16[8,128]{1,0:T(8,128)(2,1)}), bf16[4096,128]{1,0:T(8,128)(2,1)}) %all-gather.5.cloned.1.call-update) | async-done | bytes 1048592 | tf_op jit(solution)/shard_map/all_gather | solution.py:37
  438.2 3.0 collective-permute-start.16
  441.2 1.9 collective-permute-start.17
  443.1 3.2 collective-permute-start.18
  446.3 2.1 collective-permute-start.19
  458.9 1.9 collective-permute-start.20
  460.8 4.3 collective-permute-start.21
  466.1 2.3 collective-permute-start.22
  468.5 5.0 %collective-permute-start.23 = (f32[3,18,1,128]{3,2,1,0:T(1,128)S(1)}, f32[3,18,1,128]{3,2,1,0:T(1,128)S(1)}, u32[]{:S(2)}, u32[]{:S(2)}) collective-permute-start(f32[3,18,1,128]{3,2,1,0:T(1,128)S(1)} %get-tuple-element.12), channel_id=1, source_target_pairs={{0,1},{1,2},{2,3},{3,4},{4,5},{5,6},{6,7},{7,8},{8,9},{9,10},{10,1... | collective-permute-start | bytes 82952 | tf_op jit(solution)/shard_map/ppermute | solution.py:12
  (128 shorter events, 42.0 us)
Async XLA Ops:
  7.2 197.3 %copy-start = (bf16[1,1,1024,1024]{3,2,1,0:T(8,128)(2,1)S(1)}, bf16[1,1,1024,1024]{3,2,1,0:T(8,128)(2,1)}, u32[]{:S(2)}) copy-start(bf16[1,1,1024,1024]{3,2,1,0:T(8,128)(2,1)} %param.11) | copy-start | bytes 6291460
  7.2 195.6 %all-gather.3.cloned.1.call-start = ((), (), s32[]{:S(2)}) async-start(), calls=%async_computation | async-start | bytes 1050624 | tf_op jit(solution)/shard_map/all_gather | solution.py:37
  11.4 12.4 %collective-permute-start = (bf16[1,64,128]{2,1,0:T(8,128)(2,1)S(1)}, bf16[1,64,128]{2,1,0:T(8,128)(2,1)S(1)}, u32[]{:S(2)}, u32[]{:S(2)}) collective-permute-start(bf16[1,64,128]{2,1,0:T(8,128)(2,1)S(1)} %get-tuple-element.26), channel_id=1, source_target_pairs={{0,16},{16,32},{32,48},{48,64},{64,80},{80,96},{96,112},{112,128},... | collective-permute-start | bytes 49160 | tf_op jit(solution)/shard_map/ppermute | solution.py:12
  15.5 8.3 %collective-permute-start.1 = (bf16[1,64,128]{2,1,0:T(8,128)(2,1)S(1)}, bf16[1,64,128]{2,1,0:T(8,128)(2,1)S(1)}, u32[]{:S(2)}, u32[]{:S(2)}) collective-permute-start(bf16[1,64,128]{2,1,0:T(8,128)(2,1)S(1)} %get-tuple-element.25), channel_id=1, source_target_pairs={{16,0},{32,16},{48,32},{64,48},{80,64},{96,80},{112,96},{128,112},... | collective-permute-start | bytes 49160 | tf_op jit(solution)/shard_map/ppermute | solution.py:15
  17.4 6.4 %collective-permute-start.2 = (bf16[1,64,128]{2,1,0:T(8,128)(2,1)S(1)}, bf16[1,64,128]{2,1,0:T(8,128)(2,1)S(1)}, u32[]{:S(2)}, u32[]{:S(2)}) collective-permute-start(bf16[1,64,128]{2,1,0:T(8,128)(2,1)S(1)} %get-tuple-element.24), channel_id=1, source_target_pairs={{0,1},{1,2},{2,3},{3,4},{4,5},{5,6},{6,7},{7,8},{8,9},{9,10},{10,1... | collective-permute-start | bytes 49160 | tf_op jit(solution)/shard_map/ppermute | solution.py:12
  20.6 6.6 %collective-permute-start.3 = (bf16[1,64,128]{2,1,0:T(8,128)(2,1)S(1)}, bf16[1,64,128]{2,1,0:T(8,128)(2,1)S(1)}, u32[]{:S(2)}, u32[]{:S(2)}) collective-permute-start(bf16[1,64,128]{2,1,0:T(8,128)(2,1)S(1)} %get-tuple-element.23), channel_id=1, source_target_pairs={{1,0},{2,1},{3,2},{4,3},{5,4},{6,5},{7,6},{8,7},{9,8},{10,9},{11,1... | collective-permute-start | bytes 49160 | tf_op jit(solution)/shard_map/ppermute | solution.py:15
  28.6 405.2 %all-gather.5.cloned.1.call-start = ((), (), s32[]{:S(2)}) async-start(), calls=%async_computation.1 | async-start | bytes 1050624 | tf_op jit(solution)/shard_map/all_gather | solution.py:37
  36.0 166.8 %copy-start.4 = (bf16[1,1,8,1024]{3,2,1,0:T(8,128)(2,1)S(1)}, bf16[1,1,8,1024]{3,2,1,0:T(8,128)(2,1)}, u32[]{:S(2)}) copy-start(bf16[1,1,8,1024]{3,2,1,0:T(8,128)(2,1)} %param.12) | copy-start | bytes 49156
  39.2 166.2 %copy-start.7 = (pred[4096]{0:T(1024)(128)(4,1)}, pred[4096]{0:T(1024)(128)(4,1)S(1)}, u32[]{:S(2)}) copy-start(pred[4096]{0:T(1024)(128)(4,1)S(1)} %broadcast_in_dim.36) | copy-start | bytes 12292
  206.1 11.1 %collective-permute-start.4 = (f32[1,64,128]{1,2,0:T(8,128)}, f32[1,64,128]{1,2,0:T(8,128)}, u32[]{:S(2)}, u32[]{:S(2)}) collective-permute-start(f32[1,64,128]{1,2,0:T(8,128)} %get-tuple-element.10), channel_id=1, source_target_pairs={{0,16},{16,32},{32,48},{48,64},{64,80},{80,96},{96,112},{112,128},... | collective-permute-start | bytes 98312 | tf_op jit(solution)/shard_map/ppermute | solution.py:12
  209.1 9.0 %collective-permute-start.5 = (f32[1,64,128]{1,2,0:T(8,128)}, f32[1,64,128]{1,2,0:T(8,128)S(1)}, u32[]{:S(2)}, u32[]{:S(2)}) collective-permute-start(f32[1,64,128]{1,2,0:T(8,128)} %get-tuple-element.9), channel_id=1, source_target_pairs={{16,0},{32,16},{48,32},{64,48},{80,64},{96,80},{112,96},{128,112},... | collective-permute-start | bytes 98312 | tf_op jit(solution)/shard_map/ppermute | solution.py:15
  211.0 7.1 %collective-permute-start.6 = (f32[1,64,128]{1,2,0:T(8,128)}, f32[1,64,128]{1,2,0:T(8,128)S(1)}, u32[]{:S(2)}, u32[]{:S(2)}) collective-permute-start(f32[1,64,128]{1,2,0:T(8,128)} %get-tuple-element.8), channel_id=1, source_target_pairs={{0,1},{1,2},{2,3},{3,4},{4,5},{5,6},{6,7},{7,8},{8,9},{9,10},{10,1... | collective-permute-start | bytes 98312 | tf_op jit(solution)/shard_map/ppermute | solution.py:12
  214.2 8.3 %collective-permute-start.7 = (f32[1,64,128]{1,2,0:T(8,128)}, f32[1,64,128]{1,2,0:T(8,128)S(1)}, u32[]{:S(2)}, u32[]{:S(2)}) collective-permute-start(f32[1,64,128]{1,2,0:T(8,128)} %get-tuple-element.7), channel_id=1, source_target_pairs={{1,0},{2,1},{3,2},{4,3},{5,4},{6,5},{7,6},{8,7},{9,8},{10,9},{11,1... | collective-permute-start | bytes 98312 | tf_op jit(solution)/shard_map/ppermute | solution.py:15
  217.0 25.8 %copy-start.1 = (f32[3,16,16,128]{3,2,1,0:T(8,128)S(1)}, f32[3,16,16,128]{3,2,1,0:T(8,128)}, u32[]{:S(2)}) copy-start(f32[3,16,16,128]{3,2,1,0:T(8,128)} %param.9) | copy-start | bytes 1179652
  218.2 24.9 %copy-start.11 = (s32[1024]{0:T(1024)S(1)}, s32[1024]{0:T(1024)}, u32[]{:S(2)}) copy-start(s32[1024]{0:T(1024)} %copy-done.10) | copy-start | bytes 12292
  226.2 207.7 %copy-start.8 = (pred[4096]{0:T(1024)(128)(4,1)S(1)}, pred[4096]{0:T(1024)(128)(4,1)}, u32[]{:S(2)}) copy-start(pred[4096]{0:T(1024)(128)(4,1)} %copy-done.7) | copy-start | bytes 12292
  227.4 6.1 %collective-permute-start.8 = (f32[3,1,16,128]{3,2,1,0:T(8,128)S(1)}, f32[3,1,16,128]{3,2,1,0:T(8,128)S(1)}, u32[]{:S(2)}, u32[]{:S(2)}) collective-permute-start(f32[3,1,16,128]{3,2,1,0:T(8,128)S(1)} %get-tuple-element.18), channel_id=1, source_target_pairs={{16,0},{32,16},{48,32},{64,48},{80,64},{96,80},{112,96},{128,112},... | collective-permute-start | bytes 73736 | tf_op jit(solution)/shard_map/ppermute | solution.py:15
  229.8 4.6 collective-permute-start.9
  234.4 7.4 %collective-permute-start.10 = (f32[3,18,1,128]{3,2,1,0:T(1,128)S(1)}, f32[3,18,1,128]{3,2,1,0:T(1,128)S(1)}, u32[]{:S(2)}, u32[]{:S(2)}) collective-permute-start(f32[3,18,1,128]{3,2,1,0:T(1,128)S(1)} %get-tuple-element.13), channel_id=1, source_target_pairs={{1,0},{2,1},{3,2},{4,3},{5,4},{6,5},{7,6},{8,7},{9,8},{10,9},{11,1... | collective-permute-start | bytes 82952 | tf_op jit(solution)/shard_map/ppermute | solution.py:15
  236.4 6.4 %collective-permute-start.11 = (f32[3,18,1,128]{3,2,1,0:T(1,128)S(1)}, f32[3,18,1,128]{3,2,1,0:T(1,128)S(1)}, u32[]{:S(2)}, u32[]{:S(2)}) collective-permute-start(f32[3,18,1,128]{3,2,1,0:T(1,128)S(1)} %get-tuple-element.14), channel_id=1, source_target_pairs={{0,1},{1,2},{2,3},{3,4},{4,5},{5,6},{6,7},{7,8},{8,9},{9,10},{10,1... | collective-permute-start | bytes 82952 | tf_op jit(solution)/shard_map/ppermute | solution.py:12
  244.0 15.3 %collective-permute-start.12 = (bf16[1,64,128]{2,1,0:T(8,128)(2,1)S(1)}, bf16[1,64,128]{2,1,0:T(8,128)(2,1)S(1)}, u32[]{:S(2)}, u32[]{:S(2)}) collective-permute-start(bf16[1,64,128]{2,1,0:T(8,128)(2,1)S(1)} %get-tuple-element.22), channel_id=1, source_target_pairs={{0,16},{16,32},{32,48},{48,64},{64,80},{80,96},{96,112},{112,128},... | collective-permute-start | bytes 49160 | tf_op jit(solution)/shard_map/ppermute | solution.py:12
  249.4 9.9 %collective-permute-start.13 = (bf16[1,64,128]{2,1,0:T(8,128)(2,1)S(1)}, bf16[1,64,128]{2,1,0:T(8,128)(2,1)S(1)}, u32[]{:S(2)}, u32[]{:S(2)}) collective-permute-start(bf16[1,64,128]{2,1,0:T(8,128)(2,1)S(1)} %get-tuple-element.21), channel_id=1, source_target_pairs={{16,0},{32,16},{48,32},{64,48},{80,64},{96,80},{112,96},{128,112},... | collective-permute-start | bytes 49160 | tf_op jit(solution)/shard_map/ppermute | solution.py:15
  251.3 8.0 %collective-permute-start.14 = (bf16[1,64,128]{2,1,0:T(8,128)(2,1)S(1)}, bf16[1,64,128]{2,1,0:T(8,128)(2,1)S(1)}, u32[]{:S(2)}, u32[]{:S(2)}) collective-permute-start(bf16[1,64,128]{2,1,0:T(8,128)(2,1)S(1)} %get-tuple-element.20), channel_id=1, source_target_pairs={{0,1},{1,2},{2,3},{3,4},{4,5},{5,6},{6,7},{7,8},{8,9},{9,10},{10,1... | collective-permute-start | bytes 49160 | tf_op jit(solution)/shard_map/ppermute | solution.py:12
  257.4 6.6 %collective-permute-start.15 = (bf16[1,64,128]{2,1,0:T(8,128)(2,1)S(1)}, bf16[1,64,128]{2,1,0:T(8,128)(2,1)S(1)}, u32[]{:S(2)}, u32[]{:S(2)}) collective-permute-start(bf16[1,64,128]{2,1,0:T(8,128)(2,1)S(1)} %get-tuple-element.19), channel_id=1, source_target_pairs={{1,0},{2,1},{3,2},{4,3},{5,4},{6,5},{7,6},{8,7},{9,8},{10,9},{11,1... | collective-permute-start | bytes 49160 | tf_op jit(solution)/shard_map/ppermute | solution.py:15
  438.2 12.1 %collective-permute-start.16 = (f32[1,64,128]{1,2,0:T(8,128)}, f32[1,64,128]{1,2,0:T(8,128)S(1)}, u32[]{:S(2)}, u32[]{:S(2)}) collective-permute-start(f32[1,64,128]{1,2,0:T(8,128)} %get-tuple-element.6), channel_id=1, source_target_pairs={{0,16},{16,32},{32,48},{48,64},{64,80},{80,96},{96,112},{112,128},... | collective-permute-start | bytes 98312 | tf_op jit(solution)/shard_map/ppermute | solution.py:12
  441.2 10.7 %collective-permute-start.17 = (f32[1,64,128]{1,2,0:T(8,128)}, f32[1,64,128]{1,2,0:T(8,128)}, u32[]{:S(2)}, u32[]{:S(2)}) collective-permute-start(f32[1,64,128]{1,2,0:T(8,128)} %get-tuple-element.5), channel_id=1, source_target_pairs={{16,0},{32,16},{48,32},{64,48},{80,64},{96,80},{112,96},{128,112},... | collective-permute-start | bytes 98312 | tf_op jit(solution)/shard_map/ppermute | solution.py:15
  443.1 9.7 %collective-permute-start.18 = (f32[1,64,128]{1,2,0:T(8,128)}, f32[1,64,128]{1,2,0:T(8,128)S(1)}, u32[]{:S(2)}, u32[]{:S(2)}) collective-permute-start(f32[1,64,128]{1,2,0:T(8,128)} %get-tuple-element.4), channel_id=1, source_target_pairs={{0,1},{1,2},{2,3},{3,4},{4,5},{5,6},{6,7},{7,8},{8,9},{9,10},{10,1... | collective-permute-start | bytes 98312 | tf_op jit(solution)/shard_map/ppermute | solution.py:12
  446.3 8.1 %collective-permute-start.19 = (f32[1,64,128]{1,2,0:T(8,128)}, f32[1,64,128]{1,2,0:T(8,128)S(1)}, u32[]{:S(2)}, u32[]{:S(2)}) collective-permute-start(f32[1,64,128]{1,2,0:T(8,128)} %get-tuple-element.3), channel_id=1, source_target_pairs={{1,0},{2,1},{3,2},{4,3},{5,4},{6,5},{7,6},{8,7},{9,8},{10,9},{11,1... | collective-permute-start | bytes 98312 | tf_op jit(solution)/shard_map/ppermute | solution.py:15
  458.9 6.3 %collective-permute-start.20 = (f32[3,1,16,128]{3,2,1,0:T(8,128)S(1)}, f32[3,1,16,128]{3,2,1,0:T(8,128)S(1)}, u32[]{:S(2)}, u32[]{:S(2)}) collective-permute-start(f32[3,1,16,128]{3,2,1,0:T(8,128)S(1)} %get-tuple-element.16), channel_id=1, source_target_pairs={{16,0},{32,16},{48,32},{64,48},{80,64},{96,80},{112,96},{128,112},... | collective-permute-start | bytes 73736 | tf_op jit(solution)/shard_map/ppermute | solution.py:15
  460.8 5.3 %collective-permute-start.21 = (f32[3,1,16,128]{3,2,1,0:T(8,128)S(1)}, f32[3,1,16,128]{3,2,1,0:T(8,128)S(1)}, u32[]{:S(2)}, u32[]{:S(2)}) collective-permute-start(f32[3,1,16,128]{3,2,1,0:T(8,128)S(1)} %get-tuple-element.15), channel_id=1, source_target_pairs={{0,16},{16,32},{32,48},{48,64},{64,80},{80,96},{96,112},{112,128},... | collective-permute-start | bytes 73736 | tf_op jit(solution)/shard_map/ppermute | solution.py:12
  466.1 7.4 %collective-permute-start.22 = (f32[3,18,1,128]{3,2,1,0:T(1,128)S(1)}, f32[3,18,1,128]{3,2,1,0:T(1,128)S(1)}, u32[]{:S(2)}, u32[]{:S(2)}) collective-permute-start(f32[3,18,1,128]{3,2,1,0:T(1,128)S(1)} %get-tuple-element.11), channel_id=1, source_target_pairs={{1,0},{2,1},{3,2},{4,3},{5,4},{6,5},{7,6},{8,7},{9,8},{10,9},{11,1... | collective-permute-start | bytes 82952 | tf_op jit(solution)/shard_map/ppermute | solution.py:15
  468.5 6.0 %collective-permute-start.23 = (f32[3,18,1,128]{3,2,1,0:T(1,128)S(1)}, f32[3,18,1,128]{3,2,1,0:T(1,128)S(1)}, u32[]{:S(2)}, u32[]{:S(2)}) collective-permute-start(f32[3,18,1,128]{3,2,1,0:T(1,128)S(1)} %get-tuple-element.12), channel_id=1, source_target_pairs={{0,1},{1,2},{2,3},{3,4},{4,5},{5,6},{6,7},{7,8},{8,9},{9,10},{10,1... | collective-permute-start | bytes 82952 | tf_op jit(solution)/shard_map/ppermute | solution.py:12
  (14 other events, 175.6 us)
Sparse Core Ops, SparseCore 0:
  28.7 173.9 all-gather.2
  265.5 168.2 all-gather.4
where the time goes:
time: 488 us; the launch traced here: 482 us
  waiting for transfers between devices  348 us (71%)
  starting transfers between devices  74.1 us (15%)
  local copies, waits for them, and re-layouts  22.8 us (5%)
  between operations  14.8 us (3%)
  other arithmetic  14.4 us (3%)
  matrix products  8.25 us (2%)
    all_gather x2, waiting for transfers between devices, coarse_solve(): lax.all_gather(coarse_in, ('gx', 'gy'), axis=0, tiled=True)  332 us
    ppermute x12, starting transfers between devices, with_halo(): lax.ppermute(lax.slice_in_dim(block, block.shape[dim] - width, None, axis...  49.4 us
    ppermute x12, starting transfers between devices, with_halo(): lax.ppermute(lax.slice_in_dim(block, 0, width, axis=dim), axis, backward)  24.6 us
    ppermute x12, waiting for transfers between devices, with_halo(): lax.ppermute(lax.slice_in_dim(block, 0, width, axis=dim), axis, backward)  12.2 us
  transfers between devices with their start and end apart: 26, of which 9 were waited for; matrix products, arithmetic and copies ran while one was open for 4% of the time, Pallas kernels for 0%

commit v1 on v0

--- a/solution.py
+++ b/solution.py
@@ -31,12 +31,15 @@
     return (4.0 + stiffness[None, :, :, None]) * values - beside
 
 
-def coarse_solve(coarse_in, ordered):
-    return jnp.dot(
-        ordered,
-        lax.all_gather(coarse_in, ("gx", "gy"), axis=0, tiled=True),
-        preferred_element_type=jnp.float32,
+def coarse_solve(coarse_in, crossing):
+    count = lax.axis_size("gx")
+    copies = jnp.broadcast_to(coarse_in[None], (count,) + coarse_in.shape)
+    column = lax.all_to_all(copies, "gx", split_axis=0, concat_axis=0, tiled=True)
+    parts = jnp.dot(
+        crossing, column.reshape(-1, coarse_in.shape[-1]), preferred_element_type=jnp.float32
     )
+    parts = parts.reshape(lax.axis_size("gy"), *coarse_in.shape)
+    return jnp.sum(lax.all_to_all(parts, "gy", split_axis=0, concat_axis=0, tiled=True), axis=0)
 
 
 def precondition(values, inverse, basis_rows, row_lists, ordered):
@@ -89,9 +92,12 @@
     device_count = partition_map.shape[0]
     coarse_width = basis_rows.shape[0]
     stored = coarse_rows[0, 0].reshape(coarse_width, device_count, coarse_width)
-    ordered = jnp.take(stored, partition_map, axis=1).reshape(
-        coarse_width, device_count * coarse_width
-    )
+    chosen = (partition_map[None, :] == jnp.arange(device_count)[:, None]).astype(stored.dtype)
+    ordered = jnp.einsum("ipk,pe->iek", stored, chosen)
+    grid = (coarse_width, lax.axis_size("gx"), lax.axis_size("gy"), coarse_width)
+    ordered = ordered.reshape(grid).transpose(2, 0, 1, 3).reshape(grid[2], coarse_width, -1)
+    ordered = lax.all_to_all(ordered, "gy", split_axis=0, concat_axis=0, tiled=True)
+    ordered = ordered.reshape(grid[2] * coarse_width, -1)
     first_pass = precondition(residual, inverse, basis_rows, row_lists, ordered)
     middle = residual - operate(first_pass, stiffness)
     second_pass = precondition(middle, inverse, basis_rows, row_lists, ordered)

time: 488 us -> 211 us (0.43)
  waiting for transfers between devices: 348 us -> 16.1 us
  blocking collectives: 0 us -> 67.6 us
  starting transfers between devices: 74.1 us -> 88.3 us
  between operations: 14.8 us -> 1.41 us
  matrix products: 8.25 us -> 3.09 us
    all_gather x2 -> x0, waiting for transfers between devices: 332 us -> none  [coarse_solve(): lax.all_gather(coarse_in, ('gx', 'gy'), axis=0, tiled=True)]
    all_to_all x0 -> x4, blocking collectives: none -> 67.6 us  [the longest x2 49 us: coarse_solve(): lax.all_to_all(copies, 'gx', split_axis=0, concat_axis=0, tiled=True)]
    ppermute x12, starting transfers between devices: 24.6 us -> 32.7 us  [with_halo(): lax.ppermute(lax.slice_in_dim(block, 0, width, axis=dim), axis, backward)]
    all_to_all x0 -> x1, starting transfers between devices: none -> 6.6 us  [per_device(): lax.all_to_all(ordered, 'gy', split_axis=0, concat_axis=0, tiled=True)]
    gather x3 -> x0, local copies, waits for them, and re-layouts: 5.21 us -> none  [per_device(): jnp.take(stored, partition_map, axis=1)]
  transfers between devices with their start and end apart: 26 -> 25, of which waited for: 9 -> 6; matrix products, arithmetic and copies ran while one was open for 4% -> 7% of each run, Pallas kernels for 0% -> 0%
where the time goes in v1:
time: 211 us; the launch traced here: 207 us
  starting transfers between devices  88.3 us (42%)
  blocking collectives  67.6 us (32%)
  local copies, waits for them, and re-layouts  18.1 us (9%)
  waiting for transfers between devices  16.1 us (8%)
  other arithmetic  12.8 us (6%)
  matrix products  3.09 us (1%)
    all_to_all x2, blocking collectives, coarse_solve(): lax.all_to_all(copies, 'gx', split_axis=0, concat_axis=0, tiled=True)  49 us
    ppermute x12, starting transfers between devices, with_halo(): lax.ppermute(lax.slice_in_dim(block, block.shape[dim] - width, None, axis...  49 us
    ppermute x12, starting transfers between devices, with_halo(): lax.ppermute(lax.slice_in_dim(block, 0, width, axis=dim), axis, backward)  32.7 us
    all_to_all x2, blocking collectives, coarse_solve(): lax.all_to_all(parts, 'gy', split_axis=0, concat_axis=0, tiled=True)  18.6 us
    ppermute x12, waiting for transfers between devices, with_halo(): lax.ppermute(lax.slice_in_dim(block, 0, width, axis=dim), axis, backward)  9.56 us
    all_to_all x1, starting transfers between devices, per_device(): lax.all_to_all(ordered, 'gy', split_axis=0, concat_axis=0, tiled=True)  6.6 us
    another operation x2, local copies, waits for them, and re-layouts, per_device(): stored = coarse_rows[0, 0].reshape(coarse_width, device_count, coarse_width)  4.65 us
    all_to_all x1, waiting for transfers between devices, per_device(): lax.all_to_all(ordered, 'gy', split_axis=0, concat_axis=0, tiled=True)  4.6 us
  transfers between devices with their start and end apart: 25, of which 6 were waited for; matrix products, arithmetic and copies ran while one was open for 7% of the time, Pallas kernels for 0%

profile of v1, /device:TPU:7, one launch (start us, length us, event | category | flops | bytes accessed | tf_op | source)
XLA Modules:
  0.0 207.4 jit_solution(3400044156805896825)
XLA Ops:
  4.1 2.5 %collective-permute-start.3 = (bf16[1,64,128]{2,1,0:T(8,128)(2,1)S(1)}, bf16[1,64,128]{2,1,0:T(8,128)(2,1)S(1)}, u32[]{:S(2)}, u32[]{:S(2)}) collective-permute-start(bf16[1,64,128]{2,1,0:T(8,128)(2,1)S(1)} %get-tuple-element.23), channel_id=1, source_target_pairs={{1,0},{2,1},{3,2},{4,3},{5,4},{6,5},{7,6},{8,7},{9,8},{10,9},{11,1... | collective-permute-start | bytes 49160 | tf_op jit(solution)/shard_map/ppermute | solution.py:15
  6.6 4.9 %collective-permute-start.2 = (bf16[1,64,128]{2,1,0:T(8,128)(2,1)S(1)}, bf16[1,64,128]{2,1,0:T(8,128)(2,1)S(1)}, u32[]{:S(2)}, u32[]{:S(2)}) collective-permute-start(bf16[1,64,128]{2,1,0:T(8,128)(2,1)S(1)} %get-tuple-element.24), channel_id=1, source_target_pairs={{0,1},{1,2},{2,3},{3,4},{4,5},{5,6},{6,7},{7,8},{8,9},{9,10},{10,1... | collective-permute-start | bytes 49160 | tf_op jit(solution)/shard_map/ppermute | solution.py:12
  11.5 3.1 %collective-permute-start.1 = (bf16[1,64,128]{2,1,0:T(8,128)(2,1)S(1)}, bf16[1,64,128]{2,1,0:T(8,128)(2,1)S(1)}, u32[]{:S(2)}, u32[]{:S(2)}) collective-permute-start(bf16[1,64,128]{2,1,0:T(8,128)(2,1)S(1)} %get-tuple-element.25), channel_id=1, source_target_pairs={{16,0},{32,16},{48,32},{64,48},{80,64},{96,80},{112,96},{128,112},... | collective-permute-start | bytes 49160 | tf_op jit(solution)/shard_map/ppermute | solution.py:15
  14.7 3.4 %collective-permute-start = (bf16[1,64,128]{2,1,0:T(8,128)(2,1)S(1)}, bf16[1,64,128]{2,1,0:T(8,128)(2,1)S(1)}, u32[]{:S(2)}, u32[]{:S(2)}) collective-permute-start(bf16[1,64,128]{2,1,0:T(8,128)(2,1)S(1)} %get-tuple-element.26), channel_id=1, source_target_pairs={{0,16},{16,32},{32,48},{48,64},{64,80},{80,96},{96,112},{112,128},... | collective-permute-start | bytes 49160 | tf_op jit(solution)/shard_map/ppermute | solution.py:12
  18.2 3.1 %reshape_squeeze.3 = bf16[8,512,8]{2,1,0:T(8,128)(2,1)} reshape(bf16[1,1,8,4096]{3,2,1,0:T(8,128)(2,1)} %param.13) | data formatting | bytes 131072 | tf_op jit(solution)/shard_map/reshape;squeeze | solution.py:94
  26.4 6.6 %all-to-all-start = ((bf16[16,8,256]{2,1,0:T(8,128)(2,1)}), bf16[16,8,256]{2,1,0:T(8,128)(2,1)S(1)}, u32[]{:S(2)}, u32[]{:S(2)}) async-start(bf16[16,8,256]{2,1,0:T(8,128)(2,1)} %copy.47), calls=%async_computation | async-start | bytes 131072 | tf_op jit(solution)/shard_map/all_to_all | solution.py:99
  33.3 4.6 %all-to-all-done = bf16[16,8,256]{2,1,0:T(8,128)(2,1)S(1)} async-done(((bf16[16,8,256]{2,1,0:T(8,128)(2,1)}), bf16[16,8,256]{2,1,0:T(8,128)(2,1)S(1)}, u32[]{:S(2)}, u32[]{:S(2)}) %all-to-all-start) | async-done | bytes 65568 | tf_op jit(solution)/shard_map/all_to_all | solution.py:99
  37.9 28.5 %all_to_all.25 = bf16[32,8,128]{2,1,0:T(8,128)(2,1)S(1)} all-to-all(bf16[32,8,128]{2,1,0:T(8,128)(2,1)S(1)} %broadcast_in_dim.13), channel_id=1, replica_groups=mesh['gx'=32,'gy'=16] {'gx'}, dimensions={0} | all-to-all | bytes 131072 | tf_op jit(solution)/shard_map/all_to_all | solution.py:37
  66.5 9.4 %all_to_all.26 = f32[16,8,128]{2,1,0:T(8,128)S(1)} all-to-all(f32[16,8,128]{2,1,0:T(8,128)S(1)} %fusion.31), channel_id=1, replica_groups=mesh['gx'=32,'gy'=16] {'gy'}, dimensions={0} | all-to-all | bytes 131072 | tf_op jit(solution)/shard_map/all_to_all | solution.py:42
  77.8 2.3 %collective-permute-start.7 = (f32[1,64,128]{1,2,0:T(8,128)}, f32[1,64,128]{1,2,0:T(8,128)}, u32[]{:S(2)}, u32[]{:S(2)}) collective-permute-start(f32[1,64,128]{1,2,0:T(8,128)} %get-tuple-element.7), channel_id=1, source_target_pairs={{1,0},{2,1},{3,2},{4,3},{5,4},{6,5},{7,6},{8,7},{9,8},{10,9},{11,1... | collective-permute-start | bytes 98312 | tf_op jit(solution)/shard_map/ppermute | solution.py:15
  80.1 5.1 %collective-permute-start.6 = (f32[1,64,128]{1,2,0:T(8,128)}, f32[1,64,128]{1,2,0:T(8,128)S(1)}, u32[]{:S(2)}, u32[]{:S(2)}) collective-permute-start(f32[1,64,128]{1,2,0:T(8,128)} %get-tuple-element.8), channel_id=1, source_target_pairs={{0,1},{1,2},{2,3},{3,4},{4,5},{5,6},{6,7},{7,8},{8,9},{9,10},{10,1... | collective-permute-start | bytes 98312 | tf_op jit(solution)/shard_map/ppermute | solution.py:12
  85.2 5.5 %collective-permute-start.5 = (f32[1,64,128]{1,2,0:T(8,128)}, f32[1,64,128]{1,2,0:T(8,128)S(1)}, u32[]{:S(2)}, u32[]{:S(2)}) collective-permute-start(f32[1,64,128]{1,2,0:T(8,128)} %get-tuple-element.9), channel_id=1, source_target_pairs={{16,0},{32,16},{48,32},{64,48},{80,64},{96,80},{112,96},{128,112},... | collective-permute-start | bytes 98312 | tf_op jit(solution)/shard_map/ppermute | solution.py:15
  90.7 2.1 %collective-permute-start.4 = (f32[1,64,128]{1,2,0:T(8,128)}, f32[1,64,128]{1,2,0:T(8,128)S(1)}, u32[]{:S(2)}, u32[]{:S(2)}) collective-permute-start(f32[1,64,128]{1,2,0:T(8,128)} %get-tuple-element.10), channel_id=1, source_target_pairs={{0,16},{16,32},{32,48},{48,64},{64,80},{80,96},{96,112},{112,128},... | collective-permute-start | bytes 98312 | tf_op jit(solution)/shard_map/ppermute | solution.py:12
  99.6 3.9 %collective-permute-start.9 = (f32[3,1,16,128]{3,2,1,0:T(8,128)S(1)}, f32[3,1,16,128]{3,2,1,0:T(8,128)S(1)}, u32[]{:S(2)}, u32[]{:S(2)}) collective-permute-start(f32[3,1,16,128]{3,2,1,0:T(8,128)S(1)} %get-tuple-element.17), channel_id=1, source_target_pairs={{0,16},{16,32},{32,48},{48,64},{64,80},{80,96},{96,112},{112,128},... | collective-permute-start | bytes 73736 | tf_op jit(solution)/shard_map/ppermute | solution.py:12
  103.5 1.9 collective-permute-start.8
  105.4 3.2 %collective-permute-done.8 = f32[3,1,16,128]{3,2,1,0:T(8,128)S(1)} collective-permute-done((f32[3,1,16,128]{3,2,1,0:T(8,128)S(1)}, f32[3,1,16,128]{3,2,1,0:T(8,128)S(1)}, u32[]{:S(2)}, u32[]{:S(2)}) %collective-permute-start.8) | collective-permute-done | bytes 24608 | tf_op jit(solution)/shard_map/ppermute | solution.py:15
  108.7 1.9 collective-permute-start.10
  110.6 5.5 %collective-permute-start.11 = (f32[3,18,1,128]{3,2,1,0:T(1,128)S(1)}, f32[3,18,1,128]{3,2,1,0:T(1,128)S(1)}, u32[]{:S(2)}, u32[]{:S(2)}) collective-permute-start(f32[3,18,1,128]{3,2,1,0:T(1,128)S(1)} %get-tuple-element.14), channel_id=1, source_target_pairs={{0,1},{1,2},{2,3},{3,4},{4,5},{5,6},{6,7},{7,8},{8,9},{9,10},{10,1... | collective-permute-start | bytes 82952 | tf_op jit(solution)/shard_map/ppermute | solution.py:12
  118.2 3.1 %collective-permute-start.12 = (bf16[1,64,128]{2,1,0:T(8,128)(2,1)S(1)}, bf16[1,64,128]{2,1,0:T(8,128)(2,1)S(1)}, u32[]{:S(2)}, u32[]{:S(2)}) collective-permute-start(bf16[1,64,128]{2,1,0:T(8,128)(2,1)S(1)} %get-tuple-element.22), channel_id=1, source_target_pairs={{0,16},{16,32},{32,48},{48,64},{64,80},{80,96},{96,112},{112,128},... | collective-permute-start | bytes 49160 | tf_op jit(solution)/shard_map/ppermute | solution.py:12
  123.2 6.0 %collective-permute-start.14 = (bf16[1,64,128]{2,1,0:T(8,128)(2,1)S(1)}, bf16[1,64,128]{2,1,0:T(8,128)(2,1)S(1)}, u32[]{:S(2)}, u32[]{:S(2)}) collective-permute-start(bf16[1,64,128]{2,1,0:T(8,128)(2,1)S(1)} %get-tuple-element.20), channel_id=1, source_target_pairs={{0,1},{1,2},{2,3},{3,4},{4,5},{5,6},{6,7},{7,8},{8,9},{9,10},{10,1... | collective-permute-start | bytes 49160 | tf_op jit(solution)/shard_map/ppermute | solution.py:12
  131.3 3.1 %collective-permute-done.13 = bf16[1,64,128]{2,1,0:T(8,128)(2,1)S(1)} collective-permute-done((bf16[1,64,128]{2,1,0:T(8,128)(2,1)S(1)}, bf16[1,64,128]{2,1,0:T(8,128)(2,1)S(1)}, u32[]{:S(2)}, u32[]{:S(2)}) %collective-permute-start.13) | collective-permute-done | bytes 16416 | tf_op jit(solution)/shard_map/ppermute | solution.py:15
  134.6 20.6 %all_to_all.27 = bf16[32,8,128]{2,1,0:T(8,128)(2,1)S(1)} all-to-all(bf16[32,8,128]{2,1,0:T(8,128)(2,1)S(1)} %broadcast_in_dim.14), channel_id=1, replica_groups=mesh['gx'=32,'gy'=16] {'gx'}, dimensions={0} | all-to-all | bytes 131072 | tf_op jit(solution)/shard_map/all_to_all | solution.py:37
  155.3 9.2 %all_to_all.28 = f32[16,8,128]{2,1,0:T(8,128)S(1)} all-to-all(f32[16,8,128]{2,1,0:T(8,128)S(1)} %fusion.29), channel_id=1, replica_groups=mesh['gx'=32,'gy'=16] {'gy'}, dimensions={0} | all-to-all | bytes 131072 | tf_op jit(solution)/shard_map/all_to_all | solution.py:42
  166.5 2.3 %collective-permute-start.19 = (f32[1,64,128]{1,2,0:T(8,128)}, f32[1,64,128]{1,2,0:T(8,128)S(1)}, u32[]{:S(2)}, u32[]{:S(2)}) collective-permute-start(f32[1,64,128]{1,2,0:T(8,128)} %get-tuple-element.3), channel_id=1, source_target_pairs={{1,0},{2,1},{3,2},{4,3},{5,4},{6,5},{7,6},{8,7},{9,8},{10,9},{11,1... | collective-permute-start | bytes 98312 | tf_op jit(solution)/shard_map/ppermute | solution.py:15
  168.8 5.1 %collective-permute-start.18 = (f32[1,64,128]{1,2,0:T(8,128)}, f32[1,64,128]{1,2,0:T(8,128)S(1)}, u32[]{:S(2)}, u32[]{:S(2)}) collective-permute-start(f32[1,64,128]{1,2,0:T(8,128)} %get-tuple-element.4), channel_id=1, source_target_pairs={{0,1},{1,2},{2,3},{3,4},{4,5},{5,6},{6,7},{7,8},{8,9},{9,10},{10,1... | collective-permute-start | bytes 98312 | tf_op jit(solution)/shard_map/ppermute | solution.py:12
  173.8 5.5 %collective-permute-start.17 = (f32[1,64,128]{1,2,0:T(8,128)}, f32[1,64,128]{1,2,0:T(8,128)}, u32[]{:S(2)}, u32[]{:S(2)}) collective-permute-start(f32[1,64,128]{1,2,0:T(8,128)} %get-tuple-element.5), channel_id=1, source_target_pairs={{16,0},{32,16},{48,32},{64,48},{80,64},{96,80},{112,96},{128,112},... | collective-permute-start | bytes 98312 | tf_op jit(solution)/shard_map/ppermute | solution.py:15
  179.3 2.1 %collective-permute-start.16 = (f32[1,64,128]{1,2,0:T(8,128)}, f32[1,64,128]{1,2,0:T(8,128)S(1)}, u32[]{:S(2)}, u32[]{:S(2)}) collective-permute-start(f32[1,64,128]{1,2,0:T(8,128)} %get-tuple-element.6), channel_id=1, source_target_pairs={{0,16},{16,32},{32,48},{48,64},{64,80},{80,96},{96,112},{112,128},... | collective-permute-start | bytes 98312 | tf_op jit(solution)/shard_map/ppermute | solution.py:12
  190.5 2.4 %collective-permute-start.21 = (f32[3,1,16,128]{3,2,1,0:T(8,128)S(1)}, f32[3,1,16,128]{3,2,1,0:T(8,128)S(1)}, u32[]{:S(2)}, u32[]{:S(2)}) collective-permute-start(f32[3,1,16,128]{3,2,1,0:T(8,128)S(1)} %get-tuple-element.15), channel_id=1, source_target_pairs={{0,16},{16,32},{32,48},{48,64},{64,80},{80,96},{96,112},{112,128},... | collective-permute-start | bytes 73736 | tf_op jit(solution)/shard_map/ppermute | solution.py:12
  192.9 1.9 collective-permute-start.20
  194.8 3.2 %collective-permute-done.20 = f32[3,1,16,128]{3,2,1,0:T(8,128)S(1)} collective-permute-done((f32[3,1,16,128]{3,2,1,0:T(8,128)S(1)}, f32[3,1,16,128]{3,2,1,0:T(8,128)S(1)}, u32[]{:S(2)}, u32[]{:S(2)}) %collective-permute-start.20) | collective-permute-done | bytes 24608 | tf_op jit(solution)/shard_map/ppermute | solution.py:15
  198.1 1.9 collective-permute-start.22
  200.0 5.5 %collective-permute-start.23 = (f32[3,18,1,128]{3,2,1,0:T(1,128)S(1)}, f32[3,18,1,128]{3,2,1,0:T(1,128)S(1)}, u32[]{:S(2)}, u32[]{:S(2)}) collective-permute-start(f32[3,18,1,128]{3,2,1,0:T(1,128)S(1)} %get-tuple-element.12), channel_id=1, source_target_pairs={{0,1},{1,2},{2,3},{3,4},{4,5},{5,6},{6,7},{7,8},{8,9},{9,10},{10,1... | collective-permute-start | bytes 82952 | tf_op jit(solution)/shard_map/ppermute | solution.py:12
  (123 shorter events, 36.7 us)
Async XLA Ops:
  0.6 75.5 %copy-start = (bf16[1,1,1024,1024]{3,2,1,0:T(8,128)(2,1)S(1)}, bf16[1,1,1024,1024]{3,2,1,0:T(8,128)(2,1)}, u32[]{:S(2)}) copy-start(bf16[1,1,1024,1024]{3,2,1,0:T(8,128)(2,1)} %param.11) | copy-start | bytes 6291460
  0.6 22.2 %copy-start.15 = (s32[512]{0:T(512)S(1)}, s32[512]{0:T(512)}, u32[]{:S(2)}) copy-start(s32[512]{0:T(512)} %param.15) | copy-start | bytes 6148
  4.1 29.0 %collective-permute-start.3 = (bf16[1,64,128]{2,1,0:T(8,128)(2,1)S(1)}, bf16[1,64,128]{2,1,0:T(8,128)(2,1)S(1)}, u32[]{:S(2)}, u32[]{:S(2)}) collective-permute-start(bf16[1,64,128]{2,1,0:T(8,128)(2,1)S(1)} %get-tuple-element.23), channel_id=1, source_target_pairs={{1,0},{2,1},{3,2},{4,3},{5,4},{6,5},{7,6},{8,7},{9,8},{10,9},{11,1... | collective-permute-start | bytes 49160 | tf_op jit(solution)/shard_map/ppermute | solution.py:15
  6.6 26.5 %collective-permute-start.2 = (bf16[1,64,128]{2,1,0:T(8,128)(2,1)S(1)}, bf16[1,64,128]{2,1,0:T(8,128)(2,1)S(1)}, u32[]{:S(2)}, u32[]{:S(2)}) collective-permute-start(bf16[1,64,128]{2,1,0:T(8,128)(2,1)S(1)} %get-tuple-element.24), channel_id=1, source_target_pairs={{0,1},{1,2},{2,3},{3,4},{4,5},{5,6},{6,7},{7,8},{8,9},{9,10},{10,1... | collective-permute-start | bytes 49160 | tf_op jit(solution)/shard_map/ppermute | solution.py:12
  11.5 21.5 %collective-permute-start.1 = (bf16[1,64,128]{2,1,0:T(8,128)(2,1)S(1)}, bf16[1,64,128]{2,1,0:T(8,128)(2,1)S(1)}, u32[]{:S(2)}, u32[]{:S(2)}) collective-permute-start(bf16[1,64,128]{2,1,0:T(8,128)(2,1)S(1)} %get-tuple-element.25), channel_id=1, source_target_pairs={{16,0},{32,16},{48,32},{64,48},{80,64},{96,80},{112,96},{128,112},... | collective-permute-start | bytes 49160 | tf_op jit(solution)/shard_map/ppermute | solution.py:15
  14.7 18.3 %collective-permute-start = (bf16[1,64,128]{2,1,0:T(8,128)(2,1)S(1)}, bf16[1,64,128]{2,1,0:T(8,128)(2,1)S(1)}, u32[]{:S(2)}, u32[]{:S(2)}) collective-permute-start(bf16[1,64,128]{2,1,0:T(8,128)(2,1)S(1)} %get-tuple-element.26), channel_id=1, source_target_pairs={{0,16},{16,32},{32,48},{48,64},{64,80},{80,96},{96,112},{112,128},... | collective-permute-start | bytes 49160 | tf_op jit(solution)/shard_map/ppermute | solution.py:12
  26.4 11.5 %all-to-all-start = ((bf16[16,8,256]{2,1,0:T(8,128)(2,1)}), bf16[16,8,256]{2,1,0:T(8,128)(2,1)S(1)}, u32[]{:S(2)}, u32[]{:S(2)}) async-start(bf16[16,8,256]{2,1,0:T(8,128)(2,1)} %copy.47), calls=%async_computation | async-start | bytes 131072 | tf_op jit(solution)/shard_map/all_to_all | solution.py:99
  77.8 15.8 %collective-permute-start.7 = (f32[1,64,128]{1,2,0:T(8,128)}, f32[1,64,128]{1,2,0:T(8,128)}, u32[]{:S(2)}, u32[]{:S(2)}) collective-permute-start(f32[1,64,128]{1,2,0:T(8,128)} %get-tuple-element.7), channel_id=1, source_target_pairs={{1,0},{2,1},{3,2},{4,3},{5,4},{6,5},{7,6},{8,7},{9,8},{10,9},{11,1... | collective-permute-start | bytes 98312 | tf_op jit(solution)/shard_map/ppermute | solution.py:15
  80.1 14.4 %collective-permute-start.6 = (f32[1,64,128]{1,2,0:T(8,128)}, f32[1,64,128]{1,2,0:T(8,128)S(1)}, u32[]{:S(2)}, u32[]{:S(2)}) collective-permute-start(f32[1,64,128]{1,2,0:T(8,128)} %get-tuple-element.8), channel_id=1, source_target_pairs={{0,1},{1,2},{2,3},{3,4},{4,5},{5,6},{6,7},{7,8},{8,9},{9,10},{10,1... | collective-permute-start | bytes 98312 | tf_op jit(solution)/shard_map/ppermute | solution.py:12
  85.2 9.4 %collective-permute-start.5 = (f32[1,64,128]{1,2,0:T(8,128)}, f32[1,64,128]{1,2,0:T(8,128)S(1)}, u32[]{:S(2)}, u32[]{:S(2)}) collective-permute-start(f32[1,64,128]{1,2,0:T(8,128)} %get-tuple-element.9), channel_id=1, source_target_pairs={{16,0},{32,16},{48,32},{64,48},{80,64},{96,80},{112,96},{128,112},... | collective-permute-start | bytes 98312 | tf_op jit(solution)/shard_map/ppermute | solution.py:15
  90.7 4.0 %collective-permute-start.4 = (f32[1,64,128]{1,2,0:T(8,128)}, f32[1,64,128]{1,2,0:T(8,128)S(1)}, u32[]{:S(2)}, u32[]{:S(2)}) collective-permute-start(f32[1,64,128]{1,2,0:T(8,128)} %get-tuple-element.10), channel_id=1, source_target_pairs={{0,16},{16,32},{32,48},{48,64},{64,80},{80,96},{96,112},{112,128},... | collective-permute-start | bytes 98312 | tf_op jit(solution)/shard_map/ppermute | solution.py:12
  93.6 22.5 %copy-start.8 = (f32[16,16]{1,0:T(8,128)S(1)}, f32[16,16]{1,0:T(8,128)}, u32[]{:S(2)}) copy-start(f32[16,16]{1,0:T(8,128)} %param.10) | copy-start | bytes 3076
  94.6 22.7 %copy-start.7 = (s32[1024]{0:T(1024)S(1)}, s32[1024]{0:T(1024)}, u32[]{:S(2)}) copy-start(s32[1024]{0:T(1024)} %copy-done.6) | copy-start | bytes 12292
  96.0 22.1 %copy-start.10 = (pred[4,64]{1,0:T(4,128)(4,1)S(1)}, pred[4,64]{1,0:T(4,128)(4,1)}, u32[]{:S(2)}) copy-start(pred[4,64]{1,0:T(4,128)(4,1)} %copy-done.9) | copy-start | bytes 772
  99.6 5.8 %collective-permute-start.9 = (f32[3,1,16,128]{3,2,1,0:T(8,128)S(1)}, f32[3,1,16,128]{3,2,1,0:T(8,128)S(1)}, u32[]{:S(2)}, u32[]{:S(2)}) collective-permute-start(f32[3,1,16,128]{3,2,1,0:T(8,128)S(1)} %get-tuple-element.17), channel_id=1, source_target_pairs={{0,16},{16,32},{32,48},{48,64},{64,80},{80,96},{96,112},{112,128},... | collective-permute-start | bytes 73736 | tf_op jit(solution)/shard_map/ppermute | solution.py:12
  103.5 5.1 %collective-permute-start.8 = (f32[3,1,16,128]{3,2,1,0:T(8,128)S(1)}, f32[3,1,16,128]{3,2,1,0:T(8,128)S(1)}, u32[]{:S(2)}, u32[]{:S(2)}) collective-permute-start(f32[3,1,16,128]{3,2,1,0:T(8,128)S(1)} %get-tuple-element.18), channel_id=1, source_target_pairs={{16,0},{32,16},{48,32},{64,48},{80,64},{96,80},{112,96},{128,112},... | collective-permute-start | bytes 73736 | tf_op jit(solution)/shard_map/ppermute | solution.py:15
  108.7 7.4 %collective-permute-start.10 = (f32[3,18,1,128]{3,2,1,0:T(1,128)S(1)}, f32[3,18,1,128]{3,2,1,0:T(1,128)S(1)}, u32[]{:S(2)}, u32[]{:S(2)}) collective-permute-start(f32[3,18,1,128]{3,2,1,0:T(1,128)S(1)} %get-tuple-element.13), channel_id=1, source_target_pairs={{1,0},{2,1},{3,2},{4,3},{5,4},{6,5},{7,6},{8,7},{9,8},{10,9},{11,1... | collective-permute-start | bytes 82952 | tf_op jit(solution)/shard_map/ppermute | solution.py:15
  110.6 6.4 %collective-permute-start.11 = (f32[3,18,1,128]{3,2,1,0:T(1,128)S(1)}, f32[3,18,1,128]{3,2,1,0:T(1,128)S(1)}, u32[]{:S(2)}, u32[]{:S(2)}) collective-permute-start(f32[3,18,1,128]{3,2,1,0:T(1,128)S(1)} %get-tuple-element.14), channel_id=1, source_target_pairs={{0,1},{1,2},{2,3},{3,4},{4,5},{5,6},{6,7},{7,8},{8,9},{9,10},{10,1... | collective-permute-start | bytes 82952 | tf_op jit(solution)/shard_map/ppermute | solution.py:12
  118.2 13.0 %collective-permute-start.12 = (bf16[1,64,128]{2,1,0:T(8,128)(2,1)S(1)}, bf16[1,64,128]{2,1,0:T(8,128)(2,1)S(1)}, u32[]{:S(2)}, u32[]{:S(2)}) collective-permute-start(bf16[1,64,128]{2,1,0:T(8,128)(2,1)S(1)} %get-tuple-element.22), channel_id=1, source_target_pairs={{0,16},{16,32},{32,48},{48,64},{64,80},{80,96},{96,112},{112,128},... | collective-permute-start | bytes 49160 | tf_op jit(solution)/shard_map/ppermute | solution.py:12
  121.3 13.1 %collective-permute-start.15 = (bf16[1,64,128]{2,1,0:T(8,128)(2,1)S(1)}, bf16[1,64,128]{2,1,0:T(8,128)(2,1)S(1)}, u32[]{:S(2)}, u32[]{:S(2)}) collective-permute-start(bf16[1,64,128]{2,1,0:T(8,128)(2,1)S(1)} %get-tuple-element.19), channel_id=1, source_target_pairs={{1,0},{2,1},{3,2},{4,3},{5,4},{6,5},{7,6},{8,7},{9,8},{10,9},{11,1... | collective-permute-start | bytes 49160 | tf_op jit(solution)/shard_map/ppermute | solution.py:15
  123.2 11.1 %collective-permute-start.14 = (bf16[1,64,128]{2,1,0:T(8,128)(2,1)S(1)}, bf16[1,64,128]{2,1,0:T(8,128)(2,1)S(1)}, u32[]{:S(2)}, u32[]{:S(2)}) collective-permute-start(bf16[1,64,128]{2,1,0:T(8,128)(2,1)S(1)} %get-tuple-element.20), channel_id=1, source_target_pairs={{0,1},{1,2},{2,3},{3,4},{4,5},{5,6},{6,7},{7,8},{8,9},{9,10},{10,1... | collective-permute-start | bytes 49160 | tf_op jit(solution)/shard_map/ppermute | solution.py:12
  129.3 5.1 %collective-permute-start.13 = (bf16[1,64,128]{2,1,0:T(8,128)(2,1)S(1)}, bf16[1,64,128]{2,1,0:T(8,128)(2,1)S(1)}, u32[]{:S(2)}, u32[]{:S(2)}) collective-permute-start(bf16[1,64,128]{2,1,0:T(8,128)(2,1)S(1)} %get-tuple-element.21), channel_id=1, source_target_pairs={{16,0},{32,16},{48,32},{64,48},{80,64},{96,80},{112,96},{128,112},... | collective-permute-start | bytes 49160 | tf_op jit(solution)/shard_map/ppermute | solution.py:15
  165.7 22.5 %copy-start.12 = (s32[64]{0:T(128)S(1)}, s32[64]{0:T(128)}, u32[]{:S(2)}) copy-start(s32[64]{0:T(128)} %get-tuple-element.30) | copy-start | bytes 772
  165.7 23.6 %copy-start.11 = (s32[64]{0:T(128)S(1)}, s32[64]{0:T(128)}, u32[]{:S(2)}) copy-start(s32[64]{0:T(128)} %get-tuple-element.27) | copy-start | bytes 772
  166.5 16.9 %collective-permute-start.19 = (f32[1,64,128]{1,2,0:T(8,128)}, f32[1,64,128]{1,2,0:T(8,128)S(1)}, u32[]{:S(2)}, u32[]{:S(2)}) collective-permute-start(f32[1,64,128]{1,2,0:T(8,128)} %get-tuple-element.3), channel_id=1, source_target_pairs={{1,0},{2,1},{3,2},{4,3},{5,4},{6,5},{7,6},{8,7},{9,8},{10,9},{11,1... | collective-permute-start | bytes 98312 | tf_op jit(solution)/shard_map/ppermute | solution.py:15
  168.8 16.1 %collective-permute-start.18 = (f32[1,64,128]{1,2,0:T(8,128)}, f32[1,64,128]{1,2,0:T(8,128)S(1)}, u32[]{:S(2)}, u32[]{:S(2)}) collective-permute-start(f32[1,64,128]{1,2,0:T(8,128)} %get-tuple-element.4), channel_id=1, source_target_pairs={{0,1},{1,2},{2,3},{3,4},{4,5},{5,6},{6,7},{7,8},{8,9},{9,10},{10,1... | collective-permute-start | bytes 98312 | tf_op jit(solution)/shard_map/ppermute | solution.py:12
  173.8 11.2 %collective-permute-start.17 = (f32[1,64,128]{1,2,0:T(8,128)}, f32[1,64,128]{1,2,0:T(8,128)}, u32[]{:S(2)}, u32[]{:S(2)}) collective-permute-start(f32[1,64,128]{1,2,0:T(8,128)} %get-tuple-element.5), channel_id=1, source_target_pairs={{16,0},{32,16},{48,32},{64,48},{80,64},{96,80},{112,96},{128,112},... | collective-permute-start | bytes 98312 | tf_op jit(solution)/shard_map/ppermute | solution.py:15
  179.3 6.6 %collective-permute-start.16 = (f32[1,64,128]{1,2,0:T(8,128)}, f32[1,64,128]{1,2,0:T(8,128)S(1)}, u32[]{:S(2)}, u32[]{:S(2)}) collective-permute-start(f32[1,64,128]{1,2,0:T(8,128)} %get-tuple-element.6), channel_id=1, source_target_pairs={{0,16},{16,32},{32,48},{48,64},{64,80},{80,96},{96,112},{112,128},... | collective-permute-start | bytes 98312 | tf_op jit(solution)/shard_map/ppermute | solution.py:12
  190.5 4.3 %collective-permute-start.21 = (f32[3,1,16,128]{3,2,1,0:T(8,128)S(1)}, f32[3,1,16,128]{3,2,1,0:T(8,128)S(1)}, u32[]{:S(2)}, u32[]{:S(2)}) collective-permute-start(f32[3,1,16,128]{3,2,1,0:T(8,128)S(1)} %get-tuple-element.15), channel_id=1, source_target_pairs={{0,16},{16,32},{32,48},{48,64},{64,80},{80,96},{96,112},{112,128},... | collective-permute-start | bytes 73736 | tf_op jit(solution)/shard_map/ppermute | solution.py:12
  192.9 5.1 %collective-permute-start.20 = (f32[3,1,16,128]{3,2,1,0:T(8,128)S(1)}, f32[3,1,16,128]{3,2,1,0:T(8,128)S(1)}, u32[]{:S(2)}, u32[]{:S(2)}) collective-permute-start(f32[3,1,16,128]{3,2,1,0:T(8,128)S(1)} %get-tuple-element.16), channel_id=1, source_target_pairs={{16,0},{32,16},{48,32},{64,48},{80,64},{96,80},{112,96},{128,112},... | collective-permute-start | bytes 73736 | tf_op jit(solution)/shard_map/ppermute | solution.py:15
  198.1 7.4 %collective-permute-start.22 = (f32[3,18,1,128]{3,2,1,0:T(1,128)S(1)}, f32[3,18,1,128]{3,2,1,0:T(1,128)S(1)}, u32[]{:S(2)}, u32[]{:S(2)}) collective-permute-start(f32[3,18,1,128]{3,2,1,0:T(1,128)S(1)} %get-tuple-element.11), channel_id=1, source_target_pairs={{1,0},{2,1},{3,2},{4,3},{5,4},{6,5},{7,6},{8,7},{9,8},{10,9},{11,1... | collective-permute-start | bytes 82952 | tf_op jit(solution)/shard_map/ppermute | solution.py:15
  200.0 6.4 %collective-permute-start.23 = (f32[3,18,1,128]{3,2,1,0:T(1,128)S(1)}, f32[3,18,1,128]{3,2,1,0:T(1,128)S(1)}, u32[]{:S(2)}, u32[]{:S(2)}) collective-permute-start(f32[3,18,1,128]{3,2,1,0:T(1,128)S(1)} %get-tuple-element.12), channel_id=1, source_target_pairs={{0,1},{1,2},{2,3},{3,4},{4,5},{5,6},{6,7},{7,8},{8,9},{9,10},{10,1... | collective-permute-start | bytes 82952 | tf_op jit(solution)/shard_map/ppermute | solution.py:12
  (9 other events, 118.0 us)

commit v2 on v0

v2 whole, which is shorter than its diff:
```python
import functools

import jax
import jax.numpy as jnp
from jax import lax
from jax.experimental import pallas as pl
from jax.experimental.pallas import tpu as pltpu
from jax.sharding import PartitionSpec as P

F32, BF16 = jnp.float32, jnp.bfloat16
COMPONENTS, CELLS, LANES = 3, 16, 128
OWN = COMPONENTS * CELLS * CELLS
MARGIN = 64
SIDE, ABOVE = 24, 4
PLANE = SIDE * SIDE
FIELD = COMPONENTS * PLANE
BESIDE = COMPONENTS * CELLS * 8
STRIP = COMPONENTS * 2 * CELLS
EDGE = STRIP + 2 * CELLS + 8
PART = 128
TRADE = COMPONENTS * PART


def at(component, row, column=0):
    return component * PLANE + (row + ABOVE) * SIDE + column % SIDE


def column_of(component, column, first=0, count=CELLS):
    return pl.ds(at(component, first, column), count, stride=SIDE)


def matmul(a, b, contract=(1, 0)):
    return lax.dot_general(
        a, b, (((contract[0],), (contract[1],)), ((), ())), preferred_element_type=F32
    )


def call(kernel, outs, *args, scratch=(), smem=(), aliases=None):
    vmem, scalar = pl.BlockSpec(memory_space=pltpu.VMEM), pl.BlockSpec(memory_space=pltpu.SMEM)
    return pl.pallas_call(
        kernel,
        out_shape=[jax.ShapeDtypeStruct(shape, kind) for shape, kind in outs],
        in_specs=[scalar if i in smem else vmem for i in range(len(args))],
        out_specs=[vmem] * len(outs),
        scratch_shapes=[pltpu.VMEM(shape, kind) for shape, kind in scratch],
        input_output_aliases=aliases or {},
        compiler_params=pltpu.CompilerParams(vmem_limit_bytes=24 * 2**20),
    )(*args)


def order_rows(rows_ref, places_ref, out_ref, tiles):
    n_tiles, n_gy, n_groups = tiles.shape[0], out_ref.shape[0], out_ref.shape[2] // LANES
    for t in range(n_tiles):
        tiles[t] = rows_ref[:, t * LANES : (t + 1) * LANES].astype(F32)
    slot = lax.broadcasted_iota(jnp.int32, (8, LANES), 1) // 8

    def one(b, carry):
        for group in range(n_groups):
            block = jnp.zeros((8, LANES), F32)
            for q in range(16):
                place = places_ref[(group * 16 + q) * n_gy + b]
                tile = tiles[lax.shift_right_logical(place, 4)]
                turned = pltpu.roll(tile, ((q + 16 - (place & 15)) & 15) * 8, 1)
                block = jnp.where(slot == q, turned, block)
            out_ref[b, :, group * LANES : (group + 1) * LANES] = block
        return carry

    lax.fori_loop(0, n_gy, one, 0)


def make_edges(values_ref, stiff_ref, turned_ref, lists_ref, up_ref, down_ref, left_ref, right_ref):
    lists = lists_ref[...]
    component, i, j = lists >> 8, (lists >> 4) & 15, lists & 15
    codes = (
        component * 32 + i * 16 + j,
        component * 32 + (i - 14) * 16 + j,
        component * 128 + i * 8 + j,
        component * 128 + i * 8 + j - 8,
    )
    for side, ref in enumerate((up_ref, down_ref, left_ref, right_ref)):
        first = 0 if side in (0, 2) else CELLS - 2
        for c in range(COMPONENTS):
            for layer in range(2):
                if side < 2:
                    rows = pl.ds(c * 256 + (first + layer) * CELLS, CELLS)
                else:
                    rows = pl.ds(c * 256 + first + layer, CELLS, stride=CELLS)
                ref[pl.ds((c * 2 + layer) * CELLS, CELLS), :] = values_ref[rows, :]
        for layer in range(2):
            source = turned_ref if side < 2 else stiff_ref
            one = source[:, first + layer : first + layer + 1]
            ref[pl.ds(STRIP + layer * CELLS, CELLS), :] = jnp.broadcast_to(one, (CELLS, LANES))
        code = (codes[side][side : side + 1] + 1).astype(F32)
        ref[pl.ds(STRIP + 2 * CELLS, 8), 0:MARGIN] = jnp.broadcast_to(code, (8, MARGIN))


def restrict(own, strips, beside, across_ref, along_ref, basis_ref, sub_ref, coarse_ref):
    sub_ref[OWN : OWN + 2 * MARGIN] = matmul(across_ref[...], strips.astype(BF16), (0, 0)).astype(BF16)
    sub_ref[OWN + 2 * MARGIN :] = matmul(along_ref[...], beside.astype(BF16), (0, 0)).astype(BF16)
    coarse = matmul(basis_ref[...], sub_ref[...]).astype(BF16).astype(F32)
    for a in range(coarse_ref.shape[0]):
        coarse_ref[a] = coarse


def start_pass(
    values_ref, up_ref, down_ref, left_ref, right_ref, stiff_ref, turned_ref, basis_ref,
    field_ref, diagonal_ref, across_ref, along_ref, sub_ref, coarse_ref,
):
    field_ref[...] = jnp.zeros_like(field_ref)
    diagonal_ref[...] = jnp.full(diagonal_ref.shape, 4.0, F32)
    for c in range(COMPONENTS):
        for i in range(CELLS):
            rows = values_ref[c * 256 + i * CELLS : c * 256 + (i + 1) * CELLS]
            field_ref[pl.ds(at(c, i), CELLS), :] = rows
            sub_ref[c * 256 + i * CELLS : c * 256 + (i + 1) * CELLS] = rows.astype(BF16)
        for layer in range(2):
            rows = pl.ds((c * 2 + layer) * CELLS, CELLS)
            field_ref[pl.ds(at(c, layer - 2), CELLS), :] = up_ref[rows, :]
            field_ref[pl.ds(at(c, layer + CELLS), CELLS), :] = down_ref[rows, :]
            field_ref[column_of(c, layer - 2), :] = left_ref[rows, :]
            field_ref[column_of(c, layer + CELLS), :] = right_ref[rows, :]
    for i in range(CELLS):
        diagonal_ref[pl.ds(at(0, i), CELLS), :] += jnp.broadcast_to(turned_ref[:, i : i + 1], (CELLS, LANES))
    for layer in range(2):
        rows = pl.ds(STRIP + layer * CELLS, CELLS)
        diagonal_ref[pl.ds(at(0, layer - 2), CELLS), :] += up_ref[rows, :]
        diagonal_ref[pl.ds(at(0, layer + CELLS), CELLS), :] += down_ref[rows, :]
        diagonal_ref[column_of(0, layer - 2), :] += left_ref[rows, :]
        diagonal_ref[column_of(0, layer + CELLS), :] += right_ref[rows, :]

    def chosen(ref, rows):
        code = ref[STRIP + 2 * CELLS : STRIP + 2 * CELLS + 1, 0:MARGIN]
        spot = lax.broadcasted_iota(jnp.int32, (rows, MARGIN), 0).astype(F32) + 1.0
        return jnp.where(spot == code, 1.0, 0.0)

    none = jnp.zeros((STRIP, MARGIN), F32)
    across_ref[...] = jnp.concatenate(
        [
            jnp.concatenate([chosen(up_ref, STRIP), none], axis=1),
            jnp.concatenate([none, chosen(down_ref, STRIP)], axis=1),
        ],
        axis=0,
    ).astype(BF16)
    along_ref[...] = jnp.concatenate(
        [chosen(left_ref, BESIDE), chosen(right_ref, BESIDE)], axis=1
    ).astype(BF16)
    strips = jnp.concatenate([up_ref[0:STRIP], down_ref[0:STRIP]], axis=0)
    beside = jnp.concatenate(
        [field_ref[pl.ds(at(c, i, CELLS), 8), :] for c in range(COMPONENTS) for i in range(CELLS)], axis=0
    )
    restrict(None, strips, beside, across_ref, along_ref, basis_ref, sub_ref, coarse_ref)


def cross_multiply(rows_ref, column_ref, parts_ref):
    n_gy, k, width = rows_ref.shape
    rows = rows_ref[...].reshape(n_gy * k, width).astype(BF16)
    parts_ref[...] = matmul(rows, column_ref[...].reshape(width, LANES).astype(BF16)).reshape(parts_ref.shape)


def apply_patch(sub_ref, inverse_ref, basis_ref, parts_ref, across_ref, along_ref, field_ref, up_ref, down_ref, patch):
    coarse = jnp.sum(parts_ref[...], axis=0).astype(BF16)
    patch[...] = matmul(inverse_ref[...], sub_ref[...]) + matmul(basis_ref[...], coarse, (0, 0))
    field_ref[...] = jnp.zeros_like(field_ref)
    across = matmul(across_ref[...], patch[OWN : OWN + 2 * MARGIN].astype(BF16))
    along = matmul(along_ref[...], patch[OWN + 2 * MARGIN :].astype(BF16))
    for c in range(COMPONENTS):
        for i in range(CELLS):
            n = c * CELLS + i
            field_ref[pl.ds(at(c, i), CELLS), :] = patch[n * CELLS : (n + 1) * CELLS]
            field_ref[pl.ds(at(c, i, CELLS), 8), :] = along[n * 8 : (n + 1) * 8]
        for layer in range(2):
            n = (c * 2 + layer) * CELLS
            field_ref[pl.ds(at(c, layer - 2), CELLS), :] = across[n : n + CELLS]
            field_ref[pl.ds(at(c, layer + CELLS), CELLS), :] = across[STRIP + n : STRIP + n + CELLS]
        up_ref[c * PART : (c + 1) * PART] = field_ref[pl.ds(at(c, -2), PART), :].astype(BF16)
        down_ref[c * PART : (c + 1) * PART] = field_ref[pl.ds(at(c, CELLS - 3), PART), :].astype(BF16)


def add_across(field_ref, up_ref, down_ref, out_ref, left_ref, right_ref, strip):
    out_ref[...] = field_ref[...]
    for c in range(COMPONENTS):
        part = slice(c * PART, (c + 1) * PART)
        out_ref[pl.ds(at(c, -3), 5 * SIDE), :] += up_ref[part].astype(F32)[: 5 * SIDE]
        out_ref[pl.ds(at(c, CELLS - 2), 5 * SIDE), :] += down_ref[part].astype(F32)[: 5 * SIDE]
    for first, ref in ((-2, left_ref), (CELLS - 3, right_ref)):
        for c in range(COMPONENTS):
            for q in range(5):
                strip[pl.ds(q * SIDE, SIDE), :] = out_ref[column_of(c, first + q, -ABOVE, SIDE), :]
            strip[5 * SIDE :] = jnp.zeros((PART - 5 * SIDE, LANES), F32)
            ref[c * PART : (c + 1) * PART] = strip[...].astype(BF16)


def add_along(field_ref, left_ref, right_ref):
    for c in range(COMPONENTS):
        for first, ref in ((-3, left_ref), (CELLS - 2, right_ref)):
            came = ref[c * PART : (c + 1) * PART].astype(F32)
            for q in range(5):
                where = column_of(c, first + q, -ABOVE, SIDE)
                field_ref[where, :] = field_ref[where, :] + came[q * SIDE : (q + 1) * SIDE]


def operate_row(field, diagonal_ref, c, i):
    here = field(c, i)
    beside = field(c, i - 1) + field(c, i + 1) + pltpu.roll(here, 1, 0) + pltpu.roll(here, SIDE - 1, 0)
    return diagonal_ref[pl.ds(at(0, i), SIDE), :] * here - beside


def middle_pass(
    field_ref, left_ref, right_ref, values_ref, diagonal_ref, across_ref, along_ref, basis_ref,
    first_ref, sub_ref, coarse_ref, strips, beside,
):
    first_ref[...] = field_ref[...]
    add_along(first_ref, left_ref, right_ref)

    def field(c, i):
        return first_ref[pl.ds(at(c, i), SIDE), :]

    for c in range(COMPONENTS):
        for i in range(-2, CELLS + 2):
            middle = values_ref[pl.ds(at(c, i), SIDE), :] - operate_row(field, diagonal_ref, c, i)
            if 0 <= i < CELLS:
                n = c * CELLS + i
                sub_ref[n * CELLS : (n + 1) * CELLS] = middle[:CELLS].astype(BF16)
                beside[pl.ds(n * 8, 8), :] = middle[CELLS:]
            else:
                n = (c * 2 + (i + 2 if i < 0 else i - CELLS)) * CELLS + (0 if i < 0 else STRIP)
                strips[pl.ds(n, CELLS), :] = middle[:CELLS]
    restrict(None, strips[...], beside[...], across_ref, along_ref, basis_ref, sub_ref, coarse_ref)


def last_pass(field_ref, left_ref, right_ref, first_ref, values_ref, diagonal_ref, solution_ref, final_ref, total):
    total[...] = field_ref[...]
    add_along(total, left_ref, right_ref)
    total[...] += first_ref[...]

    def field(c, i):
        return total[pl.ds(at(c, i), SIDE), :]

    for c in range(COMPONENTS):
        for i in range(CELLS):
            rows = slice((c * CELLS + i) * CELLS, (c * CELLS + i + 1) * CELLS)
            solution_ref[rows] = total[pl.ds(at(c, i), CELLS), :]
            applied = operate_row(field, diagonal_ref, c, i)[:CELLS]
            final_ref[rows] = values_ref[pl.ds(at(c, i), CELLS), :] - applied


def trade(lower, upper, axis):
    count = lax.axis_size(axis)
    forward = [(i, i + 1) for i in range(count - 1)]
    backward = [(target, source) for source, target in forward]
    return lax.ppermute(upper, axis, forward), lax.ppermute(lower, axis, backward)


def per_device(residual, stiffness, local_inverse, coarse_basis, coarse_rows, send_rows, partition_map):
    inverse, basis, lists = local_inverse[0, 0], coarse_basis[0, 0], send_rows[0, 0]
    k, order = coarse_rows.shape[2:]
    n_gx, n_gy = lax.axis_size("gx"), lax.axis_size("gy")
    values = residual.reshape(OWN, LANES)
    turned = stiffness.T
    swap = functools.partial(lax.all_to_all, split_axis=0, concat_axis=0, tiled=True)

    edge = ((EDGE, LANES), F32)
    up, down, left, right = call(make_edges, [edge] * 4, values, stiffness, turned, lists)
    [crossing] = call(
        order_rows, [((n_gy, k, n_gx * k), F32)], coarse_rows[0, 0], partition_map,
        scratch=[((order // LANES, k, LANES), F32)], smem=(1,),
    )
    crossing = swap(crossing, "gy")
    up, down = trade(up, down, "gx")
    left, right = trade(left, right, "gy")

    field = ((FIELD, LANES), F32)
    copies = ((n_gx, k, LANES), F32)
    sub_kind = ((OWN + 4 * MARGIN, LANES), BF16)
    part = ((TRADE, LANES), BF16)
    ambient, diagonal, across, along, sub, coarse = call(
        start_pass,
        [field, ((PLANE, LANES), F32), ((2 * STRIP, 2 * MARGIN), BF16), ((BESIDE, 2 * MARGIN), BF16), sub_kind, copies],
        values, up, down, left, right, stiffness, turned, basis,
    )

    def correct(sub, coarse):
        [parts] = call(cross_multiply, [((n_gy, k, LANES), F32)], crossing, swap(coarse, "gx"))
        y, to_up, to_down = call(
            apply_patch, [field, part, part], sub, inverse, basis, swap(parts, "gy"), across, along,
            scratch=[((OWN + 4 * MARGIN, LANES), F32)],
        )
        y, to_left, to_right = call(
            add_across, [field, part, part], y, *trade(to_up, to_down, "gx"),
            scratch=[((PART, LANES), F32)],
        )
        return (y, *trade(to_left, to_right, "gy"))

    first, sub, coarse = call(
        middle_pass, [field, sub_kind, copies], *correct(sub, coarse), ambient, diagonal, across, along, basis,
        scratch=[((2 * STRIP, LANES), F32), ((BESIDE, LANES), F32)],
    )
    own = ((OWN, LANES), F32)
    total, final = call(
        last_pass, [own, own], *correct(sub, coarse), first, ambient, diagonal, scratch=[field]
    )
    return total.reshape(residual.shape), final.reshape(residual.shape)


def solution(mesh):
    placed = (
        P(None, "gx", "gy", None),
        P("gx", "gy"),
        P("gx", "gy", None, None),
        P("gx", "gy", None, None),
        P("gx", "gy", None, None),
        P("gx", "gy", None, None),
        P(),
    )
    return jax.shard_map(
        per_device,
        mesh=mesh,
        in_specs=placed,
        out_specs=(P(None, "gx", "gy", None), P(None, "gx", "gy", None)),
        check_vma=False,
    )
```

time: 488 us -> 164 us (0.34)
  waiting for transfers between devices: 348 us -> 24.5 us
  blocking collectives: 0 us -> 75.4 us
  starting transfers between devices: 74.1 us -> 43.4 us
  other arithmetic: 14.4 us -> 0 us
  between operations: 14.8 us -> 0.87 us
  local copies, waits for them, and re-layouts: 22.8 us -> 9.94 us
  Pallas kernels: 0 us -> 8.59 us
  matrix products: 8.25 us -> 0 us
    all_gather x2 -> x0, waiting for transfers between devices: 332 us -> none  [coarse_solve(): lax.all_gather(coarse_in, ('gx', 'gy'), axis=0, tiled=True)]
    all_to_all x0 -> x4, blocking collectives: none -> 75.4 us  [the longest x2 54.6 us: correct(): swap(coarse, 'gx')]
    ppermute x24 -> x12, starting transfers between devices: 74 us -> 36.6 us  [the longest x6 24.8 us: trade(): lax.ppermute(upper, axis, forward)]
    scatter-add x8 -> x0, other arithmetic: 9.12 us -> none  [the longest x2 2.29 us: precondition(): update = update.at[row_lists[0]].add(back_gx[0])]
    pallas_call x0 -> x11, Pallas kernels: none -> 8.59 us  [call(): pl.pallas_call(kernel, out_shape=[jax.ShapeDtypeStruct(shape, kind) for s...]
    ppermute x24 -> x12, waiting for transfers between devices: 15.9 us -> 24.5 us  [the longest x6 24.5 us: trade(): lax.ppermute(lower, axis, backward)]
    dot_general x6 -> x0, matrix products: 8.25 us -> none  [the longest x2 3.47 us: precondition(): lax.dot_general(basis_rows, coarse_out, (((0,), (0,)), ((), ())), preferr...]
    unnamed x47 -> x31, local copies, waits for them, and re-layouts: 2.13 us -> 9.94 us
  transfers between devices with their start and end apart: 26 -> 13, of which waited for: 9 -> 5; matrix products, arithmetic and copies ran while one was open for 4% -> 0% of each run, Pallas kernels for 0% -> 0%
where the time goes in v2:
time: 164 us; the launch traced here: 163 us
  blocking collectives  75.4 us (46%)
  starting transfers between devices  43.4 us (26%)
  waiting for transfers between devices  24.5 us (15%)
  local copies, waits for them, and re-layouts  9.94 us (6%)
  Pallas kernels  8.59 us (5%)
    all_to_all x2, blocking collectives, correct(): swap(coarse, 'gx')  54.6 us
    ppermute x6, starting transfers between devices, trade(): lax.ppermute(upper, axis, forward)  24.8 us
    ppermute x6, waiting for transfers between devices, trade(): lax.ppermute(lower, axis, backward)  24.5 us
    all_to_all x2, blocking collectives, correct(): swap(parts, 'gy')  20.8 us
    ppermute x6, starting transfers between devices, trade(): lax.ppermute(lower, axis, backward)  11.8 us
    unnamed x31, local copies, waits for them, and re-layouts  9.94 us
    pallas_call x11, Pallas kernels, call(): pl.pallas_call(kernel, out_shape=[jax.ShapeDtypeStruct(shape, kind) for s...  8.59 us
    all_to_all x1, starting transfers between devices, per_device(): crossing = swap(crossing, 'gy')  6.86 us
  transfers between devices with their start and end apart: 13, of which 5 were waited for; matrix products, arithmetic and copies ran while one was open for 0% of the time, Pallas kernels for 0%

profile of v2, /device:TPU:7, one launch (start us, length us, event | category | flops | bytes accessed | tf_op | source)
XLA Modules:
  0.0 162.7 jit_solution(1888098658454453121)
XLA Ops:
  0.7 1.0 copy-done.12
  2.3 3.6 %shard_map.88 = f32[16,8,256]{2,1,0:T(8,128)} custom-call(bf16[8,4096]{1,0:T(8,128)(2,1)S(1)} %bitcast.18, s32[512]{0:T(512)S(1)} %copy-done.13), custom_call_target="tpu_custom_call" | custom-call | tf_op jit(solution)/shard_map/pallas_call | solution.py:40
  5.9 6.9 %all-to-all-start = ((f32[16,8,256]{2,1,0:T(8,128)}), f32[16,8,256]{2,1,0:T(8,128)S(1)}, u32[]{:S(2)}, u32[]{:S(2)}) async-start(f32[16,8,256]{2,1,0:T(8,128)} %shard_map.88), calls=%async_computation | async-start | bytes 262144 | tf_op jit(solution)/shard_map/all_to_all | solution.py:268
  12.8 0.8 copy.9
  13.5 1.0 copy-done.1
  16.0 4.7 %collective-permute-start = (f32[136,128]{1,0:T(8,128)S(1)}, f32[136,128]{1,0:T(8,128)S(1)}, u32[]{:S(2)}, u32[]{:S(2)}) collective-permute-start(f32[136,128]{1,0:T(8,128)S(1)} %get-tuple-element.29), channel_id=1, source_target_pairs={{0,16},{16,32},{32,48},{48,64},{64,80},{80,96},{96,112},{112,128},... | collective-permute-start | bytes 208904 | tf_op jit(solution)/shard_map/ppermute | solution.py:251
  20.7 1.9 %collective-permute-start.1 = (f32[136,128]{1,0:T(8,128)S(1)}, f32[136,128]{1,0:T(8,128)S(1)}, u32[]{:S(2)}, u32[]{:S(2)}) collective-permute-start(f32[136,128]{1,0:T(8,128)S(1)} %get-tuple-element.30), channel_id=1, source_target_pairs={{16,0},{32,16},{48,32},{64,48},{80,64},{96,80},{112,96},{128,112},... | collective-permute-start | bytes 208904 | tf_op jit(solution)/shard_map/ppermute | solution.py:251
  22.6 3.1 %collective-permute-start.2 = (f32[136,128]{1,0:T(8,128)S(1)}, f32[136,128]{1,0:T(8,128)S(1)}, u32[]{:S(2)}, u32[]{:S(2)}) collective-permute-start(f32[136,128]{1,0:T(8,128)S(1)} %get-tuple-element.31), channel_id=1, source_target_pairs={{0,1},{1,2},{2,3},{3,4},{4,5},{5,6},{6,7},{7,8},{8,9},{9,10},{10,1... | collective-permute-start | bytes 208904 | tf_op jit(solution)/shard_map/ppermute | solution.py:251
  25.7 2.2 %collective-permute-start.3 = (f32[136,128]{1,0:T(8,128)S(1)}, f32[136,128]{1,0:T(8,128)S(1)}, u32[]{:S(2)}, u32[]{:S(2)}) collective-permute-start(f32[136,128]{1,0:T(8,128)S(1)} %get-tuple-element.32), channel_id=1, source_target_pairs={{1,0},{2,1},{3,2},{4,3},{5,4},{6,5},{7,6},{8,7},{9,8},{10,9},{11,1... | collective-permute-start | bytes 208904 | tf_op jit(solution)/shard_map/ppermute | solution.py:251
  27.9 5.4 %collective-permute-done.3.right_ref = f32[136,128]{1,0:T(8,128)S(1)} collective-permute-done((f32[136,128]{1,0:T(8,128)S(1)}, f32[136,128]{1,0:T(8,128)S(1)}, u32[]{:S(2)}, u32[]{:S(2)}) %collective-permute-start.3) | collective-permute-done | bytes 69664 | tf_op jit(solution)/shard_map/ppermute | solution.py:251
  33.4 0.7 copy-done.2
  37.3 33.5 %all_to_all.25.column_ref = f32[32,8,128]{2,1,0:T(8,128)S(1)} all-to-all(f32[32,8,128]{2,1,0:T(8,128)} %copy-done.7), channel_id=1, replica_groups=mesh['gx'=32,'gy'=16] {'gx'}, dimensions={0} | all-to-all | bytes 262144 | tf_op jit(solution)/shard_map/all_to_all | solution.py:283
  70.9 10.7 %all_to_all.26.parts_ref = f32[16,8,128]{2,1,0:T(8,128)S(1)} all-to-all(f32[16,8,128]{2,1,0:T(8,128)S(1)} %shard_map.89), channel_id=1, replica_groups=mesh['gx'=32,'gy'=16] {'gy'}, dimensions={0} | all-to-all | bytes 131072 | tf_op jit(solution)/shard_map/all_to_all | solution.py:285
  81.6 0.7 copy-done.3
  82.4 0.9 copy-done.6
  83.3 1.0 shard_map.90
  84.3 4.9 %collective-permute-start.4 = (bf16[384,128]{1,0:T(8,128)(2,1)S(1)}, bf16[384,128]{1,0:T(8,128)(2,1)S(1)}, u32[]{:S(2)}, u32[]{:S(2)}) collective-permute-start(bf16[384,128]{1,0:T(8,128)(2,1)S(1)} %get-tuple-element.38), channel_id=1, source_target_pairs={{0,16},{16,32},{32,48},{48,64},{64,80},{80,96},{96,112},{112,128},... | collective-permute-start | bytes 294920 | tf_op jit(solution)/shard_map/ppermute | solution.py:251
  89.2 1.9 %collective-permute-start.5 = (bf16[384,128]{1,0:T(8,128)(2,1)S(1)}, bf16[384,128]{1,0:T(8,128)(2,1)S(1)}, u32[]{:S(2)}, u32[]{:S(2)}) collective-permute-start(bf16[384,128]{1,0:T(8,128)(2,1)S(1)} %get-tuple-element.39), channel_id=1, source_target_pairs={{16,0},{32,16},{48,32},{64,48},{80,64},{96,80},{112,96},{128,112},... | collective-permute-start | bytes 294920 | tf_op jit(solution)/shard_map/ppermute | solution.py:251
  91.1 4.0 %collective-permute-done.5.down_ref = bf16[384,128]{1,0:T(8,128)(2,1)S(1)} collective-permute-done((bf16[384,128]{1,0:T(8,128)(2,1)S(1)}, bf16[384,128]{1,0:T(8,128)(2,1)S(1)}, u32[]{:S(2)}, u32[]{:S(2)}) %collective-permute-start.5) | collective-permute-done | bytes 98336 | tf_op jit(solution)/shard_map/ppermute | solution.py:251
  95.3 3.7 %collective-permute-start.6 = (bf16[384,128]{1,0:T(8,128)(2,1)S(1)}, bf16[384,128]{1,0:T(8,128)(2,1)S(1)}, u32[]{:S(2)}, u32[]{:S(2)}) collective-permute-start(bf16[384,128]{1,0:T(8,128)(2,1)S(1)} %get-tuple-element.41), channel_id=1, source_target_pairs={{0,1},{1,2},{2,3},{3,4},{4,5},{5,6},{6,7},{7,8},{8,9},{9,10},{10,1... | collective-permute-start | bytes 294920 | tf_op jit(solution)/shard_map/ppermute | solution.py:251
  98.9 1.9 %collective-permute-start.7 = (bf16[384,128]{1,0:T(8,128)(2,1)S(1)}, bf16[384,128]{1,0:T(8,128)(2,1)S(1)}, u32[]{:S(2)}, u32[]{:S(2)}) collective-permute-start(bf16[384,128]{1,0:T(8,128)(2,1)S(1)} %get-tuple-element.42), channel_id=1, source_target_pairs={{1,0},{2,1},{3,2},{4,3},{5,4},{6,5},{7,6},{8,7},{9,8},{10,9},{11,1... | collective-permute-start | bytes 294920 | tf_op jit(solution)/shard_map/ppermute | solution.py:251
  100.9 5.5 %collective-permute-done.7.right_ref = bf16[384,128]{1,0:T(8,128)(2,1)S(1)} collective-permute-done((bf16[384,128]{1,0:T(8,128)(2,1)S(1)}, bf16[384,128]{1,0:T(8,128)(2,1)S(1)}, u32[]{:S(2)}, u32[]{:S(2)}) %collective-permute-start.7) | collective-permute-done | bytes 98336 | tf_op jit(solution)/shard_map/ppermute | solution.py:251
  107.1 21.1 %all_to_all.27.column_ref = f32[32,8,128]{2,1,0:T(8,128)S(1)} all-to-all(f32[32,8,128]{2,1,0:T(8,128)S(1)} %get-tuple-element.46), channel_id=1, replica_groups=mesh['gx'=32,'gy'=16] {'gx'}, dimensions={0} | all-to-all | bytes 262144 | tf_op jit(solution)/shard_map/all_to_all | solution.py:283
  128.3 10.1 %all_to_all.28.parts_ref = f32[16,8,128]{2,1,0:T(8,128)S(1)} all-to-all(f32[16,8,128]{2,1,0:T(8,128)S(1)} %shard_map.93), channel_id=1, replica_groups=mesh['gx'=32,'gy'=16] {'gy'}, dimensions={0} | all-to-all | bytes 131072 | tf_op jit(solution)/shard_map/all_to_all | solution.py:285
  138.4 1.0 shard_map.94
  139.5 4.9 %collective-permute-start.8 = (bf16[384,128]{1,0:T(8,128)(2,1)S(1)}, bf16[384,128]{1,0:T(8,128)(2,1)S(1)}, u32[]{:S(2)}, u32[]{:S(2)}) collective-permute-start(bf16[384,128]{1,0:T(8,128)(2,1)S(1)} %get-tuple-element.48), channel_id=1, source_target_pairs={{0,16},{16,32},{32,48},{48,64},{64,80},{80,96},{96,112},{112,128},... | collective-permute-start | bytes 294920 | tf_op jit(solution)/shard_map/ppermute | solution.py:251
  144.3 1.9 %collective-permute-start.9 = (bf16[384,128]{1,0:T(8,128)(2,1)S(1)}, bf16[384,128]{1,0:T(8,128)(2,1)S(1)}, u32[]{:S(2)}, u32[]{:S(2)}) collective-permute-start(bf16[384,128]{1,0:T(8,128)(2,1)S(1)} %get-tuple-element.49), channel_id=1, source_target_pairs={{16,0},{32,16},{48,32},{64,48},{80,64},{96,80},{112,96},{128,112},... | collective-permute-start | bytes 294920 | tf_op jit(solution)/shard_map/ppermute | solution.py:251
  146.3 4.0 %collective-permute-done.9.down_ref = bf16[384,128]{1,0:T(8,128)(2,1)S(1)} collective-permute-done((bf16[384,128]{1,0:T(8,128)(2,1)S(1)}, bf16[384,128]{1,0:T(8,128)(2,1)S(1)}, u32[]{:S(2)}, u32[]{:S(2)}) %collective-permute-start.9) | collective-permute-done | bytes 98336 | tf_op jit(solution)/shard_map/ppermute | solution.py:251
  150.4 3.7 %collective-permute-start.10 = (bf16[384,128]{1,0:T(8,128)(2,1)S(1)}, bf16[384,128]{1,0:T(8,128)(2,1)S(1)}, u32[]{:S(2)}, u32[]{:S(2)}) collective-permute-start(bf16[384,128]{1,0:T(8,128)(2,1)S(1)} %get-tuple-element.51), channel_id=1, source_target_pairs={{0,1},{1,2},{2,3},{3,4},{4,5},{5,6},{6,7},{7,8},{8,9},{9,10},{10,1... | collective-permute-start | bytes 294920 | tf_op jit(solution)/shard_map/ppermute | solution.py:251
  154.0 1.9 %collective-permute-start.11 = (bf16[384,128]{1,0:T(8,128)(2,1)S(1)}, bf16[384,128]{1,0:T(8,128)(2,1)S(1)}, u32[]{:S(2)}, u32[]{:S(2)}) collective-permute-start(bf16[384,128]{1,0:T(8,128)(2,1)S(1)} %get-tuple-element.52), channel_id=1, source_target_pairs={{1,0},{2,1},{3,2},{4,3},{5,4},{6,5},{7,6},{8,7},{9,8},{10,9},{11,1... | collective-permute-start | bytes 294920 | tf_op jit(solution)/shard_map/ppermute | solution.py:251
  156.0 5.5 %collective-permute-done.11.right_ref = bf16[384,128]{1,0:T(8,128)(2,1)S(1)} collective-permute-done((bf16[384,128]{1,0:T(8,128)(2,1)S(1)}, bf16[384,128]{1,0:T(8,128)(2,1)S(1)}, u32[]{:S(2)}, u32[]{:S(2)}) %collective-permute-start.11) | collective-permute-done | bytes 98336 | tf_op jit(solution)/shard_map/ppermute | solution.py:251
  161.5 1.2 shard_map.96
  (40 shorter events, 6.6 us)
Async XLA Ops:
  0.6 81.0 %copy-start = (bf16[1,1,1024,1024]{3,2,1,0:T(8,128)(2,1)S(1)}, bf16[1,1,1024,1024]{3,2,1,0:T(8,128)(2,1)}, u32[]{:S(2)}) copy-start(bf16[1,1,1024,1024]{3,2,1,0:T(8,128)(2,1)} %param.9) | copy-start | bytes 6291460
  0.6 1.0 copy-start.12
  1.6 0.7 copy-start.13
  5.9 31.4 %all-to-all-start = ((f32[16,8,256]{2,1,0:T(8,128)}), f32[16,8,256]{2,1,0:T(8,128)S(1)}, u32[]{:S(2)}, u32[]{:S(2)}) async-start(f32[16,8,256]{2,1,0:T(8,128)} %shard_map.88), calls=%async_computation | async-start | bytes 262144 | tf_op jit(solution)/shard_map/all_to_all | solution.py:268
  13.5 19.8 %copy-start.10 = (f32[16,16]{0,1:T(8,128)}, f32[16,16]{0,1:T(8,128)S(1)}, u32[]{:S(2)}) copy-start(f32[16,16]{0,1:T(8,128)S(1)} %copy.9) | copy-start | bytes 3076
  13.5 1.0 copy-start.1
  14.5 0.7 copy-start.8
  15.2 0.7 copy-start.14
  16.0 11.9 %collective-permute-start = (f32[136,128]{1,0:T(8,128)S(1)}, f32[136,128]{1,0:T(8,128)S(1)}, u32[]{:S(2)}, u32[]{:S(2)}) collective-permute-start(f32[136,128]{1,0:T(8,128)S(1)} %get-tuple-element.29), channel_id=1, source_target_pairs={{0,16},{16,32},{32,48},{48,64},{64,80},{80,96},{96,112},{112,128},... | collective-permute-start | bytes 208904 | tf_op jit(solution)/shard_map/ppermute | solution.py:251
  20.7 7.2 %collective-permute-start.1 = (f32[136,128]{1,0:T(8,128)S(1)}, f32[136,128]{1,0:T(8,128)S(1)}, u32[]{:S(2)}, u32[]{:S(2)}) collective-permute-start(f32[136,128]{1,0:T(8,128)S(1)} %get-tuple-element.30), channel_id=1, source_target_pairs={{16,0},{32,16},{48,32},{64,48},{80,64},{96,80},{112,96},{128,112},... | collective-permute-start | bytes 208904 | tf_op jit(solution)/shard_map/ppermute | solution.py:251
  22.6 5.3 %collective-permute-start.2 = (f32[136,128]{1,0:T(8,128)S(1)}, f32[136,128]{1,0:T(8,128)S(1)}, u32[]{:S(2)}, u32[]{:S(2)}) collective-permute-start(f32[136,128]{1,0:T(8,128)S(1)} %get-tuple-element.31), channel_id=1, source_target_pairs={{0,1},{1,2},{2,3},{3,4},{4,5},{5,6},{6,7},{7,8},{8,9},{9,10},{10,1... | collective-permute-start | bytes 208904 | tf_op jit(solution)/shard_map/ppermute | solution.py:251
  25.7 7.6 %collective-permute-start.3 = (f32[136,128]{1,0:T(8,128)S(1)}, f32[136,128]{1,0:T(8,128)S(1)}, u32[]{:S(2)}, u32[]{:S(2)}) collective-permute-start(f32[136,128]{1,0:T(8,128)S(1)} %get-tuple-element.32), channel_id=1, source_target_pairs={{1,0},{2,1},{3,2},{4,3},{5,4},{6,5},{7,6},{8,7},{9,8},{10,9},{11,1... | collective-permute-start | bytes 208904 | tf_op jit(solution)/shard_map/ppermute | solution.py:251
  33.3 0.7 copy-start.2
  34.1 0.7 copy-start.9
  34.8 0.7 copy-start.11
  36.0 0.7 copy-start.5
  36.7 0.6 copy-start.7
  81.6 0.7 copy-start.3
  82.4 0.9 copy-start.6
  84.3 6.8 %collective-permute-start.4 = (bf16[384,128]{1,0:T(8,128)(2,1)S(1)}, bf16[384,128]{1,0:T(8,128)(2,1)S(1)}, u32[]{:S(2)}, u32[]{:S(2)}) collective-permute-start(bf16[384,128]{1,0:T(8,128)(2,1)S(1)} %get-tuple-element.38), channel_id=1, source_target_pairs={{0,16},{16,32},{32,48},{48,64},{64,80},{80,96},{96,112},{112,128},... | collective-permute-start | bytes 294920 | tf_op jit(solution)/shard_map/ppermute | solution.py:251
  89.2 5.9 %collective-permute-start.5 = (bf16[384,128]{1,0:T(8,128)(2,1)S(1)}, bf16[384,128]{1,0:T(8,128)(2,1)S(1)}, u32[]{:S(2)}, u32[]{:S(2)}) collective-permute-start(bf16[384,128]{1,0:T(8,128)(2,1)S(1)} %get-tuple-element.39), channel_id=1, source_target_pairs={{16,0},{32,16},{48,32},{64,48},{80,64},{96,80},{112,96},{128,112},... | collective-permute-start | bytes 294920 | tf_op jit(solution)/shard_map/ppermute | solution.py:251
  95.1 43.3 %copy-start.4 = (bf16[1,1,8,1024]{3,2,1,0:T(8,128)(2,1)S(1)}, bf16[1,1,8,1024]{3,2,1,0:T(8,128)(2,1)}, u32[]{:S(2)}) copy-start(bf16[1,1,8,1024]{3,2,1,0:T(8,128)(2,1)} %param.10) | copy-start | bytes 49156
  95.3 5.6 %collective-permute-start.6 = (bf16[384,128]{1,0:T(8,128)(2,1)S(1)}, bf16[384,128]{1,0:T(8,128)(2,1)S(1)}, u32[]{:S(2)}, u32[]{:S(2)}) collective-permute-start(bf16[384,128]{1,0:T(8,128)(2,1)S(1)} %get-tuple-element.41), channel_id=1, source_target_pairs={{0,1},{1,2},{2,3},{3,4},{4,5},{5,6},{6,7},{7,8},{8,9},{9,10},{10,1... | collective-permute-start | bytes 294920 | tf_op jit(solution)/shard_map/ppermute | solution.py:251
  98.9 7.5 %collective-permute-start.7 = (bf16[384,128]{1,0:T(8,128)(2,1)S(1)}, bf16[384,128]{1,0:T(8,128)(2,1)S(1)}, u32[]{:S(2)}, u32[]{:S(2)}) collective-permute-start(bf16[384,128]{1,0:T(8,128)(2,1)S(1)} %get-tuple-element.42), channel_id=1, source_target_pairs={{1,0},{2,1},{3,2},{4,3},{5,4},{6,5},{7,6},{8,7},{9,8},{10,9},{11,1... | collective-permute-start | bytes 294920 | tf_op jit(solution)/shard_map/ppermute | solution.py:251
  139.5 6.8 %collective-permute-start.8 = (bf16[384,128]{1,0:T(8,128)(2,1)S(1)}, bf16[384,128]{1,0:T(8,128)(2,1)S(1)}, u32[]{:S(2)}, u32[]{:S(2)}) collective-permute-start(bf16[384,128]{1,0:T(8,128)(2,1)S(1)} %get-tuple-element.48), channel_id=1, source_target_pairs={{0,16},{16,32},{32,48},{48,64},{64,80},{80,96},{96,112},{112,128},... | collective-permute-start | bytes 294920 | tf_op jit(solution)/shard_map/ppermute | solution.py:251
  144.3 5.9 %collective-permute-start.9 = (bf16[384,128]{1,0:T(8,128)(2,1)S(1)}, bf16[384,128]{1,0:T(8,128)(2,1)S(1)}, u32[]{:S(2)}, u32[]{:S(2)}) collective-permute-start(bf16[384,128]{1,0:T(8,128)(2,1)S(1)} %get-tuple-element.49), channel_id=1, source_target_pairs={{16,0},{32,16},{48,32},{64,48},{80,64},{96,80},{112,96},{128,112},... | collective-permute-start | bytes 294920 | tf_op jit(solution)/shard_map/ppermute | solution.py:251
  150.4 5.6 %collective-permute-start.10 = (bf16[384,128]{1,0:T(8,128)(2,1)S(1)}, bf16[384,128]{1,0:T(8,128)(2,1)S(1)}, u32[]{:S(2)}, u32[]{:S(2)}) collective-permute-start(bf16[384,128]{1,0:T(8,128)(2,1)S(1)} %get-tuple-element.51), channel_id=1, source_target_pairs={{0,1},{1,2},{2,3},{3,4},{4,5},{5,6},{6,7},{7,8},{8,9},{9,10},{10,1... | collective-permute-start | bytes 294920 | tf_op jit(solution)/shard_map/ppermute | solution.py:251
  154.0 7.5 %collective-permute-start.11 = (bf16[384,128]{1,0:T(8,128)(2,1)S(1)}, bf16[384,128]{1,0:T(8,128)(2,1)S(1)}, u32[]{:S(2)}, u32[]{:S(2)}) collective-permute-start(bf16[384,128]{1,0:T(8,128)(2,1)S(1)} %get-tuple-element.52), channel_id=1, source_target_pairs={{1,0},{2,1},{3,2},{4,3},{5,4},{6,5},{7,6},{8,7},{9,8},{10,9},{11,1... | collective-permute-start | bytes 294920 | tf_op jit(solution)/shard_map/ppermute | solution.py:251

commit v3 on v2

v3 whole, which is shorter than its diff:
```python
import functools

import jax
import jax.numpy as jnp
from jax import lax
from jax.experimental import pallas as pl
from jax.experimental.pallas import tpu as pltpu
from jax.sharding import Mesh
from jax.sharding import PartitionSpec as P

F32, BF16 = jnp.float32, jnp.bfloat16
COMPONENTS, CELLS, LANES = 3, 16, 128
OWN = COMPONENTS * CELLS * CELLS
MARGIN = 64
SIDE, ABOVE = 24, 4
PLANE = SIDE * SIDE
FIELD = COMPONENTS * PLANE
BESIDE = COMPONENTS * CELLS * 8
STRIP = COMPONENTS * 2 * CELLS
EDGE = STRIP + 2 * CELLS + 8
VMEM_BYTES = 8 * 2**20


def part_of(depth):
    return -(-(depth + 2) * SIDE // 16) * 16


def at(component, row, column=0):
    return component * PLANE + (row + ABOVE) * SIDE + column % SIDE


def column_of(component, column, first=0, count=CELLS):
    return pl.ds(at(component, first, column), count, stride=SIDE)


def matmul(a, b, contract=(1, 0)):
    return lax.dot_general(
        a, b, (((contract[0],), (contract[1],)), ((), ())), preferred_element_type=F32
    )


def call(kernel, outs, *args, scratch=(), fetched=0, copies=None, cost=None):
    vmem, hbm = pl.BlockSpec(memory_space=pltpu.VMEM), pl.BlockSpec(memory_space=pltpu.HBM)
    copies = [pltpu.SemaphoreType.DMA((copies or fetched,))] if fetched else []
    return pl.pallas_call(
        kernel,
        out_shape=[jax.ShapeDtypeStruct(shape, kind) for shape, kind in outs],
        in_specs=[hbm if i < fetched else vmem for i in range(len(args))],
        out_specs=[vmem] * len(outs),
        scratch_shapes=[*(pltpu.VMEM(*s) if isinstance(s, tuple) else s for s in scratch), *copies],
        compiler_params=pltpu.CompilerParams(vmem_limit_bytes=VMEM_BYTES),
        cost_estimate=pl.CostEstimate(flops=cost[0], bytes_accessed=cost[1], transcendentals=0) if cost else None,
    )(*(pltpu.with_memory_space_constraint(a, pltpu.HBM) if i < fetched else a for i, a in enumerate(args)))


def fetch(pairs, sems):
    copies = [pltpu.make_async_copy(source, target, sems.at[i]) for i, (source, target) in enumerate(pairs)]
    for copy in copies:
        copy.start()
    for copy in copies:
        copy.wait()


def order_rows(rows_hbm, places_hbm, after_ref, out_ref, rows, places, tiles, sems):
    fetch([(rows_hbm, rows), (places_hbm, places)], sems)
    n_targets, width = out_ref.shape[0], out_ref.shape[2]
    for t in range(tiles.shape[0]):
        tiles[t] = rows[:, t * LANES : (t + 1) * LANES].astype(F32)
    slot = lax.broadcasted_iota(jnp.int32, (8, LANES), 1) // 8

    def one(target, carry):
        block = jnp.zeros((8, LANES), F32)
        for q in range(width // 8):
            place = places[q * n_targets + target]
            tile = tiles[lax.shift_right_logical(place, 4)]
            turned = pltpu.roll(tile, ((q + 16 - (place & 15)) & 15) * 8, 1)
            block = jnp.where(slot == q, turned, block)
        out_ref[target] = block[:, :width]
        return carry

    lax.fori_loop(0, n_targets, one, 0, unroll=8)


def make_edges(
    values_hbm, stiff_hbm, lists_hbm, up_ref, down_ref, left_ref, right_ref, values_ref, stiff_ref, lists_ref, sems
):
    fetch([(values_hbm, values_ref), (stiff_hbm, stiff_ref), (lists_hbm, lists_ref)], sems)
    lists = lists_ref[...]
    stiff = stiff_ref[...]
    turned = stiff.T
    component, i, j = lists >> 8, (lists >> 4) & 15, lists & 15
    codes = (
        component * 32 + i * 16 + j,
        component * 32 + (i - 14) * 16 + j,
        component * 128 + i * 8 + j,
        component * 128 + i * 8 + j - 8,
    )
    for side, ref in enumerate((up_ref, down_ref, left_ref, right_ref)):
        first = 0 if side in (0, 2) else CELLS - 2
        for c in range(COMPONENTS):
            for layer in range(2):
                if side < 2:
                    rows = pl.ds(c * 256 + (first + layer) * CELLS, CELLS)
                else:
                    rows = pl.ds(c * 256 + first + layer, CELLS, stride=CELLS)
                ref[pl.ds((c * 2 + layer) * CELLS, CELLS), :] = values_ref[rows, :]
        for layer in range(2):
            source = turned if side < 2 else stiff
            one = source[:, first + layer : first + layer + 1]
            ref[pl.ds(STRIP + layer * CELLS, CELLS), :] = jnp.broadcast_to(one, (CELLS, LANES))
        code = (codes[side][side : side + 1] + 1).astype(F32)
        ref[pl.ds(STRIP + 2 * CELLS, 8), 0:MARGIN] = jnp.broadcast_to(code, (8, MARGIN))


def restrict(strips, beside, across_ref, along_ref, basis_ref, sub_ref, coarse_ref):
    sub_ref[OWN : OWN + 2 * MARGIN] = matmul(across_ref[...], strips.astype(BF16), (0, 0)).astype(BF16)
    sub_ref[OWN + 2 * MARGIN :] = matmul(along_ref[...], beside.astype(BF16), (0, 0)).astype(BF16)
    coarse = matmul(basis_ref[...], sub_ref[...]).astype(BF16).astype(F32)
    for a in range(coarse_ref.shape[0]):
        coarse_ref[a] = coarse


def start_pass(
    values_hbm, stiff_hbm, basis_hbm, up_ref, down_ref, left_ref, right_ref,
    field_ref, diagonal_ref, across_ref, along_ref, sub_ref, basis_ref, coarse_ref,
    values_ref, stiff_ref, sems,
):
    fetch([(values_hbm, values_ref), (stiff_hbm, stiff_ref), (basis_hbm, basis_ref)], sems)
    turned = stiff_ref[...].T
    field_ref[...] = jnp.zeros_like(field_ref)
    diagonal_ref[...] = jnp.full(diagonal_ref.shape, 4.0, F32)
    for c in range(COMPONENTS):
        for i in range(CELLS):
            rows = values_ref[c * 256 + i * CELLS : c * 256 + (i + 1) * CELLS]
            field_ref[pl.ds(at(c, i), CELLS), :] = rows
            sub_ref[c * 256 + i * CELLS : c * 256 + (i + 1) * CELLS] = rows.astype(BF16)
        for layer in range(2):
            rows = pl.ds((c * 2 + layer) * CELLS, CELLS)
            field_ref[pl.ds(at(c, layer - 2), CELLS), :] = up_ref[rows, :]
            field_ref[pl.ds(at(c, layer + CELLS), CELLS), :] = down_ref[rows, :]
            field_ref[column_of(c, layer - 2), :] = left_ref[rows, :]
            field_ref[column_of(c, layer + CELLS), :] = right_ref[rows, :]
    for i in range(CELLS):
        diagonal_ref[pl.ds(at(0, i), CELLS), :] += jnp.broadcast_to(turned[:, i : i + 1], (CELLS, LANES))
    for layer in range(2):
        rows = pl.ds(STRIP + layer * CELLS, CELLS)
        diagonal_ref[pl.ds(at(0, layer - 2), CELLS), :] += up_ref[rows, :]
        diagonal_ref[pl.ds(at(0, layer + CELLS), CELLS), :] += down_ref[rows, :]
        diagonal_ref[column_of(0, layer - 2), :] += left_ref[rows, :]
        diagonal_ref[column_of(0, layer + CELLS), :] += right_ref[rows, :]

    def chosen(ref, rows):
        code = ref[STRIP + 2 * CELLS : STRIP + 2 * CELLS + 1, 0:MARGIN]
        spot = lax.broadcasted_iota(jnp.int32, (rows, MARGIN), 0).astype(F32) + 1.0
        return jnp.where(spot == code, 1.0, 0.0)

    none = jnp.zeros((STRIP, MARGIN), F32)
    across_ref[...] = jnp.concatenate(
        [
            jnp.concatenate([chosen(up_ref, STRIP), none], axis=1),
            jnp.concatenate([none, chosen(down_ref, STRIP)], axis=1),
        ],
        axis=0,
    ).astype(BF16)
    along_ref[...] = jnp.concatenate(
        [chosen(left_ref, BESIDE), chosen(right_ref, BESIDE)], axis=1
    ).astype(BF16)
    strips = jnp.concatenate([up_ref[0:STRIP], down_ref[0:STRIP]], axis=0)
    beside = jnp.concatenate(
        [field_ref[pl.ds(at(c, i, CELLS), 8), :] for c in range(COMPONENTS) for i in range(CELLS)], axis=0
    )
    restrict(strips, beside, across_ref, along_ref, basis_ref, sub_ref, coarse_ref)


def cross_multiply(rows_ref, column_ref, parts_ref):
    n_gy, k, width = rows_ref.shape
    rows = rows_ref[...].reshape(n_gy * k, width).astype(BF16)
    parts_ref[...] = matmul(rows, column_ref[...].reshape(width, LANES).astype(BF16)).reshape(parts_ref.shape)


def apply_inverse(inverse_hbm, sub_ref, patch_ref, inverse, sems):
    count = sems.shape[0]
    size = inverse.shape[0] // count
    parts = [pl.ds(i * size, size) for i in range(count)]
    chunks = [pltpu.make_async_copy(inverse_hbm.at[p], inverse.at[p], sems.at[i]) for i, p in enumerate(parts)]
    for chunk in chunks:
        chunk.start()
    for chunk, p in zip(chunks, parts):
        chunk.wait()
        patch_ref[p, :] = matmul(inverse[p, :], sub_ref[...])


def spread(depth, local_ref, basis_ref, parts_ref, across_ref, along_ref, field_ref, up_ref, down_ref, patch):
    coarse = jnp.sum(parts_ref[...], axis=0).astype(BF16)
    patch[...] = local_ref[...] + matmul(basis_ref[...], coarse, (0, 0))
    field_ref[...] = jnp.zeros_like(field_ref)
    across = matmul(across_ref[...], patch[OWN : OWN + 2 * MARGIN].astype(BF16))
    along = matmul(along_ref[...], patch[OWN + 2 * MARGIN :].astype(BF16))
    for c in range(COMPONENTS):
        for i in range(CELLS):
            n = c * CELLS + i
            field_ref[pl.ds(at(c, i), CELLS), :] = patch[n * CELLS : (n + 1) * CELLS]
            field_ref[pl.ds(at(c, i, CELLS), 8), :] = along[n * 8 : (n + 1) * 8]
        for layer in range(2):
            n = (c * 2 + layer) * CELLS
            field_ref[pl.ds(at(c, layer - 2), CELLS), :] = across[n : n + CELLS]
            field_ref[pl.ds(at(c, layer + CELLS), CELLS), :] = across[STRIP + n : STRIP + n + CELLS]
        part = part_of(depth)
        up_ref[c * part : (c + 1) * part] = field_ref[pl.ds(at(c, -2), part), :].astype(BF16)
        down_ref[c * part : (c + 1) * part] = field_ref[pl.ds(at(c, CELLS - depth), part), :].astype(BF16)


def add_across(depth, field_ref, up_ref, down_ref, out_ref, left_ref, right_ref, strip):
    part, layers = part_of(depth), depth + 2
    out_ref[...] = field_ref[...]
    for c in range(COMPONENTS):
        for first, ref in ((-depth, up_ref), (CELLS - 2, down_ref)):
            came = ref[c * part : (c + 1) * part].astype(F32)
            out_ref[pl.ds(at(c, first), layers * SIDE), :] += came[: layers * SIDE]
    for first, ref in ((-2, left_ref), (CELLS - depth, right_ref)):
        for c in range(COMPONENTS):
            for q in range(layers):
                strip[pl.ds(q * SIDE, SIDE), :] = out_ref[column_of(c, first + q, -ABOVE, SIDE), :]
            strip[layers * SIDE :] = jnp.zeros((part - layers * SIDE, LANES), F32)
            ref[c * part : (c + 1) * part] = strip[...].astype(BF16)


def add_along(depth, field_ref, left_ref, right_ref):
    part = part_of(depth)
    for c in range(COMPONENTS):
        for first, ref in ((-depth, left_ref), (CELLS - 2, right_ref)):
            came = ref[c * part : (c + 1) * part].astype(F32)
            for q in range(depth + 2):
                where = column_of(c, first + q, -ABOVE, SIDE)
                field_ref[where, :] = field_ref[where, :] + came[q * SIDE : (q + 1) * SIDE]


def operate_row(field, diagonal_ref, c, i):
    here = field(c, i)
    beside = field(c, i - 1) + field(c, i + 1) + pltpu.roll(here, 1, 0) + pltpu.roll(here, SIDE - 1, 0)
    return diagonal_ref[pl.ds(at(0, i), SIDE), :] * here - beside


def middle_pass(
    field_ref, left_ref, right_ref, values_ref, diagonal_ref, across_ref, along_ref, basis_ref,
    first_ref, sub_ref, coarse_ref, strips, beside,
):
    first_ref[...] = field_ref[...]
    add_along(3, first_ref, left_ref, right_ref)

    def field(c, i):
        return first_ref[pl.ds(at(c, i), SIDE), :]

    for c in range(COMPONENTS):
        for i in range(-2, CELLS + 2):
            middle = values_ref[pl.ds(at(c, i), SIDE), :] - operate_row(field, diagonal_ref, c, i)
            if 0 <= i < CELLS:
                n = c * CELLS + i
                sub_ref[n * CELLS : (n + 1) * CELLS] = middle[:CELLS].astype(BF16)
                beside[pl.ds(n * 8, 8), :] = middle[CELLS:]
            else:
                n = (c * 2 + (i + 2 if i < 0 else i - CELLS)) * CELLS + (0 if i < 0 else STRIP)
                strips[pl.ds(n, CELLS), :] = middle[:CELLS]
    restrict(strips[...], beside[...], across_ref, along_ref, basis_ref, sub_ref, coarse_ref)


def last_pass(field_ref, left_ref, right_ref, first_ref, values_ref, diagonal_ref, solution_ref, final_ref, total):
    total[...] = field_ref[...]
    add_along(1, total, left_ref, right_ref)
    total[...] += first_ref[...]

    def field(c, i):
        return total[pl.ds(at(c, i), SIDE), :]

    for c in range(COMPONENTS):
        for i in range(CELLS):
            rows = slice((c * CELLS + i) * CELLS, (c * CELLS + i + 1) * CELLS)
            solution_ref[rows] = total[pl.ds(at(c, i), CELLS), :]
            applied = operate_row(field, diagonal_ref, c, i)[:CELLS]
            final_ref[rows] = values_ref[pl.ds(at(c, i), CELLS), :] - applied


def trade(lower, upper, axis):
    count = lax.axis_size(axis)
    forward = [(i, i + 1) for i in range(count - 1)]
    backward = [(target, source) for source, target in forward]
    return lax.ppermute(upper, axis, forward), lax.ppermute(lower, axis, backward)


GX, GY = ("z", "core"), "gy"
FIRST, SECOND = "z", ("core", "gy")


def per_device(residual, stiffness, local_inverse, coarse_basis, coarse_rows, send_rows, partition_map):
    inverse, basis, lists = local_inverse[0, 0], coarse_basis[0, 0], send_rows[0, 0]
    k, order = coarse_rows.shape[2:]
    n_first, n_second = lax.axis_size(FIRST), lax.axis_size(SECOND)
    values = residual.reshape(OWN, LANES)
    swap = functools.partial(lax.all_to_all, split_axis=0, concat_axis=0, tiled=True)

    own, stiff = ((OWN, LANES), F32), (stiffness.shape, F32)
    edge = ((EDGE, LANES), F32)
    up, down, left, right = call(
        make_edges, [edge] * 4, values, stiffness, lists, fetched=3,
        scratch=[own, stiff, (lists.shape, jnp.int32)],
    )
    [crossing] = call(
        order_rows, [((n_second, k, n_first * k), F32)], coarse_rows[0, 0], partition_map, up, fetched=2,
        scratch=[((k, order), BF16), pltpu.SMEM(partition_map.shape, jnp.int32), ((order // LANES, k, LANES), F32)],
    )
    crossing = swap(crossing, SECOND)
    up, down = trade(up, down, GX)
    left, right = trade(left, right, GY)
    field = ((FIELD, LANES), F32)
    copies = ((n_first, k, LANES), F32)
    sub_kind = ((OWN + 4 * MARGIN, LANES), BF16)
    ambient, diagonal, across, along, sub, basis, coarse = call(
        start_pass,
        [
            field, ((PLANE, LANES), F32), ((2 * STRIP, 2 * MARGIN), BF16), ((BESIDE, 2 * MARGIN), BF16), sub_kind,
            (basis.shape, BF16), copies,
        ],
        values, stiffness, basis, up, down, left, right, fetched=3, scratch=[own, stiff],
    )

    def correct(depth, sub, coarse):
        patch = ((OWN + 4 * MARGIN, LANES), F32)
        [local] = call(
            apply_inverse, [patch], inverse, sub, fetched=1, copies=4, scratch=[(inverse.shape, BF16)],
            cost=(inverse.size * LANES * 2, inverse.size * 2),
        )
        [parts] = call(cross_multiply, [((n_second, k, LANES), F32)], crossing, swap(coarse, FIRST))
        part = ((COMPONENTS * part_of(depth), LANES), BF16)
        y, to_up, to_down = call(
            functools.partial(spread, depth), [field, part, part],
            local, basis, swap(parts, SECOND), across, along, scratch=[patch],
        )
        y, to_left, to_right = call(
            functools.partial(add_across, depth), [field, part, part], y, *trade(to_up, to_down, GX),
            scratch=[((part_of(depth), LANES), F32)],
        )
        return (y, *trade(to_left, to_right, GY))

    first, sub, coarse = call(
        middle_pass, [field, sub_kind, copies], *correct(3, sub, coarse), ambient, diagonal, across, along, basis,
        scratch=[((2 * STRIP, LANES), F32), ((BESIDE, LANES), F32)],
    )
    total, final = call(
        last_pass, [own, own], *correct(1, sub, coarse), first, ambient, diagonal, scratch=[field]
    )
    return total.reshape(residual.shape), final.reshape(residual.shape)


def solution(mesh):
    split = Mesh(mesh.devices.reshape(-1, 2, mesh.devices.shape[1]), ("z", "core", "gy"))
    cells = P(None, GX, GY, None)
    placed = (cells, P(GX, GY), *[P(GX, GY, None, None)] * 4, P())
    return jax.shard_map(per_device, mesh=split, in_specs=placed, out_specs=(cells, cells), check_vma=False)
```

time: 164 us -> 145 us (0.88)
  blocking collectives: 75.4 us -> 43 us
  starting transfers between devices: 43.4 us -> 57.3 us
  local copies, waits for them, and re-layouts: 9.94 us -> 0 us
  Pallas kernels: 8.59 us -> 14.9 us
  waiting for transfers between devices: 24.5 us -> 28.3 us
    all_to_all x4 -> x2, blocking collectives: 75.4 us -> 43 us  [correct(): swap(coarse, FIRST)]
    all_to_all x1 -> x3, starting transfers between devices: 6.86 us -> 24.9 us  [the longest x2 15.1 us: correct(): swap(parts, SECOND)]
    unnamed x31 -> x0, local copies, waits for them, and re-layouts: 9.94 us -> none
    all_to_all x1 -> x3, waiting for transfers between devices: 0.01 us -> 7.2 us  [the longest x2 7.2 us: correct(): swap(parts, SECOND)]
    pallas_call x11 -> x13, Pallas kernels: 8.59 us -> 14.9 us  [call(): pl.pallas_call(kernel, out_shape=[jax.ShapeDtypeStruct(shape, kind) for s...]
    ppermute x6, starting transfers between devices: 24.8 us -> 19.4 us  [trade(): lax.ppermute(upper, axis, forward)]
    ppermute x6, waiting for transfers between devices: 24.5 us -> 21.1 us  [trade(): lax.ppermute(lower, axis, backward)]
  transfers between devices with their start and end apart: 13 -> 15, of which waited for: 5 -> 9; matrix products, arithmetic and copies ran while one was open for 0% -> 0% of each run, Pallas kernels for 0% -> 4%
where the time goes in v3:
time: 145 us; the launch traced here: 144 us
  starting transfers between devices  57.3 us (40%)
  blocking collectives  43 us (30%)
  waiting for transfers between devices  28.3 us (20%)
  Pallas kernels  14.9 us (10%)
    all_to_all x2, blocking collectives, correct(): swap(coarse, FIRST)  43 us
    ppermute x6, waiting for transfers between devices, trade(): lax.ppermute(lower, axis, backward)  21.1 us
    ppermute x6, starting transfers between devices, trade(): lax.ppermute(upper, axis, forward)  19.4 us
    all_to_all x2, starting transfers between devices, correct(): swap(parts, SECOND)  15.1 us
    pallas_call x13, Pallas kernels, call(): pl.pallas_call(kernel, out_shape=[jax.ShapeDtypeStruct(shape, kind) for s...  14.9 us
    ppermute x6, starting transfers between devices, trade(): lax.ppermute(lower, axis, backward)  12.9 us
    all_to_all x1, starting transfers between devices, per_device(): crossing = swap(crossing, SECOND)  9.78 us
    all_to_all x2, waiting for transfers between devices, correct(): swap(parts, SECOND)  7.2 us
  transfers between devices with their start and end apart: 15, of which 9 were waited for; matrix products, arithmetic and copies ran while one was open for 0% of the time, Pallas kernels for 4%

profile of v3, /device:TPU:7, one launch (start us, length us, event | category | flops | bytes accessed | tf_op | source)
XLA Modules:
  0.0 144.3 jit_solution(1226091475286633002)
XLA Ops:
  0.6 1.2 shard_map.86
  1.8 3.1 %shard_map.89 = f32[32,8,128]{2,1,0:T(8,128)} custom-call(bf16[8,4096]{1,0:T(8,128)(2,1)} %bitcast.11, s32[512]{0:T(512)} %places_hbm.1, f32[136,128]{1,0:T(8,128)S(1)} %get-tuple-element.31.after_ref), custom_call_target="tpu_custom_call" | custom-call | tf_op jit(solution)/shard_map/pallas_call | solution.py:45
  5.0 9.8 %all-to-all-start = ((f32[32,8,128]{2,1,0:T(8,128)}), f32[32,8,128]{2,1,0:T(8,128)S(1)}, u32[]{:S(2)}, u32[]{:S(2)}) async-start(f32[32,8,128]{2,1,0:T(8,128)} %shard_map.89), calls=%async_computation | async-start | bytes 262144 | tf_op jit(solution)/shard_map/all_to_all | solution.py:311
  14.8 1.9 %collective-permute-start = (f32[136,128]{1,0:T(8,128)S(1)}, f32[136,128]{1,0:T(8,128)S(1)}, u32[]{:S(2)}, u32[]{:S(2)}) collective-permute-start(f32[136,128]{1,0:T(8,128)S(1)} %get-tuple-element.30), channel_id=1, source_target_pairs={{0,16},{16,32},{32,48},{48,64},{64,80},{80,96},{96,112},{112,128},... | collective-permute-start | bytes 208904 | tf_op jit(solution)/shard_map/ppermute | solution.py:287
  16.7 3.1 %collective-permute-start.2 = (f32[136,128]{1,0:T(8,128)S(1)}, f32[136,128]{1,0:T(8,128)S(1)}, u32[]{:S(2)}, u32[]{:S(2)}) collective-permute-start(f32[136,128]{1,0:T(8,128)S(1)} %get-tuple-element.32), channel_id=1, source_target_pairs={{0,1},{1,2},{2,3},{3,4},{4,5},{5,6},{6,7},{7,8},{8,9},{9,10},{10,1... | collective-permute-start | bytes 208904 | tf_op jit(solution)/shard_map/ppermute | solution.py:287
  19.8 2.2 %collective-permute-start.3 = (f32[136,128]{1,0:T(8,128)S(1)}, f32[136,128]{1,0:T(8,128)S(1)}, u32[]{:S(2)}, u32[]{:S(2)}) collective-permute-start(f32[136,128]{1,0:T(8,128)S(1)} %get-tuple-element.33), channel_id=1, source_target_pairs={{1,0},{2,1},{3,2},{4,3},{5,4},{6,5},{7,6},{8,7},{9,8},{10,9},{11,1... | collective-permute-start | bytes 208904 | tf_op jit(solution)/shard_map/ppermute | solution.py:287
  22.0 3.0 %collective-permute-start.1 = (f32[136,128]{1,0:T(8,128)S(1)}, f32[136,128]{1,0:T(8,128)S(1)}, u32[]{:S(2)}, u32[]{:S(2)}) collective-permute-start(f32[136,128]{1,0:T(8,128)S(1)} %get-tuple-element.31.after_ref), channel_id=1, source_target_pairs={{16,0},{32,16},{48,32},{64,48},{80,64},{96,80},{112,96},{128,112},... | collective-permute-start | bytes 208904 | tf_op jit(solution)/shard_map/ppermute | solution.py:287
  25.0 2.0 %collective-permute-done.3.right_ref = f32[136,128]{1,0:T(8,128)S(1)} collective-permute-done((f32[136,128]{1,0:T(8,128)S(1)}, f32[136,128]{1,0:T(8,128)S(1)}, u32[]{:S(2)}, u32[]{:S(2)}) %collective-permute-start.3) | collective-permute-done | bytes 69664 | tf_op jit(solution)/shard_map/ppermute | solution.py:287
  27.0 1.0 collective-permute-done.1.down_ref
  27.9 1.5 %shard_map.87 = (f32[1728,128]{1,0:T(8,128)S(1)}, f32[576,128]{1,0:T(8,128)S(1)}, bf16[192,128]{1,0:T(8,128)(2,1)S(1)}, bf16[384,128]{1,0:T(8,128)(2,1)S(1)}, bf...) custom-call(f32[768,128]{1,0:T(8,128)} %bitcast.10, f32[16,16]{1,0:T(8,128)} %stiff_hbm.3, ...), custom_call_target="tpu_custom_call" | custom-call | tf_op jit(solution)/shard_map/pallas_call | solution.py:45
  29.5 25.9 %all_to_all.25.column_ref = f32[16,8,128]{2,1,0:T(8,128)S(1)} all-to-all(f32[16,8,128]{2,1,0:T(8,128)S(1)} %get-tuple-element.36), channel_id=1, replica_groups=mesh['z'=16,'core'=2,'gy'=16] {'z'}, dimensions={0} | all-to-all | bytes 131072 | tf_op jit(solution)/shard_map/all_to_all | solution.py:332
  55.4 0.8 shard_map.90
  56.2 8.6 %all-to-all-start.2 = ((f32[32,8,128]{2,1,0:T(8,128)}), f32[32,8,128]{2,1,0:T(8,128)S(1)}, u32[]{:S(2)}, u32[]{:S(2)}) async-start(f32[32,8,128]{2,1,0:T(8,128)} %shard_map.90), calls=%async_computation.2 | async-start | bytes 262144 | tf_op jit(solution)/shard_map/all_to_all | solution.py:336
  64.8 2.2 %shard_map.88.local_ref = f32[1024,128]{1,0:T(8,128)S(1)} custom-call(bf16[1024,1024]{1,0:T(8,128)(2,1)} %bitcast.7, bf16[1024,128]{1,0:T(8,128)(2,1)S(1)} %get-tuple-element.34.sub_ref), custom_call_target="tpu_custom_call" | custom-call | flops 268435456 | bytes 2097152 | tf_op jit(solution)/shard_map/pallas_call | solution.py:45
  67.1 3.6 %all-to-all-done.2.parts_ref = f32[32,8,128]{2,1,0:T(8,128)S(1)} async-done(((f32[32,8,128]{2,1,0:T(8,128)}), f32[32,8,128]{2,1,0:T(8,128)S(1)}, u32[]{:S(2)}, u32[]{:S(2)}) %all-to-all-start.2) | async-done | bytes 131104 | tf_op jit(solution)/shard_map/all_to_all | solution.py:336
  71.2 3.8 %collective-permute-start.4 = (bf16[384,128]{1,0:T(8,128)(2,1)S(1)}, bf16[384,128]{1,0:T(8,128)(2,1)S(1)}, u32[]{:S(2)}, u32[]{:S(2)}) collective-permute-start(bf16[384,128]{1,0:T(8,128)(2,1)S(1)} %get-tuple-element.40), channel_id=1, source_target_pairs={{0,16},{16,32},{32,48},{48,64},{64,80},{80,96},{96,112},{112,128},... | collective-permute-start | bytes 294920 | tf_op jit(solution)/shard_map/ppermute | solution.py:287
  75.0 1.9 %collective-permute-start.5 = (bf16[384,128]{1,0:T(8,128)(2,1)S(1)}, bf16[384,128]{1,0:T(8,128)(2,1)S(1)}, u32[]{:S(2)}, u32[]{:S(2)}) collective-permute-start(bf16[384,128]{1,0:T(8,128)(2,1)S(1)} %get-tuple-element.41), channel_id=1, source_target_pairs={{16,0},{32,16},{48,32},{64,48},{80,64},{96,80},{112,96},{128,112},... | collective-permute-start | bytes 294920 | tf_op jit(solution)/shard_map/ppermute | solution.py:287
  76.9 4.0 %collective-permute-done.5.down_ref = bf16[384,128]{1,0:T(8,128)(2,1)S(1)} collective-permute-done((bf16[384,128]{1,0:T(8,128)(2,1)S(1)}, bf16[384,128]{1,0:T(8,128)(2,1)S(1)}, u32[]{:S(2)}, u32[]{:S(2)}) %collective-permute-start.5) | collective-permute-done | bytes 98336 | tf_op jit(solution)/shard_map/ppermute | solution.py:287
  81.1 3.3 %collective-permute-start.6 = (bf16[384,128]{1,0:T(8,128)(2,1)S(1)}, bf16[384,128]{1,0:T(8,128)(2,1)S(1)}, u32[]{:S(2)}, u32[]{:S(2)}) collective-permute-start(bf16[384,128]{1,0:T(8,128)(2,1)S(1)} %get-tuple-element.43), channel_id=1, source_target_pairs={{0,1},{1,2},{2,3},{3,4},{4,5},{5,6},{6,7},{7,8},{8,9},{9,10},{10,1... | collective-permute-start | bytes 294920 | tf_op jit(solution)/shard_map/ppermute | solution.py:287
  84.4 2.0 %collective-permute-start.7 = (bf16[384,128]{1,0:T(8,128)(2,1)S(1)}, bf16[384,128]{1,0:T(8,128)(2,1)S(1)}, u32[]{:S(2)}, u32[]{:S(2)}) collective-permute-start(bf16[384,128]{1,0:T(8,128)(2,1)S(1)} %get-tuple-element.44), channel_id=1, source_target_pairs={{1,0},{2,1},{3,2},{4,3},{5,4},{6,5},{7,6},{8,7},{9,8},{10,9},{11,1... | collective-permute-start | bytes 294920 | tf_op jit(solution)/shard_map/ppermute | solution.py:287
  86.4 5.4 %collective-permute-done.7.right_ref = bf16[384,128]{1,0:T(8,128)(2,1)S(1)} collective-permute-done((bf16[384,128]{1,0:T(8,128)(2,1)S(1)}, bf16[384,128]{1,0:T(8,128)(2,1)S(1)}, u32[]{:S(2)}, u32[]{:S(2)}) %collective-permute-start.7) | collective-permute-done | bytes 98336 | tf_op jit(solution)/shard_map/ppermute | solution.py:287
  92.5 17.1 %all_to_all.26.column_ref = f32[16,8,128]{2,1,0:T(8,128)S(1)} all-to-all(f32[16,8,128]{2,1,0:T(8,128)S(1)} %get-tuple-element.48), channel_id=1, replica_groups=mesh['z'=16,'core'=2,'gy'=16] {'z'}, dimensions={0} | all-to-all | bytes 131072 | tf_op jit(solution)/shard_map/all_to_all | solution.py:332
  110.4 6.5 %all-to-all-start.4 = ((f32[32,8,128]{2,1,0:T(8,128)}), f32[32,8,128]{2,1,0:T(8,128)S(1)}, u32[]{:S(2)}, u32[]{:S(2)}) async-start(f32[32,8,128]{2,1,0:T(8,128)} %shard_map.95), calls=%async_computation.4 | async-start | bytes 262144 | tf_op jit(solution)/shard_map/all_to_all | solution.py:336
  116.9 2.2 %shard_map.94.local_ref = f32[1024,128]{1,0:T(8,128)S(1)} custom-call(bf16[1024,1024]{1,0:T(8,128)(2,1)} %bitcast.8, bf16[1024,128]{1,0:T(8,128)(2,1)S(1)} %get-tuple-element.47.sub_ref), custom_call_target="tpu_custom_call" | custom-call | flops 268435456 | bytes 2097152 | tf_op jit(solution)/shard_map/pallas_call | solution.py:45
  119.1 3.6 %all-to-all-done.4.parts_ref = f32[32,8,128]{2,1,0:T(8,128)S(1)} async-done(((f32[32,8,128]{2,1,0:T(8,128)}), f32[32,8,128]{2,1,0:T(8,128)S(1)}, u32[]{:S(2)}, u32[]{:S(2)}) %all-to-all-start.4) | async-done | bytes 131104 | tf_op jit(solution)/shard_map/all_to_all | solution.py:336
  123.2 3.9 %collective-permute-start.8 = (bf16[240,128]{1,0:T(8,128)(2,1)S(1)}, bf16[240,128]{1,0:T(8,128)(2,1)S(1)}, u32[]{:S(2)}, u32[]{:S(2)}) collective-permute-start(bf16[240,128]{1,0:T(8,128)(2,1)S(1)} %get-tuple-element.50), channel_id=1, source_target_pairs={{0,16},{16,32},{32,48},{48,64},{64,80},{80,96},{96,112},{112,128},... | collective-permute-start | bytes 184328 | tf_op jit(solution)/shard_map/ppermute | solution.py:287
  127.1 1.9 %collective-permute-start.9 = (bf16[240,128]{1,0:T(8,128)(2,1)S(1)}, bf16[240,128]{1,0:T(8,128)(2,1)S(1)}, u32[]{:S(2)}, u32[]{:S(2)}) collective-permute-start(bf16[240,128]{1,0:T(8,128)(2,1)S(1)} %get-tuple-element.51), channel_id=1, source_target_pairs={{16,0},{32,16},{48,32},{64,48},{80,64},{96,80},{112,96},{128,112},... | collective-permute-start | bytes 184328 | tf_op jit(solution)/shard_map/ppermute | solution.py:287
  129.1 3.6 %collective-permute-done.9.down_ref = bf16[240,128]{1,0:T(8,128)(2,1)S(1)} collective-permute-done((bf16[240,128]{1,0:T(8,128)(2,1)S(1)}, bf16[240,128]{1,0:T(8,128)(2,1)S(1)}, u32[]{:S(2)}, u32[]{:S(2)}) %collective-permute-start.9) | collective-permute-done | bytes 61472 | tf_op jit(solution)/shard_map/ppermute | solution.py:287
  132.8 3.3 %collective-permute-start.10 = (bf16[240,128]{1,0:T(8,128)(2,1)S(1)}, bf16[240,128]{1,0:T(8,128)(2,1)S(1)}, u32[]{:S(2)}, u32[]{:S(2)}) collective-permute-start(bf16[240,128]{1,0:T(8,128)(2,1)S(1)} %get-tuple-element.53), channel_id=1, source_target_pairs={{0,1},{1,2},{2,3},{3,4},{4,5},{5,6},{6,7},{7,8},{8,9},{9,10},{10,1... | collective-permute-start | bytes 184328 | tf_op jit(solution)/shard_map/ppermute | solution.py:287
  136.1 2.0 %collective-permute-start.11 = (bf16[240,128]{1,0:T(8,128)(2,1)S(1)}, bf16[240,128]{1,0:T(8,128)(2,1)S(1)}, u32[]{:S(2)}, u32[]{:S(2)}) collective-permute-start(bf16[240,128]{1,0:T(8,128)(2,1)S(1)} %get-tuple-element.54), channel_id=1, source_target_pairs={{1,0},{2,1},{3,2},{4,3},{5,4},{6,5},{7,6},{8,7},{9,8},{10,9},{11,1... | collective-permute-start | bytes 184328 | tf_op jit(solution)/shard_map/ppermute | solution.py:287
  138.1 5.1 %collective-permute-done.11.right_ref = bf16[240,128]{1,0:T(8,128)(2,1)S(1)} collective-permute-done((bf16[240,128]{1,0:T(8,128)(2,1)S(1)}, bf16[240,128]{1,0:T(8,128)(2,1)S(1)}, u32[]{:S(2)}, u32[]{:S(2)}) %collective-permute-start.11) | collective-permute-done | bytes 61472 | tf_op jit(solution)/shard_map/ppermute | solution.py:287
  143.2 1.1 shard_map.98
  (13 shorter events, 2.7 us)
Async XLA Ops:
  5.0 24.5 %all-to-all-start = ((f32[32,8,128]{2,1,0:T(8,128)}), f32[32,8,128]{2,1,0:T(8,128)S(1)}, u32[]{:S(2)}, u32[]{:S(2)}) async-start(f32[32,8,128]{2,1,0:T(8,128)} %shard_map.89), calls=%async_computation | async-start | bytes 262144 | tf_op jit(solution)/shard_map/all_to_all | solution.py:311
  14.8 10.2 %collective-permute-start = (f32[136,128]{1,0:T(8,128)S(1)}, f32[136,128]{1,0:T(8,128)S(1)}, u32[]{:S(2)}, u32[]{:S(2)}) collective-permute-start(f32[136,128]{1,0:T(8,128)S(1)} %get-tuple-element.30), channel_id=1, source_target_pairs={{0,16},{16,32},{32,48},{48,64},{64,80},{80,96},{96,112},{112,128},... | collective-permute-start | bytes 208904 | tf_op jit(solution)/shard_map/ppermute | solution.py:287
  16.7 8.3 %collective-permute-start.2 = (f32[136,128]{1,0:T(8,128)S(1)}, f32[136,128]{1,0:T(8,128)S(1)}, u32[]{:S(2)}, u32[]{:S(2)}) collective-permute-start(f32[136,128]{1,0:T(8,128)S(1)} %get-tuple-element.32), channel_id=1, source_target_pairs={{0,1},{1,2},{2,3},{3,4},{4,5},{5,6},{6,7},{7,8},{8,9},{9,10},{10,1... | collective-permute-start | bytes 208904 | tf_op jit(solution)/shard_map/ppermute | solution.py:287
  19.8 7.2 %collective-permute-start.3 = (f32[136,128]{1,0:T(8,128)S(1)}, f32[136,128]{1,0:T(8,128)S(1)}, u32[]{:S(2)}, u32[]{:S(2)}) collective-permute-start(f32[136,128]{1,0:T(8,128)S(1)} %get-tuple-element.33), channel_id=1, source_target_pairs={{1,0},{2,1},{3,2},{4,3},{5,4},{6,5},{7,6},{8,7},{9,8},{10,9},{11,1... | collective-permute-start | bytes 208904 | tf_op jit(solution)/shard_map/ppermute | solution.py:287
  22.0 5.9 %collective-permute-start.1 = (f32[136,128]{1,0:T(8,128)S(1)}, f32[136,128]{1,0:T(8,128)S(1)}, u32[]{:S(2)}, u32[]{:S(2)}) collective-permute-start(f32[136,128]{1,0:T(8,128)S(1)} %get-tuple-element.31.after_ref), channel_id=1, source_target_pairs={{16,0},{32,16},{48,32},{64,48},{80,64},{96,80},{112,96},{128,112},... | collective-permute-start | bytes 208904 | tf_op jit(solution)/shard_map/ppermute | solution.py:287
  56.2 14.5 %all-to-all-start.2 = ((f32[32,8,128]{2,1,0:T(8,128)}), f32[32,8,128]{2,1,0:T(8,128)S(1)}, u32[]{:S(2)}, u32[]{:S(2)}) async-start(f32[32,8,128]{2,1,0:T(8,128)} %shard_map.90), calls=%async_computation.2 | async-start | bytes 262144 | tf_op jit(solution)/shard_map/all_to_all | solution.py:336
  71.2 5.8 %collective-permute-start.4 = (bf16[384,128]{1,0:T(8,128)(2,1)S(1)}, bf16[384,128]{1,0:T(8,128)(2,1)S(1)}, u32[]{:S(2)}, u32[]{:S(2)}) collective-permute-start(bf16[384,128]{1,0:T(8,128)(2,1)S(1)} %get-tuple-element.40), channel_id=1, source_target_pairs={{0,16},{16,32},{32,48},{48,64},{64,80},{80,96},{96,112},{112,128},... | collective-permute-start | bytes 294920 | tf_op jit(solution)/shard_map/ppermute | solution.py:287
  75.0 5.9 %collective-permute-start.5 = (bf16[384,128]{1,0:T(8,128)(2,1)S(1)}, bf16[384,128]{1,0:T(8,128)(2,1)S(1)}, u32[]{:S(2)}, u32[]{:S(2)}) collective-permute-start(bf16[384,128]{1,0:T(8,128)(2,1)S(1)} %get-tuple-element.41), channel_id=1, source_target_pairs={{16,0},{32,16},{48,32},{64,48},{80,64},{96,80},{112,96},{128,112},... | collective-permute-start | bytes 294920 | tf_op jit(solution)/shard_map/ppermute | solution.py:287
  81.1 5.4 %collective-permute-start.6 = (bf16[384,128]{1,0:T(8,128)(2,1)S(1)}, bf16[384,128]{1,0:T(8,128)(2,1)S(1)}, u32[]{:S(2)}, u32[]{:S(2)}) collective-permute-start(bf16[384,128]{1,0:T(8,128)(2,1)S(1)} %get-tuple-element.43), channel_id=1, source_target_pairs={{0,1},{1,2},{2,3},{3,4},{4,5},{5,6},{6,7},{7,8},{8,9},{9,10},{10,1... | collective-permute-start | bytes 294920 | tf_op jit(solution)/shard_map/ppermute | solution.py:287
  84.4 7.5 %collective-permute-start.7 = (bf16[384,128]{1,0:T(8,128)(2,1)S(1)}, bf16[384,128]{1,0:T(8,128)(2,1)S(1)}, u32[]{:S(2)}, u32[]{:S(2)}) collective-permute-start(bf16[384,128]{1,0:T(8,128)(2,1)S(1)} %get-tuple-element.44), channel_id=1, source_target_pairs={{1,0},{2,1},{3,2},{4,3},{5,4},{6,5},{7,6},{8,7},{9,8},{10,9},{11,1... | collective-permute-start | bytes 294920 | tf_op jit(solution)/shard_map/ppermute | solution.py:287
  110.4 12.3 %all-to-all-start.4 = ((f32[32,8,128]{2,1,0:T(8,128)}), f32[32,8,128]{2,1,0:T(8,128)S(1)}, u32[]{:S(2)}, u32[]{:S(2)}) async-start(f32[32,8,128]{2,1,0:T(8,128)} %shard_map.95), calls=%async_computation.4 | async-start | bytes 262144 | tf_op jit(solution)/shard_map/all_to_all | solution.py:336
  123.2 5.9 %collective-permute-start.8 = (bf16[240,128]{1,0:T(8,128)(2,1)S(1)}, bf16[240,128]{1,0:T(8,128)(2,1)S(1)}, u32[]{:S(2)}, u32[]{:S(2)}) collective-permute-start(bf16[240,128]{1,0:T(8,128)(2,1)S(1)} %get-tuple-element.50), channel_id=1, source_target_pairs={{0,16},{16,32},{32,48},{48,64},{64,80},{80,96},{96,112},{112,128},... | collective-permute-start | bytes 184328 | tf_op jit(solution)/shard_map/ppermute | solution.py:287
  127.1 5.5 %collective-permute-start.9 = (bf16[240,128]{1,0:T(8,128)(2,1)S(1)}, bf16[240,128]{1,0:T(8,128)(2,1)S(1)}, u32[]{:S(2)}, u32[]{:S(2)}) collective-permute-start(bf16[240,128]{1,0:T(8,128)(2,1)S(1)} %get-tuple-element.51), channel_id=1, source_target_pairs={{16,0},{32,16},{48,32},{64,48},{80,64},{96,80},{112,96},{128,112},... | collective-permute-start | bytes 184328 | tf_op jit(solution)/shard_map/ppermute | solution.py:287
  132.8 5.3 %collective-permute-start.10 = (bf16[240,128]{1,0:T(8,128)(2,1)S(1)}, bf16[240,128]{1,0:T(8,128)(2,1)S(1)}, u32[]{:S(2)}, u32[]{:S(2)}) collective-permute-start(bf16[240,128]{1,0:T(8,128)(2,1)S(1)} %get-tuple-element.53), channel_id=1, source_target_pairs={{0,1},{1,2},{2,3},{3,4},{4,5},{5,6},{6,7},{7,8},{8,9},{9,10},{10,1... | collective-permute-start | bytes 184328 | tf_op jit(solution)/shard_map/ppermute | solution.py:287
  136.1 7.1 %collective-permute-start.11 = (bf16[240,128]{1,0:T(8,128)(2,1)S(1)}, bf16[240,128]{1,0:T(8,128)(2,1)S(1)}, u32[]{:S(2)}, u32[]{:S(2)}) collective-permute-start(bf16[240,128]{1,0:T(8,128)(2,1)S(1)} %get-tuple-element.54), channel_id=1, source_target_pairs={{1,0},{2,1},{3,2},{4,3},{5,4},{6,5},{7,6},{8,7},{9,8},{10,9},{11,1... | collective-permute-start | bytes 184328 | tf_op jit(solution)/shard_map/ppermute | solution.py:287

commit v4 on v3

--- a/solution.py
+++ b/solution.py
@@ -61,9 +61,9 @@
         copy.wait()
 
 
-def order_rows(rows_hbm, places_hbm, after_ref, out_ref, rows, places, tiles, sems):
-    fetch([(rows_hbm, rows), (places_hbm, places)], sems)
-    n_targets, width = out_ref.shape[0], out_ref.shape[2]
+def order_rows(width, rows_hbm, places_hbm, basis_hbm, after_ref, out_ref, basis_ref, rows, places, tiles, sems):
+    fetch([(rows_hbm, rows), (places_hbm, places), (basis_hbm, basis_ref)], sems)
+    n_targets = out_ref.shape[0]
     for t in range(tiles.shape[0]):
         tiles[t] = rows[:, t * LANES : (t + 1) * LANES].astype(F32)
     slot = lax.broadcasted_iota(jnp.int32, (8, LANES), 1) // 8
@@ -75,14 +75,14 @@
             tile = tiles[lax.shift_right_logical(place, 4)]
             turned = pltpu.roll(tile, ((q + 16 - (place & 15)) & 15) * 8, 1)
             block = jnp.where(slot == q, turned, block)
-        out_ref[target] = block[:, :width]
+        out_ref[target] = block
         return carry
 
     lax.fori_loop(0, n_targets, one, 0, unroll=8)
 
 
 def make_edges(
-    values_hbm, stiff_hbm, lists_hbm, up_ref, down_ref, left_ref, right_ref, values_ref, stiff_ref, lists_ref, sems
+    values_hbm, stiff_hbm, lists_hbm, values_ref, stiff_ref, up_ref, down_ref, left_ref, right_ref, lists_ref, sems
 ):
     fetch([(values_hbm, values_ref), (stiff_hbm, stiff_ref), (lists_hbm, lists_ref)], sems)
     lists = lists_ref[...]
@@ -112,20 +112,16 @@
         ref[pl.ds(STRIP + 2 * CELLS, 8), 0:MARGIN] = jnp.broadcast_to(code, (8, MARGIN))
 
 
-def restrict(strips, beside, across_ref, along_ref, basis_ref, sub_ref, coarse_ref):
+def restrict(strips, beside, across_ref, along_ref, basis_ref, sub_ref):
     sub_ref[OWN : OWN + 2 * MARGIN] = matmul(across_ref[...], strips.astype(BF16), (0, 0)).astype(BF16)
     sub_ref[OWN + 2 * MARGIN :] = matmul(along_ref[...], beside.astype(BF16), (0, 0)).astype(BF16)
-    coarse = matmul(basis_ref[...], sub_ref[...]).astype(BF16).astype(F32)
-    for a in range(coarse_ref.shape[0]):
-        coarse_ref[a] = coarse
+    return matmul(basis_ref[...], sub_ref[...]).astype(BF16).astype(F32)
 
 
 def start_pass(
-    values_hbm, stiff_hbm, basis_hbm, up_ref, down_ref, left_ref, right_ref,
-    field_ref, diagonal_ref, across_ref, along_ref, sub_ref, basis_ref, coarse_ref,
-    values_ref, stiff_ref, sems,
+    values_ref, stiff_ref, basis_ref, ordered_ref, up_ref, down_ref, left_ref, right_ref,
+    field_ref, diagonal_ref, across_ref, along_ref, sub_ref, both_ref,
 ):
-    fetch([(values_hbm, values_ref), (stiff_hbm, stiff_ref), (basis_hbm, basis_ref)], sems)
     turned = stiff_ref[...].T
     field_ref[...] = jnp.zeros_like(field_ref)
     diagonal_ref[...] = jnp.full(diagonal_ref.shape, 4.0, F32)
@@ -169,13 +165,23 @@
     beside = jnp.concatenate(
         [field_ref[pl.ds(at(c, i, CELLS), 8), :] for c in range(COMPONENTS) for i in range(CELLS)], axis=0
     )
-    restrict(strips, beside, across_ref, along_ref, basis_ref, sub_ref, coarse_ref)
-
-
-def cross_multiply(rows_ref, column_ref, parts_ref):
-    n_gy, k, width = rows_ref.shape
-    rows = rows_ref[...].reshape(n_gy * k, width).astype(BF16)
-    parts_ref[...] = matmul(rows, column_ref[...].reshape(width, LANES).astype(BF16)).reshape(parts_ref.shape)
+    coarse = restrict(strips, beside, across_ref, along_ref, basis_ref, sub_ref)
+    for target in range(both_ref.shape[0]):
+        both_ref[target] = jnp.concatenate([ordered_ref[target], coarse], axis=0).astype(BF16)
+
+
+def cross_first(both_ref, rows_ref, parts_ref):
+    n, k = both_ref.shape[0], both_ref.shape[1] // 2
+    both = both_ref[...].astype(F32)
+    rows_ref[...] = both[:, :k].reshape(n * k, LANES).astype(BF16)
+    parts = matmul(rows_ref[...], both[:, k:].reshape(n * k, LANES).astype(BF16), (0, 0))
+    parts_ref[...] = parts[: parts_ref.shape[0] * k].reshape(parts_ref.shape)
+
+
+def cross_second(rows_ref, column_ref, parts_ref):
+    n, k = column_ref.shape[:2]
+    parts = matmul(rows_ref[...], column_ref[...].reshape(n * k, LANES).astype(BF16), (0, 0))
+    parts_ref[...] = parts[: parts_ref.shape[0] * k].reshape(parts_ref.shape)
 
 
 def apply_inverse(inverse_hbm, sub_ref, patch_ref, inverse, sems):
@@ -261,7 +267,9 @@
             else:
                 n = (c * 2 + (i + 2 if i < 0 else i - CELLS)) * CELLS + (0 if i < 0 else STRIP)
                 strips[pl.ds(n, CELLS), :] = middle[:CELLS]
-    restrict(strips[...], beside[...], across_ref, along_ref, basis_ref, sub_ref, coarse_ref)
+    coarse = restrict(strips[...], beside[...], across_ref, along_ref, basis_ref, sub_ref)
+    for target in range(coarse_ref.shape[0]):
+        coarse_ref[target] = coarse
 
 
 def last_pass(field_ref, left_ref, right_ref, first_ref, values_ref, diagonal_ref, solution_ref, final_ref, total):
@@ -288,7 +296,7 @@
 
 
 GX, GY = ("z", "core"), "gy"
-FIRST, SECOND = "z", ("core", "gy")
+FIRST, SECOND = ("core", "gy"), "z"
 
 
 def per_device(residual, stiffness, local_inverse, coarse_basis, coarse_rows, send_rows, partition_map):
@@ -298,39 +306,35 @@
     values = residual.reshape(OWN, LANES)
     swap = functools.partial(lax.all_to_all, split_axis=0, concat_axis=0, tiled=True)
 
-    own, stiff = ((OWN, LANES), F32), (stiffness.shape, F32)
-    edge = ((EDGE, LANES), F32)
-    up, down, left, right = call(
-        make_edges, [edge] * 4, values, stiffness, lists, fetched=3,
-        scratch=[own, stiff, (lists.shape, jnp.int32)],
-    )
-    [crossing] = call(
-        order_rows, [((n_second, k, n_first * k), F32)], coarse_rows[0, 0], partition_map, up, fetched=2,
+    own, field, edge = ((OWN, LANES), F32), ((FIELD, LANES), F32), ((EDGE, LANES), F32)
+    sub_kind, patch = ((OWN + 4 * MARGIN, LANES), BF16), ((OWN + 4 * MARGIN, LANES), F32)
+    copies, sums = ((n_first, k, LANES), F32), ((n_second, k, LANES), F32)
+    values, stiffness, up, down, left, right = call(
+        make_edges, [own, (stiffness.shape, F32), *[edge] * 4], values, stiffness, lists, fetched=3,
+        scratch=[(lists.shape, jnp.int32)],
+    )
+    ordered, basis = call(
+        functools.partial(order_rows, n_second * k), [copies, (basis.shape, BF16)],
+        coarse_rows[0, 0], partition_map, basis, up, fetched=3,
         scratch=[((k, order), BF16), pltpu.SMEM(partition_map.shape, jnp.int32), ((order // LANES, k, LANES), F32)],
     )
-    crossing = swap(crossing, SECOND)
     up, down = trade(up, down, GX)
     left, right = trade(left, right, GY)
-    field = ((FIELD, LANES), F32)
-    copies = ((n_first, k, LANES), F32)
-    sub_kind = ((OWN + 4 * MARGIN, LANES), BF16)
-    ambient, diagonal, across, along, sub, basis, coarse = call(
+    ambient, diagonal, across, along, sub, both = call(
         start_pass,
         [
             field, ((PLANE, LANES), F32), ((2 * STRIP, 2 * MARGIN), BF16), ((BESIDE, 2 * MARGIN), BF16), sub_kind,
-            (basis.shape, BF16), copies,
+            ((n_first, 2 * k, LANES), BF16),
         ],
-        values, stiffness, basis, up, down, left, right, fetched=3, scratch=[own, stiff],
-    )
-
-    def correct(depth, sub, coarse):
-        patch = ((OWN + 4 * MARGIN, LANES), F32)
+        values, stiffness, basis, ordered, up, down, left, right,
+    )
+
+    def correct(depth, sub, parts):
+        part = ((COMPONENTS * part_of(depth), LANES), BF16)
         [local] = call(
             apply_inverse, [patch], inverse, sub, fetched=1, copies=4, scratch=[(inverse.shape, BF16)],
             cost=(inverse.size * LANES * 2, inverse.size * 2),
         )
-        [parts] = call(cross_multiply, [((n_second, k, LANES), F32)], crossing, swap(coarse, FIRST))
-        part = ((COMPONENTS * part_of(depth), LANES), BF16)
         y, to_up, to_down = call(
             functools.partial(spread, depth), [field, part, part],
             local, basis, swap(parts, SECOND), across, along, scratch=[patch],
@@ -341,12 +345,14 @@
         )
         return (y, *trade(to_left, to_right, GY))
 
+    crossing, parts = call(cross_first, [((n_first * k, LANES), BF16), sums], swap(both, FIRST))
     first, sub, coarse = call(
-        middle_pass, [field, sub_kind, copies], *correct(3, sub, coarse), ambient, diagonal, across, along, basis,
+        middle_pass, [field, sub_kind, copies], *correct(3, sub, parts), ambient, diagonal, across, along, basis,
         scratch=[((2 * STRIP, LANES), F32), ((BESIDE, LANES), F32)],
     )
+    [parts] = call(cross_second, [sums], crossing, swap(coarse, FIRST))
     total, final = call(
-        last_pass, [own, own], *correct(1, sub, coarse), first, ambient, diagonal, scratch=[field]
+        last_pass, [own, own], *correct(1, sub, parts), first, ambient, diagonal, scratch=[field]
     )
     return total.reshape(residual.shape), final.reshape(residual.shape)
 

time: 145 us -> 133 us (0.917)
  blocking collectives: 43 us -> 24.6 us
  waiting for transfers between devices: 28.3 us -> 38.2 us
  starting transfers between devices: 57.3 us -> 55.6 us
  Pallas kernels: 14.9 us -> 13.3 us
    all_to_all x2, blocking collectives: 43 us -> 24.6 us  [the longest x1 13 us: per_device(): swap(both, FIRST)]
    all_to_all x2, waiting for transfers between devices: 7.2 us -> 18.7 us  [correct(): swap(parts, SECOND)]
    all_to_all x1 -> x0, starting transfers between devices: 9.78 us -> none  [per_device(): crossing = swap(crossing, SECOND)]
    all_to_all x2, starting transfers between devices: 15.1 us -> 20.4 us  [correct(): swap(parts, SECOND)]
    ppermute x6, starting transfers between devices: 19.4 us -> 23.5 us  [trade(): lax.ppermute(upper, axis, forward)]
    ppermute x6, waiting for transfers between devices: 21.1 us -> 19.4 us  [trade(): lax.ppermute(lower, axis, backward)]
    pallas_call x13, Pallas kernels: 14.9 us -> 13.3 us  [call(): pl.pallas_call(kernel, out_shape=[jax.ShapeDtypeStruct(shape, kind) for s...]
  transfers between devices with their start and end apart: 15 -> 14, of which waited for: 9 -> 8; matrix products, arithmetic and copies ran while one was open for 0% -> 0% of each run, Pallas kernels for 4% -> 5%
where the time goes in v4:
time: 133 us; the launch traced here: 132 us
  starting transfers between devices  55.6 us (42%)
  waiting for transfers between devices  38.2 us (29%)
  blocking collectives  24.6 us (18%)
  Pallas kernels  13.3 us (10%)
    ppermute x6, starting transfers between devices, trade(): lax.ppermute(upper, axis, forward)  23.5 us
    all_to_all x2, starting transfers between devices, correct(): swap(parts, SECOND)  20.4 us
    ppermute x6, waiting for transfers between devices, trade(): lax.ppermute(lower, axis, backward)  19.4 us
    all_to_all x2, waiting for transfers between devices, correct(): swap(parts, SECOND)  18.7 us
    pallas_call x13, Pallas kernels, call(): pl.pallas_call(kernel, out_shape=[jax.ShapeDtypeStruct(shape, kind) for s...  13.3 us
    all_to_all x1, blocking collectives, per_device(): swap(both, FIRST)  13 us
    ppermute x6, starting transfers between devices, trade(): lax.ppermute(lower, axis, backward)  11.8 us
    all_to_all x1, blocking collectives, per_device(): [parts] = call(cross_second, [sums], crossing, swap(coarse, FIRST))  11.6 us
  transfers between devices with their start and end apart: 14, of which 8 were waited for; matrix products, arithmetic and copies ran while one was open for 0% of the time, Pallas kernels for 5%

profile of v4, /device:TPU:7, one launch (start us, length us, event | category | flops | bytes accessed | tf_op | source)
XLA Modules:
  0.0 132.5 jit_solution(1452014631176586476)
XLA Ops:
  0.6 1.2 shard_map.86
  1.8 4.1 %collective-permute-start = (f32[136,128]{1,0:T(8,128)S(1)}, f32[136,128]{1,0:T(8,128)S(1)}, u32[]{:S(2)}, u32[]{:S(2)}) collective-permute-start(f32[136,128]{1,0:T(8,128)S(1)} %get-tuple-element.40), channel_id=1, source_target_pairs={{0,16},{16,32},{32,48},{48,64},{64,80},{80,96},{96,112},{112,128},... | collective-permute-start | bytes 208904 | tf_op jit(solution)/shard_map/ppermute | solution.py:295
  5.9 3.1 %collective-permute-start.2 = (f32[136,128]{1,0:T(8,128)S(1)}, f32[136,128]{1,0:T(8,128)S(1)}, u32[]{:S(2)}, u32[]{:S(2)}) collective-permute-start(f32[136,128]{1,0:T(8,128)S(1)} %get-tuple-element.41), channel_id=1, source_target_pairs={{0,1},{1,2},{2,3},{3,4},{4,5},{5,6},{6,7},{7,8},{8,9},{9,10},{10,1... | collective-permute-start | bytes 208904 | tf_op jit(solution)/shard_map/ppermute | solution.py:295
  9.1 2.2 %collective-permute-start.3 = (f32[136,128]{1,0:T(8,128)S(1)}, f32[136,128]{1,0:T(8,128)S(1)}, u32[]{:S(2)}, u32[]{:S(2)}) collective-permute-start(f32[136,128]{1,0:T(8,128)S(1)} %get-tuple-element.42), channel_id=1, source_target_pairs={{1,0},{2,1},{3,2},{4,3},{5,4},{6,5},{7,6},{8,7},{9,8},{10,9},{11,1... | collective-permute-start | bytes 208904 | tf_op jit(solution)/shard_map/ppermute | solution.py:295
  11.2 1.9 %collective-permute-start.1 = (f32[136,128]{1,0:T(8,128)S(1)}, f32[136,128]{1,0:T(8,128)S(1)}, u32[]{:S(2)}, u32[]{:S(2)}) collective-permute-start(f32[136,128]{1,0:T(8,128)S(1)} %get-tuple-element.37.after_ref), channel_id=1, source_target_pairs={{16,0},{32,16},{48,32},{64,48},{80,64},{96,80},{112,96},{128,112},... | collective-permute-start | bytes 208904 | tf_op jit(solution)/shard_map/ppermute | solution.py:295
  13.2 2.5 %shard_map.87 = (f32[32,8,128]{2,1,0:T(8,128)S(1)}, bf16[8,1024]{1,0:T(8,128)(2,1)S(1)}) custom-call(bf16[8,4096]{1,0:T(8,128)(2,1)} %bitcast.10, s32[512]{0:T(512)} %places_hbm.1, bf16[8,1024]{1,0:T(8,128)(2,1)} %bitcast.11, f32[136,128]{1,0:T(8,128)S(1)} %get-tuple-element.37.after_ref), custom_call_target="tpu_custom_call" | custom-call | tf_op jit(solution)/shard_map/pallas_call | solution.py:45
  15.7 0.5 collective-permute-done.3.right_ref
  16.2 0.6 collective-permute-done.1.down_ref
  17.4 13.0 %all_to_all.20.both_ref = bf16[32,16,128]{2,1,0:T(8,128)(2,1)S(1)} all-to-all(bf16[32,16,128]{2,1,0:T(8,128)(2,1)S(1)} %get-tuple-element.44), channel_id=1, replica_groups=mesh['z'=16,'core'=2,'gy'=16] {'core','gy'}, dimensions={0} | all-to-all | bytes 262144 | tf_op jit(solution)/shard_map/all_to_all | solution.py:348
  30.3 0.8 shard_map.90
  31.2 15.1 %all-to-all-start.1 = ((f32[16,8,128]{2,1,0:T(8,128)}), f32[16,8,128]{2,1,0:T(8,128)S(1)}, u32[]{:S(2)}, u32[]{:S(2)}) async-start(f32[16,8,128]{2,1,0:T(8,128)} %get-tuple-element.45), calls=%async_computation.1 | async-start | bytes 131072 | tf_op jit(solution)/shard_map/all_to_all | solution.py:340
  46.3 2.2 %shard_map.89.local_ref = f32[1024,128]{1,0:T(8,128)S(1)} custom-call(bf16[1024,1024]{1,0:T(8,128)(2,1)} %bitcast.7, bf16[1024,128]{1,0:T(8,128)(2,1)S(1)} %get-tuple-element.43.sub_ref), custom_call_target="tpu_custom_call" | custom-call | flops 268435456 | bytes 2097152 | tf_op jit(solution)/shard_map/pallas_call | solution.py:45
  48.5 9.4 %all-to-all-done.1.parts_ref = f32[16,8,128]{2,1,0:T(8,128)S(1)} async-done(((f32[16,8,128]{2,1,0:T(8,128)}), f32[16,8,128]{2,1,0:T(8,128)S(1)}, u32[]{:S(2)}, u32[]{:S(2)}) %all-to-all-start.1) | async-done | bytes 65568 | tf_op jit(solution)/shard_map/all_to_all | solution.py:340
  58.3 4.6 %collective-permute-start.4 = (bf16[384,128]{1,0:T(8,128)(2,1)S(1)}, bf16[384,128]{1,0:T(8,128)(2,1)S(1)}, u32[]{:S(2)}, u32[]{:S(2)}) collective-permute-start(bf16[384,128]{1,0:T(8,128)(2,1)S(1)} %get-tuple-element.49), channel_id=1, source_target_pairs={{0,16},{16,32},{32,48},{48,64},{64,80},{80,96},{96,112},{112,128},... | collective-permute-start | bytes 294920 | tf_op jit(solution)/shard_map/ppermute | solution.py:295
  62.9 1.9 %collective-permute-start.5 = (bf16[384,128]{1,0:T(8,128)(2,1)S(1)}, bf16[384,128]{1,0:T(8,128)(2,1)S(1)}, u32[]{:S(2)}, u32[]{:S(2)}) collective-permute-start(bf16[384,128]{1,0:T(8,128)(2,1)S(1)} %get-tuple-element.50), channel_id=1, source_target_pairs={{16,0},{32,16},{48,32},{64,48},{80,64},{96,80},{112,96},{128,112},... | collective-permute-start | bytes 294920 | tf_op jit(solution)/shard_map/ppermute | solution.py:295
  64.9 4.0 %collective-permute-done.5.down_ref = bf16[384,128]{1,0:T(8,128)(2,1)S(1)} collective-permute-done((bf16[384,128]{1,0:T(8,128)(2,1)S(1)}, bf16[384,128]{1,0:T(8,128)(2,1)S(1)}, u32[]{:S(2)}, u32[]{:S(2)}) %collective-permute-start.5) | collective-permute-done | bytes 98336 | tf_op jit(solution)/shard_map/ppermute | solution.py:295
  69.0 3.5 %collective-permute-start.6 = (bf16[384,128]{1,0:T(8,128)(2,1)S(1)}, bf16[384,128]{1,0:T(8,128)(2,1)S(1)}, u32[]{:S(2)}, u32[]{:S(2)}) collective-permute-start(bf16[384,128]{1,0:T(8,128)(2,1)S(1)} %get-tuple-element.52), channel_id=1, source_target_pairs={{0,1},{1,2},{2,3},{3,4},{4,5},{5,6},{6,7},{7,8},{8,9},{9,10},{10,1... | collective-permute-start | bytes 294920 | tf_op jit(solution)/shard_map/ppermute | solution.py:295
  72.5 1.9 %collective-permute-start.7 = (bf16[384,128]{1,0:T(8,128)(2,1)S(1)}, bf16[384,128]{1,0:T(8,128)(2,1)S(1)}, u32[]{:S(2)}, u32[]{:S(2)}) collective-permute-start(bf16[384,128]{1,0:T(8,128)(2,1)S(1)} %get-tuple-element.53), channel_id=1, source_target_pairs={{1,0},{2,1},{3,2},{4,3},{5,4},{6,5},{7,6},{8,7},{9,8},{10,9},{11,1... | collective-permute-start | bytes 294920 | tf_op jit(solution)/shard_map/ppermute | solution.py:295
  74.5 5.5 %collective-permute-done.7.right_ref = bf16[384,128]{1,0:T(8,128)(2,1)S(1)} collective-permute-done((bf16[384,128]{1,0:T(8,128)(2,1)S(1)}, bf16[384,128]{1,0:T(8,128)(2,1)S(1)}, u32[]{:S(2)}, u32[]{:S(2)}) %collective-permute-start.7) | collective-permute-done | bytes 98336 | tf_op jit(solution)/shard_map/ppermute | solution.py:295
  80.0 0.6 shard_map.93
  80.7 11.6 %all_to_all.21.column_ref = f32[32,8,128]{2,1,0:T(8,128)S(1)} all-to-all(f32[32,8,128]{2,1,0:T(8,128)S(1)} %get-tuple-element.58), channel_id=1, replica_groups=mesh['z'=16,'core'=2,'gy'=16] {'core','gy'}, dimensions={0} | all-to-all | bytes 262144 | tf_op jit(solution)/shard_map/all_to_all | solution.py:353
  92.3 0.8 shard_map.95
  93.1 5.3 %all-to-all-start.3 = ((f32[16,8,128]{2,1,0:T(8,128)}), f32[16,8,128]{2,1,0:T(8,128)S(1)}, u32[]{:S(2)}, u32[]{:S(2)}) async-start(f32[16,8,128]{2,1,0:T(8,128)} %shard_map.95), calls=%async_computation.3 | async-start | bytes 131072 | tf_op jit(solution)/shard_map/all_to_all | solution.py:340
  98.4 2.2 %shard_map.94.local_ref = f32[1024,128]{1,0:T(8,128)S(1)} custom-call(bf16[1024,1024]{1,0:T(8,128)(2,1)} %bitcast.8, bf16[1024,128]{1,0:T(8,128)(2,1)S(1)} %get-tuple-element.56.sub_ref), custom_call_target="tpu_custom_call" | custom-call | flops 268435456 | bytes 2097152 | tf_op jit(solution)/shard_map/pallas_call | solution.py:45
  100.7 9.4 %all-to-all-done.3.parts_ref = f32[16,8,128]{2,1,0:T(8,128)S(1)} async-done(((f32[16,8,128]{2,1,0:T(8,128)}), f32[16,8,128]{2,1,0:T(8,128)S(1)}, u32[]{:S(2)}, u32[]{:S(2)}) %all-to-all-start.3) | async-done | bytes 65568 | tf_op jit(solution)/shard_map/all_to_all | solution.py:340
  110.5 4.6 %collective-permute-start.8 = (bf16[240,128]{1,0:T(8,128)(2,1)S(1)}, bf16[240,128]{1,0:T(8,128)(2,1)S(1)}, u32[]{:S(2)}, u32[]{:S(2)}) collective-permute-start(bf16[240,128]{1,0:T(8,128)(2,1)S(1)} %get-tuple-element.60), channel_id=1, source_target_pairs={{0,16},{16,32},{32,48},{48,64},{64,80},{80,96},{96,112},{112,128},... | collective-permute-start | bytes 184328 | tf_op jit(solution)/shard_map/ppermute | solution.py:295
  115.1 1.9 %collective-permute-start.9 = (bf16[240,128]{1,0:T(8,128)(2,1)S(1)}, bf16[240,128]{1,0:T(8,128)(2,1)S(1)}, u32[]{:S(2)}, u32[]{:S(2)}) collective-permute-start(bf16[240,128]{1,0:T(8,128)(2,1)S(1)} %get-tuple-element.61), channel_id=1, source_target_pairs={{16,0},{32,16},{48,32},{64,48},{80,64},{96,80},{112,96},{128,112},... | collective-permute-start | bytes 184328 | tf_op jit(solution)/shard_map/ppermute | solution.py:295
  117.0 3.6 %collective-permute-done.9.down_ref = bf16[240,128]{1,0:T(8,128)(2,1)S(1)} collective-permute-done((bf16[240,128]{1,0:T(8,128)(2,1)S(1)}, bf16[240,128]{1,0:T(8,128)(2,1)S(1)}, u32[]{:S(2)}, u32[]{:S(2)}) %collective-permute-start.9) | collective-permute-done | bytes 61472 | tf_op jit(solution)/shard_map/ppermute | solution.py:295
  120.7 3.5 %collective-permute-start.10 = (bf16[240,128]{1,0:T(8,128)(2,1)S(1)}, bf16[240,128]{1,0:T(8,128)(2,1)S(1)}, u32[]{:S(2)}, u32[]{:S(2)}) collective-permute-start(bf16[240,128]{1,0:T(8,128)(2,1)S(1)} %get-tuple-element.63), channel_id=1, source_target_pairs={{0,1},{1,2},{2,3},{3,4},{4,5},{5,6},{6,7},{7,8},{8,9},{9,10},{10,1... | collective-permute-start | bytes 184328 | tf_op jit(solution)/shard_map/ppermute | solution.py:295
  124.3 1.9 %collective-permute-start.11 = (bf16[240,128]{1,0:T(8,128)(2,1)S(1)}, bf16[240,128]{1,0:T(8,128)(2,1)S(1)}, u32[]{:S(2)}, u32[]{:S(2)}) collective-permute-start(bf16[240,128]{1,0:T(8,128)(2,1)S(1)} %get-tuple-element.64), channel_id=1, source_target_pairs={{1,0},{2,1},{3,2},{4,3},{5,4},{6,5},{7,6},{8,7},{9,8},{10,9},{11,1... | collective-permute-start | bytes 184328 | tf_op jit(solution)/shard_map/ppermute | solution.py:295
  126.2 5.1 %collective-permute-done.11.right_ref = bf16[240,128]{1,0:T(8,128)(2,1)S(1)} collective-permute-done((bf16[240,128]{1,0:T(8,128)(2,1)S(1)}, bf16[240,128]{1,0:T(8,128)(2,1)S(1)}, u32[]{:S(2)}, u32[]{:S(2)}) %collective-permute-start.11) | collective-permute-done | bytes 61472 | tf_op jit(solution)/shard_map/ppermute | solution.py:295
  131.3 1.1 shard_map.98
  (11 shorter events, 1.7 us)
Async XLA Ops:
  1.8 13.8 %collective-permute-start = (f32[136,128]{1,0:T(8,128)S(1)}, f32[136,128]{1,0:T(8,128)S(1)}, u32[]{:S(2)}, u32[]{:S(2)}) collective-permute-start(f32[136,128]{1,0:T(8,128)S(1)} %get-tuple-element.40), channel_id=1, source_target_pairs={{0,16},{16,32},{32,48},{48,64},{64,80},{80,96},{96,112},{112,128},... | collective-permute-start | bytes 208904 | tf_op jit(solution)/shard_map/ppermute | solution.py:295
  5.9 9.7 %collective-permute-start.2 = (f32[136,128]{1,0:T(8,128)S(1)}, f32[136,128]{1,0:T(8,128)S(1)}, u32[]{:S(2)}, u32[]{:S(2)}) collective-permute-start(f32[136,128]{1,0:T(8,128)S(1)} %get-tuple-element.41), channel_id=1, source_target_pairs={{0,1},{1,2},{2,3},{3,4},{4,5},{5,6},{6,7},{7,8},{8,9},{9,10},{10,1... | collective-permute-start | bytes 208904 | tf_op jit(solution)/shard_map/ppermute | solution.py:295
  9.1 7.2 %collective-permute-start.3 = (f32[136,128]{1,0:T(8,128)S(1)}, f32[136,128]{1,0:T(8,128)S(1)}, u32[]{:S(2)}, u32[]{:S(2)}) collective-permute-start(f32[136,128]{1,0:T(8,128)S(1)} %get-tuple-element.42), channel_id=1, source_target_pairs={{1,0},{2,1},{3,2},{4,3},{5,4},{6,5},{7,6},{8,7},{9,8},{10,9},{11,1... | collective-permute-start | bytes 208904 | tf_op jit(solution)/shard_map/ppermute | solution.py:295
  11.2 5.6 %collective-permute-start.1 = (f32[136,128]{1,0:T(8,128)S(1)}, f32[136,128]{1,0:T(8,128)S(1)}, u32[]{:S(2)}, u32[]{:S(2)}) collective-permute-start(f32[136,128]{1,0:T(8,128)S(1)} %get-tuple-element.37.after_ref), channel_id=1, source_target_pairs={{16,0},{32,16},{48,32},{64,48},{80,64},{96,80},{112,96},{128,112},... | collective-permute-start | bytes 208904 | tf_op jit(solution)/shard_map/ppermute | solution.py:295
  31.2 26.7 %all-to-all-start.1 = ((f32[16,8,128]{2,1,0:T(8,128)}), f32[16,8,128]{2,1,0:T(8,128)S(1)}, u32[]{:S(2)}, u32[]{:S(2)}) async-start(f32[16,8,128]{2,1,0:T(8,128)} %get-tuple-element.45), calls=%async_computation.1 | async-start | bytes 131072 | tf_op jit(solution)/shard_map/all_to_all | solution.py:340
  58.3 6.5 %collective-permute-start.4 = (bf16[384,128]{1,0:T(8,128)(2,1)S(1)}, bf16[384,128]{1,0:T(8,128)(2,1)S(1)}, u32[]{:S(2)}, u32[]{:S(2)}) collective-permute-start(bf16[384,128]{1,0:T(8,128)(2,1)S(1)} %get-tuple-element.49), channel_id=1, source_target_pairs={{0,16},{16,32},{32,48},{48,64},{64,80},{80,96},{96,112},{112,128},... | collective-permute-start | bytes 294920 | tf_op jit(solution)/shard_map/ppermute | solution.py:295
  62.9 5.9 %collective-permute-start.5 = (bf16[384,128]{1,0:T(8,128)(2,1)S(1)}, bf16[384,128]{1,0:T(8,128)(2,1)S(1)}, u32[]{:S(2)}, u32[]{:S(2)}) collective-permute-start(bf16[384,128]{1,0:T(8,128)(2,1)S(1)} %get-tuple-element.50), channel_id=1, source_target_pairs={{16,0},{32,16},{48,32},{64,48},{80,64},{96,80},{112,96},{128,112},... | collective-permute-start | bytes 294920 | tf_op jit(solution)/shard_map/ppermute | solution.py:295
  69.0 5.5 %collective-permute-start.6 = (bf16[384,128]{1,0:T(8,128)(2,1)S(1)}, bf16[384,128]{1,0:T(8,128)(2,1)S(1)}, u32[]{:S(2)}, u32[]{:S(2)}) collective-permute-start(bf16[384,128]{1,0:T(8,128)(2,1)S(1)} %get-tuple-element.52), channel_id=1, source_target_pairs={{0,1},{1,2},{2,3},{3,4},{4,5},{5,6},{6,7},{7,8},{8,9},{9,10},{10,1... | collective-permute-start | bytes 294920 | tf_op jit(solution)/shard_map/ppermute | solution.py:295
  72.5 7.5 %collective-permute-start.7 = (bf16[384,128]{1,0:T(8,128)(2,1)S(1)}, bf16[384,128]{1,0:T(8,128)(2,1)S(1)}, u32[]{:S(2)}, u32[]{:S(2)}) collective-permute-start(bf16[384,128]{1,0:T(8,128)(2,1)S(1)} %get-tuple-element.53), channel_id=1, source_target_pairs={{1,0},{2,1},{3,2},{4,3},{5,4},{6,5},{7,6},{8,7},{9,8},{10,9},{11,1... | collective-permute-start | bytes 294920 | tf_op jit(solution)/shard_map/ppermute | solution.py:295
  93.1 16.9 %all-to-all-start.3 = ((f32[16,8,128]{2,1,0:T(8,128)}), f32[16,8,128]{2,1,0:T(8,128)S(1)}, u32[]{:S(2)}, u32[]{:S(2)}) async-start(f32[16,8,128]{2,1,0:T(8,128)} %shard_map.95), calls=%async_computation.3 | async-start | bytes 131072 | tf_op jit(solution)/shard_map/all_to_all | solution.py:340
  110.5 6.5 %collective-permute-start.8 = (bf16[240,128]{1,0:T(8,128)(2,1)S(1)}, bf16[240,128]{1,0:T(8,128)(2,1)S(1)}, u32[]{:S(2)}, u32[]{:S(2)}) collective-permute-start(bf16[240,128]{1,0:T(8,128)(2,1)S(1)} %get-tuple-element.60), channel_id=1, source_target_pairs={{0,16},{16,32},{32,48},{48,64},{64,80},{80,96},{96,112},{112,128},... | collective-permute-start | bytes 184328 | tf_op jit(solution)/shard_map/ppermute | solution.py:295
  115.1 5.5 %collective-permute-start.9 = (bf16[240,128]{1,0:T(8,128)(2,1)S(1)}, bf16[240,128]{1,0:T(8,128)(2,1)S(1)}, u32[]{:S(2)}, u32[]{:S(2)}) collective-permute-start(bf16[240,128]{1,0:T(8,128)(2,1)S(1)} %get-tuple-element.61), channel_id=1, source_target_pairs={{16,0},{32,16},{48,32},{64,48},{80,64},{96,80},{112,96},{128,112},... | collective-permute-start | bytes 184328 | tf_op jit(solution)/shard_map/ppermute | solution.py:295
  120.7 5.5 %collective-permute-start.10 = (bf16[240,128]{1,0:T(8,128)(2,1)S(1)}, bf16[240,128]{1,0:T(8,128)(2,1)S(1)}, u32[]{:S(2)}, u32[]{:S(2)}) collective-permute-start(bf16[240,128]{1,0:T(8,128)(2,1)S(1)} %get-tuple-element.63), channel_id=1, source_target_pairs={{0,1},{1,2},{2,3},{3,4},{4,5},{5,6},{6,7},{7,8},{8,9},{9,10},{10,1... | collective-permute-start | bytes 184328 | tf_op jit(solution)/shard_map/ppermute | solution.py:295
  124.3 7.1 %collective-permute-start.11 = (bf16[240,128]{1,0:T(8,128)(2,1)S(1)}, bf16[240,128]{1,0:T(8,128)(2,1)S(1)}, u32[]{:S(2)}, u32[]{:S(2)}) collective-permute-start(bf16[240,128]{1,0:T(8,128)(2,1)S(1)} %get-tuple-element.64), channel_id=1, source_target_pairs={{1,0},{2,1},{3,2},{4,3},{5,4},{6,5},{7,6},{8,7},{9,8},{10,9},{11,1... | collective-permute-start | bytes 184328 | tf_op jit(solution)/shard_map/ppermute | solution.py:295

commit v5 on v4

--- a/solution.py
+++ b/solution.py
@@ -61,6 +61,16 @@
         copy.wait()
 
 
+def by_chip(lower, upper):
+    second = lax.axis_index("core") == 1
+    return jnp.where(second, lower, upper), jnp.where(second, upper, lower)
+
+
+def by_side(inner, outer):
+    second = lax.axis_index("core") == 1
+    return jnp.where(second, inner, outer), jnp.where(second, outer, inner)
+
+
 def order_rows(width, rows_hbm, places_hbm, basis_hbm, after_ref, out_ref, basis_ref, rows, places, tiles, sems):
     fetch([(rows_hbm, rows), (places_hbm, places), (basis_hbm, basis_ref)], sems)
     n_targets = out_ref.shape[0]
@@ -82,7 +92,8 @@
 
 
 def make_edges(
-    values_hbm, stiff_hbm, lists_hbm, values_ref, stiff_ref, up_ref, down_ref, left_ref, right_ref, lists_ref, sems
+    values_hbm, stiff_hbm, lists_hbm, values_ref, stiff_ref, inner_ref, outer_ref, left_ref, right_ref,
+    lists_ref, up_ref, down_ref, sems,
 ):
     fetch([(values_hbm, values_ref), (stiff_hbm, stiff_ref), (lists_hbm, lists_ref)], sems)
     lists = lists_ref[...]
@@ -109,7 +120,9 @@
             one = source[:, first + layer : first + layer + 1]
             ref[pl.ds(STRIP + layer * CELLS, CELLS), :] = jnp.broadcast_to(one, (CELLS, LANES))
         code = (codes[side][side : side + 1] + 1).astype(F32)
-        ref[pl.ds(STRIP + 2 * CELLS, 8), 0:MARGIN] = jnp.broadcast_to(code, (8, MARGIN))
+        code = jnp.concatenate([code, jnp.zeros((1, LANES - MARGIN), F32)], axis=1)
+        ref[pl.ds(STRIP + 2 * CELLS, 8), :] = jnp.broadcast_to(code, (8, LANES))
+    inner_ref[...], outer_ref[...] = by_chip(up_ref[...], down_ref[...])
 
 
 def restrict(strips, beside, across_ref, along_ref, basis_ref, sub_ref):
@@ -119,9 +132,10 @@
 
 
 def start_pass(
-    values_ref, stiff_ref, basis_ref, ordered_ref, up_ref, down_ref, left_ref, right_ref,
-    field_ref, diagonal_ref, across_ref, along_ref, sub_ref, both_ref,
+    values_ref, stiff_ref, basis_ref, ordered_ref, inner_ref, outer_ref, left_ref, right_ref,
+    field_ref, diagonal_ref, across_ref, along_ref, sub_ref, both_ref, up_ref, down_ref,
 ):
+    up_ref[...], down_ref[...] = by_side(inner_ref[...], outer_ref[...])
     turned = stiff_ref[...].T
     field_ref[...] = jnp.zeros_like(field_ref)
     diagonal_ref[...] = jnp.full(diagonal_ref.shape, 4.0, F32)
@@ -196,7 +210,7 @@
         patch_ref[p, :] = matmul(inverse[p, :], sub_ref[...])
 
 
-def spread(depth, local_ref, basis_ref, parts_ref, across_ref, along_ref, field_ref, up_ref, down_ref, patch):
+def spread(depth, local_ref, basis_ref, parts_ref, across_ref, along_ref, field_ref, inner_ref, outer_ref, patch):
     coarse = jnp.sum(parts_ref[...], axis=0).astype(BF16)
     patch[...] = local_ref[...] + matmul(basis_ref[...], coarse, (0, 0))
     field_ref[...] = jnp.zeros_like(field_ref)
@@ -212,16 +226,18 @@
             field_ref[pl.ds(at(c, layer - 2), CELLS), :] = across[n : n + CELLS]
             field_ref[pl.ds(at(c, layer + CELLS), CELLS), :] = across[STRIP + n : STRIP + n + CELLS]
         part = part_of(depth)
-        up_ref[c * part : (c + 1) * part] = field_ref[pl.ds(at(c, -2), part), :].astype(BF16)
-        down_ref[c * part : (c + 1) * part] = field_ref[pl.ds(at(c, CELLS - depth), part), :].astype(BF16)
-
-
-def add_across(depth, field_ref, up_ref, down_ref, out_ref, left_ref, right_ref, strip):
+        inner, outer = by_chip(field_ref[pl.ds(at(c, -2), part), :], field_ref[pl.ds(at(c, CELLS - depth), part), :])
+        inner_ref[c * part : (c + 1) * part] = inner.astype(BF16)
+        outer_ref[c * part : (c + 1) * part] = outer.astype(BF16)
+
+
+def add_across(depth, field_ref, inner_ref, outer_ref, out_ref, left_ref, right_ref, strip):
     part, layers = part_of(depth), depth + 2
     out_ref[...] = field_ref[...]
     for c in range(COMPONENTS):
-        for first, ref in ((-depth, up_ref), (CELLS - 2, down_ref)):
-            came = ref[c * part : (c + 1) * part].astype(F32)
+        rows = slice(c * part, (c + 1) * part)
+        up, down = by_side(inner_ref[rows].astype(F32), outer_ref[rows].astype(F32))
+        for first, came in ((-depth, up), (CELLS - 2, down)):
             out_ref[pl.ds(at(c, first), layers * SIDE), :] += came[: layers * SIDE]
     for first, ref in ((-2, left_ref), (CELLS - depth, right_ref)):
         for c in range(COMPONENTS):
@@ -295,6 +311,17 @@
     return lax.ppermute(upper, axis, forward), lax.ppermute(lower, axis, backward)
 
 
+def trade_by_chip(inner, outer):
+    count = lax.axis_size(GX)
+
+    def swap(message, start):
+        pairs = [(i, i + 1) for i in range(start, count - 1, 2)]
+        return lax.ppermute(message, GX, pairs + [(target, source) for source, target in pairs])
+
+    outer = swap(outer, 1)
+    return swap(inner, 0), outer
+
+
 GX, GY = ("z", "core"), "gy"
 FIRST, SECOND = ("core", "gy"), "z"
 
@@ -309,16 +336,16 @@
     own, field, edge = ((OWN, LANES), F32), ((FIELD, LANES), F32), ((EDGE, LANES), F32)
     sub_kind, patch = ((OWN + 4 * MARGIN, LANES), BF16), ((OWN + 4 * MARGIN, LANES), F32)
     copies, sums = ((n_first, k, LANES), F32), ((n_second, k, LANES), F32)
-    values, stiffness, up, down, left, right = call(
+    values, stiffness, inner, outer, left, right = call(
         make_edges, [own, (stiffness.shape, F32), *[edge] * 4], values, stiffness, lists, fetched=3,
-        scratch=[(lists.shape, jnp.int32)],
+        scratch=[(lists.shape, jnp.int32), edge, edge],
     )
     ordered, basis = call(
         functools.partial(order_rows, n_second * k), [copies, (basis.shape, BF16)],
-        coarse_rows[0, 0], partition_map, basis, up, fetched=3,
+        coarse_rows[0, 0], partition_map, basis, inner, fetched=3,
         scratch=[((k, order), BF16), pltpu.SMEM(partition_map.shape, jnp.int32), ((order // LANES, k, LANES), F32)],
     )
-    up, down = trade(up, down, GX)
+    inner, outer = trade_by_chip(inner, outer)
     left, right = trade(left, right, GY)
     ambient, diagonal, across, along, sub, both = call(
         start_pass,
@@ -326,7 +353,7 @@
             field, ((PLANE, LANES), F32), ((2 * STRIP, 2 * MARGIN), BF16), ((BESIDE, 2 * MARGIN), BF16), sub_kind,
             ((n_first, 2 * k, LANES), BF16),
         ],
-        values, stiffness, basis, ordered, up, down, left, right,
+        values, stiffness, basis, ordered, inner, outer, left, right, scratch=[edge, edge],
     )
 
     def correct(depth, sub, parts):
@@ -335,12 +362,12 @@
             apply_inverse, [patch], inverse, sub, fetched=1, copies=4, scratch=[(inverse.shape, BF16)],
             cost=(inverse.size * LANES * 2, inverse.size * 2),
         )
-        y, to_up, to_down = call(
+        y, inner, outer = call(
             functools.partial(spread, depth), [field, part, part],
             local, basis, swap(parts, SECOND), across, along, scratch=[patch],
         )
         y, to_left, to_right = call(
-            functools.partial(add_across, depth), [field, part, part], y, *trade(to_up, to_down, GX),
+            functools.partial(add_across, depth), [field, part, part], y, *trade_by_chip(inner, outer),
             scratch=[((part_of(depth), LANES), F32)],
         )
         return (y, *trade(to_left, to_right, GY))

time: 133 us -> 131 us (0.985)
  waiting for transfers between devices: 38.2 us -> 36.7 us
    ppermute x0 -> x6, starting transfers between devices: none -> 19.1 us  [swap(): lax.ppermute(message, GX, pairs + [(target, source) for source, target in...]
    ppermute x6 -> x3, starting transfers between devices: 23.5 us -> 10 us  [trade(): lax.ppermute(upper, axis, forward)]
    ppermute x6 -> x3, waiting for transfers between devices: 19.4 us -> 11.2 us  [trade(): lax.ppermute(lower, axis, backward)]
    ppermute x0 -> x6, waiting for transfers between devices: none -> 6.79 us  [swap(): lax.ppermute(message, GX, pairs + [(target, source) for source, target in...]
    ppermute x6 -> x3, starting transfers between devices: 11.8 us -> 6 us  [trade(): lax.ppermute(lower, axis, backward)]
  transfers between devices with their start and end apart: 14 -> 14, of which waited for: 8 -> 7; matrix products, arithmetic and copies ran while one was open for 0% -> 0% of each run, Pallas kernels for 5% -> 5%
where the time goes in v5:
time: 131 us; the launch traced here: 130 us
  starting transfers between devices  55.2 us (42%)
  waiting for transfers between devices  36.7 us (28%)
  blocking collectives  24.3 us (19%)
  Pallas kernels  13.3 us (10%)
    all_to_all x2, starting transfers between devices, correct(): swap(parts, SECOND)  20.2 us
    ppermute x6, starting transfers between devices, swap(): lax.ppermute(message, GX, pairs + [(target, source) for source, target in...  19.1 us
    all_to_all x2, waiting for transfers between devices, correct(): swap(parts, SECOND)  18.7 us
    pallas_call x13, Pallas kernels, call(): pl.pallas_call(kernel, out_shape=[jax.ShapeDtypeStruct(shape, kind) for s...  13.3 us
    all_to_all x1, blocking collectives, per_device(): swap(both, FIRST)  12.8 us
    all_to_all x1, blocking collectives, per_device(): [parts] = call(cross_second, [sums], crossing, swap(coarse, FIRST))  11.5 us
    ppermute x3, waiting for transfers between devices, trade(): lax.ppermute(lower, axis, backward)  11.2 us
    ppermute x3, starting transfers between devices, trade(): lax.ppermute(upper, axis, forward)  10 us
  transfers between devices with their start and end apart: 14, of which 7 were waited for; matrix products, arithmetic and copies ran while one was open for 0% of the time, Pallas kernels for 5%

profile of v5, /device:TPU:7, one launch (start us, length us, event | category | flops | bytes accessed | tf_op | source)
XLA Modules:
  0.0 130.4 jit_solution(6615015515266262290)
XLA Ops:
  0.6 1.2 shard_map.86
  1.8 4.1 %collective-permute-start.1 = (f32[136,128]{1,0:T(8,128)S(1)}, f32[136,128]{1,0:T(8,128)S(1)}, u32[]{:S(2)}, u32[]{:S(2)}) collective-permute-start(f32[136,128]{1,0:T(8,128)S(1)} %get-tuple-element.40), channel_id=1, source_target_pairs={{16,32},{48,64},{80,96},{112,128},{144,160},{176,192},{208,224},{2... | collective-permute-start | bytes 208904 | tf_op jit(solution)/shard_map/ppermute | solution.py:319
  6.0 3.1 %collective-permute-start.2 = (f32[136,128]{1,0:T(8,128)S(1)}, f32[136,128]{1,0:T(8,128)S(1)}, u32[]{:S(2)}, u32[]{:S(2)}) collective-permute-start(f32[136,128]{1,0:T(8,128)S(1)} %get-tuple-element.41), channel_id=1, source_target_pairs={{0,1},{1,2},{2,3},{3,4},{4,5},{5,6},{6,7},{7,8},{8,9},{9,10},{10,1... | collective-permute-start | bytes 208904 | tf_op jit(solution)/shard_map/ppermute | solution.py:311
  9.1 2.2 %collective-permute-start.3 = (f32[136,128]{1,0:T(8,128)S(1)}, f32[136,128]{1,0:T(8,128)S(1)}, u32[]{:S(2)}, u32[]{:S(2)}) collective-permute-start(f32[136,128]{1,0:T(8,128)S(1)} %get-tuple-element.42), channel_id=1, source_target_pairs={{1,0},{2,1},{3,2},{4,3},{5,4},{6,5},{7,6},{8,7},{9,8},{10,9},{11,1... | collective-permute-start | bytes 208904 | tf_op jit(solution)/shard_map/ppermute | solution.py:311
  11.3 1.9 %collective-permute-start = (f32[136,128]{1,0:T(8,128)S(1)}, f32[136,128]{1,0:T(8,128)S(1)}, u32[]{:S(2)}, u32[]{:S(2)}) collective-permute-start(f32[136,128]{1,0:T(8,128)S(1)} %get-tuple-element.37.after_ref), channel_id=1, source_target_pairs={{0,16},{32,48},{64,80},{96,112},{128,144},{160,176},{192,208},{224... | collective-permute-start | bytes 208904 | tf_op jit(solution)/shard_map/ppermute | solution.py:319
  13.2 2.5 %shard_map.87 = (f32[32,8,128]{2,1,0:T(8,128)S(1)}, bf16[8,1024]{1,0:T(8,128)(2,1)S(1)}) custom-call(bf16[8,4096]{1,0:T(8,128)(2,1)} %bitcast.10, s32[512]{0:T(512)} %places_hbm.1, bf16[8,1024]{1,0:T(8,128)(2,1)} %bitcast.11, f32[136,128]{1,0:T(8,128)S(1)} %get-tuple-element.37.after_ref), custom_call_target="tpu_custom_call" | custom-call | tf_op jit(solution)/shard_map/pallas_call | solution.py:45
  15.7 0.5 collective-permute-done.3.right_ref
  16.3 0.5 shard_map.88
  16.8 12.8 %all_to_all.20.both_ref = bf16[32,16,128]{2,1,0:T(8,128)(2,1)S(1)} all-to-all(bf16[32,16,128]{2,1,0:T(8,128)(2,1)S(1)} %get-tuple-element.44), channel_id=1, replica_groups=mesh['z'=16,'core'=2,'gy'=16] {'core','gy'}, dimensions={0} | all-to-all | bytes 262144 | tf_op jit(solution)/shard_map/all_to_all | solution.py:375
  29.6 0.8 shard_map.90
  30.4 14.9 %all-to-all-start.1 = ((f32[16,8,128]{2,1,0:T(8,128)}), f32[16,8,128]{2,1,0:T(8,128)S(1)}, u32[]{:S(2)}, u32[]{:S(2)}) async-start(f32[16,8,128]{2,1,0:T(8,128)} %get-tuple-element.45), calls=%async_computation.1 | async-start | bytes 131072 | tf_op jit(solution)/shard_map/all_to_all | solution.py:367
  45.4 2.2 %shard_map.89.local_ref = f32[1024,128]{1,0:T(8,128)S(1)} custom-call(bf16[1024,1024]{1,0:T(8,128)(2,1)} %bitcast.7, bf16[1024,128]{1,0:T(8,128)(2,1)S(1)} %get-tuple-element.43.sub_ref), custom_call_target="tpu_custom_call" | custom-call | flops 268435456 | bytes 2097152 | tf_op jit(solution)/shard_map/pallas_call | solution.py:45
  47.6 9.4 %all-to-all-done.1.parts_ref = f32[16,8,128]{2,1,0:T(8,128)S(1)} async-done(((f32[16,8,128]{2,1,0:T(8,128)}), f32[16,8,128]{2,1,0:T(8,128)S(1)}, u32[]{:S(2)}, u32[]{:S(2)}) %all-to-all-start.1) | async-done | bytes 65568 | tf_op jit(solution)/shard_map/all_to_all | solution.py:367
  57.4 4.2 %collective-permute-start.4 = (bf16[384,128]{1,0:T(8,128)(2,1)S(1)}, bf16[384,128]{1,0:T(8,128)(2,1)S(1)}, u32[]{:S(2)}, u32[]{:S(2)}) collective-permute-start(bf16[384,128]{1,0:T(8,128)(2,1)S(1)} %get-tuple-element.49), channel_id=1, source_target_pairs={{0,16},{32,48},{64,80},{96,112},{128,144},{160,176},{192,208},{224... | collective-permute-start | bytes 294920 | tf_op jit(solution)/shard_map/ppermute | solution.py:319
  61.6 2.3 %collective-permute-start.5 = (bf16[384,128]{1,0:T(8,128)(2,1)S(1)}, bf16[384,128]{1,0:T(8,128)(2,1)S(1)}, u32[]{:S(2)}, u32[]{:S(2)}) collective-permute-start(bf16[384,128]{1,0:T(8,128)(2,1)S(1)} %get-tuple-element.50), channel_id=1, source_target_pairs={{16,32},{48,64},{80,96},{112,128},{144,160},{176,192},{208,224},{2... | collective-permute-start | bytes 294920 | tf_op jit(solution)/shard_map/ppermute | solution.py:319
  64.0 3.6 %collective-permute-done.5.outer_ref = bf16[384,128]{1,0:T(8,128)(2,1)S(1)} collective-permute-done((bf16[384,128]{1,0:T(8,128)(2,1)S(1)}, bf16[384,128]{1,0:T(8,128)(2,1)S(1)}, u32[]{:S(2)}, u32[]{:S(2)}) %collective-permute-start.5) | collective-permute-done | bytes 98336 | tf_op jit(solution)/shard_map/ppermute | solution.py:319
  67.7 3.4 %collective-permute-start.6 = (bf16[384,128]{1,0:T(8,128)(2,1)S(1)}, bf16[384,128]{1,0:T(8,128)(2,1)S(1)}, u32[]{:S(2)}, u32[]{:S(2)}) collective-permute-start(bf16[384,128]{1,0:T(8,128)(2,1)S(1)} %get-tuple-element.52), channel_id=1, source_target_pairs={{0,1},{1,2},{2,3},{3,4},{4,5},{5,6},{6,7},{7,8},{8,9},{9,10},{10,1... | collective-permute-start | bytes 294920 | tf_op jit(solution)/shard_map/ppermute | solution.py:311
  71.2 1.9 %collective-permute-start.7 = (bf16[384,128]{1,0:T(8,128)(2,1)S(1)}, bf16[384,128]{1,0:T(8,128)(2,1)S(1)}, u32[]{:S(2)}, u32[]{:S(2)}) collective-permute-start(bf16[384,128]{1,0:T(8,128)(2,1)S(1)} %get-tuple-element.53), channel_id=1, source_target_pairs={{1,0},{2,1},{3,2},{4,3},{5,4},{6,5},{7,6},{8,7},{9,8},{10,9},{11,1... | collective-permute-start | bytes 294920 | tf_op jit(solution)/shard_map/ppermute | solution.py:311
  73.1 5.5 %collective-permute-done.7.right_ref = bf16[384,128]{1,0:T(8,128)(2,1)S(1)} collective-permute-done((bf16[384,128]{1,0:T(8,128)(2,1)S(1)}, bf16[384,128]{1,0:T(8,128)(2,1)S(1)}, u32[]{:S(2)}, u32[]{:S(2)}) %collective-permute-start.7) | collective-permute-done | bytes 98336 | tf_op jit(solution)/shard_map/ppermute | solution.py:311
  78.6 0.6 shard_map.93
  79.3 11.5 %all_to_all.21.column_ref = f32[32,8,128]{2,1,0:T(8,128)S(1)} all-to-all(f32[32,8,128]{2,1,0:T(8,128)S(1)} %get-tuple-element.58), channel_id=1, replica_groups=mesh['z'=16,'core'=2,'gy'=16] {'core','gy'}, dimensions={0} | all-to-all | bytes 262144 | tf_op jit(solution)/shard_map/all_to_all | solution.py:380
  90.8 0.8 shard_map.95
  91.6 5.2 %all-to-all-start.3 = ((f32[16,8,128]{2,1,0:T(8,128)}), f32[16,8,128]{2,1,0:T(8,128)S(1)}, u32[]{:S(2)}, u32[]{:S(2)}) async-start(f32[16,8,128]{2,1,0:T(8,128)} %shard_map.95), calls=%async_computation.3 | async-start | bytes 131072 | tf_op jit(solution)/shard_map/all_to_all | solution.py:367
  96.9 2.2 %shard_map.94.local_ref = f32[1024,128]{1,0:T(8,128)S(1)} custom-call(bf16[1024,1024]{1,0:T(8,128)(2,1)} %bitcast.8, bf16[1024,128]{1,0:T(8,128)(2,1)S(1)} %get-tuple-element.56.sub_ref), custom_call_target="tpu_custom_call" | custom-call | flops 268435456 | bytes 2097152 | tf_op jit(solution)/shard_map/pallas_call | solution.py:45
  99.1 9.4 %all-to-all-done.3.parts_ref = f32[16,8,128]{2,1,0:T(8,128)S(1)} async-done(((f32[16,8,128]{2,1,0:T(8,128)}), f32[16,8,128]{2,1,0:T(8,128)S(1)}, u32[]{:S(2)}, u32[]{:S(2)}) %all-to-all-start.3) | async-done | bytes 65568 | tf_op jit(solution)/shard_map/all_to_all | solution.py:367
  108.9 4.2 %collective-permute-start.8 = (bf16[240,128]{1,0:T(8,128)(2,1)S(1)}, bf16[240,128]{1,0:T(8,128)(2,1)S(1)}, u32[]{:S(2)}, u32[]{:S(2)}) collective-permute-start(bf16[240,128]{1,0:T(8,128)(2,1)S(1)} %get-tuple-element.60), channel_id=1, source_target_pairs={{0,16},{32,48},{64,80},{96,112},{128,144},{160,176},{192,208},{224... | collective-permute-start | bytes 184328 | tf_op jit(solution)/shard_map/ppermute | solution.py:319
  113.1 2.3 %collective-permute-start.9 = (bf16[240,128]{1,0:T(8,128)(2,1)S(1)}, bf16[240,128]{1,0:T(8,128)(2,1)S(1)}, u32[]{:S(2)}, u32[]{:S(2)}) collective-permute-start(bf16[240,128]{1,0:T(8,128)(2,1)S(1)} %get-tuple-element.61), channel_id=1, source_target_pairs={{16,32},{48,64},{80,96},{112,128},{144,160},{176,192},{208,224},{2... | collective-permute-start | bytes 184328 | tf_op jit(solution)/shard_map/ppermute | solution.py:319
  115.5 3.2 %collective-permute-done.9.outer_ref = bf16[240,128]{1,0:T(8,128)(2,1)S(1)} collective-permute-done((bf16[240,128]{1,0:T(8,128)(2,1)S(1)}, bf16[240,128]{1,0:T(8,128)(2,1)S(1)}, u32[]{:S(2)}, u32[]{:S(2)}) %collective-permute-start.9) | collective-permute-done | bytes 61472 | tf_op jit(solution)/shard_map/ppermute | solution.py:319
  118.8 3.4 %collective-permute-start.10 = (bf16[240,128]{1,0:T(8,128)(2,1)S(1)}, bf16[240,128]{1,0:T(8,128)(2,1)S(1)}, u32[]{:S(2)}, u32[]{:S(2)}) collective-permute-start(bf16[240,128]{1,0:T(8,128)(2,1)S(1)} %get-tuple-element.63), channel_id=1, source_target_pairs={{0,1},{1,2},{2,3},{3,4},{4,5},{5,6},{6,7},{7,8},{8,9},{9,10},{10,1... | collective-permute-start | bytes 184328 | tf_op jit(solution)/shard_map/ppermute | solution.py:311
  122.2 1.9 %collective-permute-start.11 = (bf16[240,128]{1,0:T(8,128)(2,1)S(1)}, bf16[240,128]{1,0:T(8,128)(2,1)S(1)}, u32[]{:S(2)}, u32[]{:S(2)}) collective-permute-start(bf16[240,128]{1,0:T(8,128)(2,1)S(1)} %get-tuple-element.64), channel_id=1, source_target_pairs={{1,0},{2,1},{3,2},{4,3},{5,4},{6,5},{7,6},{8,7},{9,8},{10,9},{11,1... | collective-permute-start | bytes 184328 | tf_op jit(solution)/shard_map/ppermute | solution.py:311
  124.2 5.1 %collective-permute-done.11.right_ref = bf16[240,128]{1,0:T(8,128)(2,1)S(1)} collective-permute-done((bf16[240,128]{1,0:T(8,128)(2,1)S(1)}, bf16[240,128]{1,0:T(8,128)(2,1)S(1)}, u32[]{:S(2)}, u32[]{:S(2)}) %collective-permute-start.11) | collective-permute-done | bytes 61472 | tf_op jit(solution)/shard_map/ppermute | solution.py:311
  129.3 1.1 shard_map.98
  (11 shorter events, 1.2 us)
Async XLA Ops:
  1.8 13.8 %collective-permute-start.1 = (f32[136,128]{1,0:T(8,128)S(1)}, f32[136,128]{1,0:T(8,128)S(1)}, u32[]{:S(2)}, u32[]{:S(2)}) collective-permute-start(f32[136,128]{1,0:T(8,128)S(1)} %get-tuple-element.40), channel_id=1, source_target_pairs={{16,32},{48,64},{80,96},{112,128},{144,160},{176,192},{208,224},{2... | collective-permute-start | bytes 208904 | tf_op jit(solution)/shard_map/ppermute | solution.py:319
  6.0 9.7 %collective-permute-start.2 = (f32[136,128]{1,0:T(8,128)S(1)}, f32[136,128]{1,0:T(8,128)S(1)}, u32[]{:S(2)}, u32[]{:S(2)}) collective-permute-start(f32[136,128]{1,0:T(8,128)S(1)} %get-tuple-element.41), channel_id=1, source_target_pairs={{0,1},{1,2},{2,3},{3,4},{4,5},{5,6},{6,7},{7,8},{8,9},{9,10},{10,1... | collective-permute-start | bytes 208904 | tf_op jit(solution)/shard_map/ppermute | solution.py:311
  9.1 7.2 %collective-permute-start.3 = (f32[136,128]{1,0:T(8,128)S(1)}, f32[136,128]{1,0:T(8,128)S(1)}, u32[]{:S(2)}, u32[]{:S(2)}) collective-permute-start(f32[136,128]{1,0:T(8,128)S(1)} %get-tuple-element.42), channel_id=1, source_target_pairs={{1,0},{2,1},{3,2},{4,3},{5,4},{6,5},{7,6},{8,7},{9,8},{10,9},{11,1... | collective-permute-start | bytes 208904 | tf_op jit(solution)/shard_map/ppermute | solution.py:311
  11.3 5.0 %collective-permute-start = (f32[136,128]{1,0:T(8,128)S(1)}, f32[136,128]{1,0:T(8,128)S(1)}, u32[]{:S(2)}, u32[]{:S(2)}) collective-permute-start(f32[136,128]{1,0:T(8,128)S(1)} %get-tuple-element.37.after_ref), channel_id=1, source_target_pairs={{0,16},{32,48},{64,80},{96,112},{128,144},{160,176},{192,208},{224... | collective-permute-start | bytes 208904 | tf_op jit(solution)/shard_map/ppermute | solution.py:319
  30.4 26.5 %all-to-all-start.1 = ((f32[16,8,128]{2,1,0:T(8,128)}), f32[16,8,128]{2,1,0:T(8,128)S(1)}, u32[]{:S(2)}, u32[]{:S(2)}) async-start(f32[16,8,128]{2,1,0:T(8,128)} %get-tuple-element.45), calls=%async_computation.1 | async-start | bytes 131072 | tf_op jit(solution)/shard_map/all_to_all | solution.py:367
  57.4 6.5 %collective-permute-start.4 = (bf16[384,128]{1,0:T(8,128)(2,1)S(1)}, bf16[384,128]{1,0:T(8,128)(2,1)S(1)}, u32[]{:S(2)}, u32[]{:S(2)}) collective-permute-start(bf16[384,128]{1,0:T(8,128)(2,1)S(1)} %get-tuple-element.49), channel_id=1, source_target_pairs={{0,16},{32,48},{64,80},{96,112},{128,144},{160,176},{192,208},{224... | collective-permute-start | bytes 294920 | tf_op jit(solution)/shard_map/ppermute | solution.py:319
  61.6 5.9 %collective-permute-start.5 = (bf16[384,128]{1,0:T(8,128)(2,1)S(1)}, bf16[384,128]{1,0:T(8,128)(2,1)S(1)}, u32[]{:S(2)}, u32[]{:S(2)}) collective-permute-start(bf16[384,128]{1,0:T(8,128)(2,1)S(1)} %get-tuple-element.50), channel_id=1, source_target_pairs={{16,32},{48,64},{80,96},{112,128},{144,160},{176,192},{208,224},{2... | collective-permute-start | bytes 294920 | tf_op jit(solution)/shard_map/ppermute | solution.py:319
  67.7 5.4 %collective-permute-start.6 = (bf16[384,128]{1,0:T(8,128)(2,1)S(1)}, bf16[384,128]{1,0:T(8,128)(2,1)S(1)}, u32[]{:S(2)}, u32[]{:S(2)}) collective-permute-start(bf16[384,128]{1,0:T(8,128)(2,1)S(1)} %get-tuple-element.52), channel_id=1, source_target_pairs={{0,1},{1,2},{2,3},{3,4},{4,5},{5,6},{6,7},{7,8},{8,9},{9,10},{10,1... | collective-permute-start | bytes 294920 | tf_op jit(solution)/shard_map/ppermute | solution.py:311
  71.2 7.5 %collective-permute-start.7 = (bf16[384,128]{1,0:T(8,128)(2,1)S(1)}, bf16[384,128]{1,0:T(8,128)(2,1)S(1)}, u32[]{:S(2)}, u32[]{:S(2)}) collective-permute-start(bf16[384,128]{1,0:T(8,128)(2,1)S(1)} %get-tuple-element.53), channel_id=1, source_target_pairs={{1,0},{2,1},{3,2},{4,3},{5,4},{6,5},{7,6},{8,7},{9,8},{10,9},{11,1... | collective-permute-start | bytes 294920 | tf_op jit(solution)/shard_map/ppermute | solution.py:311
  91.6 16.8 %all-to-all-start.3 = ((f32[16,8,128]{2,1,0:T(8,128)}), f32[16,8,128]{2,1,0:T(8,128)S(1)}, u32[]{:S(2)}, u32[]{:S(2)}) async-start(f32[16,8,128]{2,1,0:T(8,128)} %shard_map.95), calls=%async_computation.3 | async-start | bytes 131072 | tf_op jit(solution)/shard_map/all_to_all | solution.py:367
  108.9 6.5 %collective-permute-start.8 = (bf16[240,128]{1,0:T(8,128)(2,1)S(1)}, bf16[240,128]{1,0:T(8,128)(2,1)S(1)}, u32[]{:S(2)}, u32[]{:S(2)}) collective-permute-start(bf16[240,128]{1,0:T(8,128)(2,1)S(1)} %get-tuple-element.60), channel_id=1, source_target_pairs={{0,16},{32,48},{64,80},{96,112},{128,144},{160,176},{192,208},{224... | collective-permute-start | bytes 184328 | tf_op jit(solution)/shard_map/ppermute | solution.py:319
  113.1 5.5 %collective-permute-start.9 = (bf16[240,128]{1,0:T(8,128)(2,1)S(1)}, bf16[240,128]{1,0:T(8,128)(2,1)S(1)}, u32[]{:S(2)}, u32[]{:S(2)}) collective-permute-start(bf16[240,128]{1,0:T(8,128)(2,1)S(1)} %get-tuple-element.61), channel_id=1, source_target_pairs={{16,32},{48,64},{80,96},{112,128},{144,160},{176,192},{208,224},{2... | collective-permute-start | bytes 184328 | tf_op jit(solution)/shard_map/ppermute | solution.py:319
  118.8 5.4 %collective-permute-start.10 = (bf16[240,128]{1,0:T(8,128)(2,1)S(1)}, bf16[240,128]{1,0:T(8,128)(2,1)S(1)}, u32[]{:S(2)}, u32[]{:S(2)}) collective-permute-start(bf16[240,128]{1,0:T(8,128)(2,1)S(1)} %get-tuple-element.63), channel_id=1, source_target_pairs={{0,1},{1,2},{2,3},{3,4},{4,5},{5,6},{6,7},{7,8},{8,9},{9,10},{10,1... | collective-permute-start | bytes 184328 | tf_op jit(solution)/shard_map/ppermute | solution.py:311
  122.2 7.1 %collective-permute-start.11 = (bf16[240,128]{1,0:T(8,128)(2,1)S(1)}, bf16[240,128]{1,0:T(8,128)(2,1)S(1)}, u32[]{:S(2)}, u32[]{:S(2)}) collective-permute-start(bf16[240,128]{1,0:T(8,128)(2,1)S(1)} %get-tuple-element.64), channel_id=1, source_target_pairs={{1,0},{2,1},{3,2},{4,3},{5,4},{6,5},{7,6},{8,7},{9,8},{10,9},{11,1... | collective-permute-start | bytes 184328 | tf_op jit(solution)/shard_map/ppermute | solution.py:311

commit v6 on v5

--- a/solution.py
+++ b/solution.py
@@ -231,7 +231,7 @@
         outer_ref[c * part : (c + 1) * part] = outer.astype(BF16)
 
 
-def add_across(depth, field_ref, inner_ref, outer_ref, out_ref, left_ref, right_ref, strip):
+def add_across(depth, field_ref, outer_ref, inner_ref, out_ref, left_ref, right_ref, strip):
     part, layers = part_of(depth), depth + 2
     out_ref[...] = field_ref[...]
     for c in range(COMPONENTS):
@@ -367,7 +367,7 @@
             local, basis, swap(parts, SECOND), across, along, scratch=[patch],
         )
         y, to_left, to_right = call(
-            functools.partial(add_across, depth), [field, part, part], y, *trade_by_chip(inner, outer),
+            functools.partial(add_across, depth), [field, part, part], y, *trade_by_chip(inner, outer)[::-1],
             scratch=[((part_of(depth), LANES), F32)],
         )
         return (y, *trade(to_left, to_right, GY))

time: 131 us -> 129 us (0.985); the launches traced: 130 us -> 127 us
  waiting for transfers between devices: 36.7 us -> 32.9 us
    ppermute x6, waiting for transfers between devices: 6.79 us -> 2.48 us  [swap(): lax.ppermute(message, GX, pairs + [(target, source) for source, target in...]
  transfers between devices with their start and end apart: 14 -> 14, of which waited for: 7 -> 9; matrix products, arithmetic and copies ran while one was open for 0% -> 0% of each run, Pallas kernels for 5% -> 5%
where the time goes in v6:
time: 129 us; the launch traced here: 127 us
  starting transfers between devices  54.3 us (42%)
  waiting for transfers between devices  32.9 us (26%)
  blocking collectives  25.6 us (20%)
  Pallas kernels  13.3 us (10%)
    ppermute x6, starting transfers between devices, swap(): lax.ppermute(message, GX, pairs + [(target, source) for source, target in...  19.1 us
    all_to_all x2, starting transfers between devices, correct(): swap(parts, SECOND)  19 us
    all_to_all x2, waiting for transfers between devices, correct(): swap(parts, SECOND)  18.7 us
    pallas_call x13, Pallas kernels, call(): pl.pallas_call(kernel, out_shape=[jax.ShapeDtypeStruct(shape, kind) for s...  13.3 us
    all_to_all x1, blocking collectives, per_device(): swap(both, FIRST)  12.8 us
    all_to_all x1, blocking collectives, per_device(): [parts] = call(cross_second, [sums], crossing, swap(coarse, FIRST))  12.8 us
    ppermute x3, waiting for transfers between devices, trade(): lax.ppermute(lower, axis, backward)  11 us
    ppermute x3, starting transfers between devices, trade(): lax.ppermute(upper, axis, forward)  10.2 us
  transfers between devices with their start and end apart: 14, of which 9 were waited for; matrix products, arithmetic and copies ran while one was open for 0% of the time, Pallas kernels for 5%

profile of v6, /device:TPU:7, one launch (start us, length us, event | category | flops | bytes accessed | tf_op | source)
XLA Modules:
  0.0 126.9 jit_solution(6019963806173058879)
XLA Ops:
  0.6 1.2 shard_map.86
  1.8 4.1 %collective-permute-start.1 = (f32[136,128]{1,0:T(8,128)S(1)}, f32[136,128]{1,0:T(8,128)S(1)}, u32[]{:S(2)}, u32[]{:S(2)}) collective-permute-start(f32[136,128]{1,0:T(8,128)S(1)} %get-tuple-element.40), channel_id=1, source_target_pairs={{16,32},{48,64},{80,96},{112,128},{144,160},{176,192},{208,224},{2... | collective-permute-start | bytes 208904 | tf_op jit(solution)/shard_map/ppermute | solution.py:319
  6.0 3.1 %collective-permute-start.2 = (f32[136,128]{1,0:T(8,128)S(1)}, f32[136,128]{1,0:T(8,128)S(1)}, u32[]{:S(2)}, u32[]{:S(2)}) collective-permute-start(f32[136,128]{1,0:T(8,128)S(1)} %get-tuple-element.41), channel_id=1, source_target_pairs={{0,1},{1,2},{2,3},{3,4},{4,5},{5,6},{6,7},{7,8},{8,9},{9,10},{10,1... | collective-permute-start | bytes 208904 | tf_op jit(solution)/shard_map/ppermute | solution.py:311
  9.1 2.2 %collective-permute-start.3 = (f32[136,128]{1,0:T(8,128)S(1)}, f32[136,128]{1,0:T(8,128)S(1)}, u32[]{:S(2)}, u32[]{:S(2)}) collective-permute-start(f32[136,128]{1,0:T(8,128)S(1)} %get-tuple-element.42), channel_id=1, source_target_pairs={{1,0},{2,1},{3,2},{4,3},{5,4},{6,5},{7,6},{8,7},{9,8},{10,9},{11,1... | collective-permute-start | bytes 208904 | tf_op jit(solution)/shard_map/ppermute | solution.py:311
  11.3 1.9 %collective-permute-start = (f32[136,128]{1,0:T(8,128)S(1)}, f32[136,128]{1,0:T(8,128)S(1)}, u32[]{:S(2)}, u32[]{:S(2)}) collective-permute-start(f32[136,128]{1,0:T(8,128)S(1)} %get-tuple-element.37.after_ref), channel_id=1, source_target_pairs={{0,16},{32,48},{64,80},{96,112},{128,144},{160,176},{192,208},{224... | collective-permute-start | bytes 208904 | tf_op jit(solution)/shard_map/ppermute | solution.py:319
  13.2 2.5 %shard_map.87 = (f32[32,8,128]{2,1,0:T(8,128)S(1)}, bf16[8,1024]{1,0:T(8,128)(2,1)S(1)}) custom-call(bf16[8,4096]{1,0:T(8,128)(2,1)} %bitcast.10, s32[512]{0:T(512)} %places_hbm.1, bf16[8,1024]{1,0:T(8,128)(2,1)} %bitcast.11, f32[136,128]{1,0:T(8,128)S(1)} %get-tuple-element.37.after_ref), custom_call_target="tpu_custom_call" | custom-call | tf_op jit(solution)/shard_map/pallas_call | solution.py:45
  15.7 0.5 collective-permute-done.3.right_ref
  16.8 12.8 %all_to_all.20.both_ref = bf16[32,16,128]{2,1,0:T(8,128)(2,1)S(1)} all-to-all(bf16[32,16,128]{2,1,0:T(8,128)(2,1)S(1)} %get-tuple-element.44), channel_id=1, replica_groups=mesh['z'=16,'core'=2,'gy'=16] {'core','gy'}, dimensions={0} | all-to-all | bytes 262144 | tf_op jit(solution)/shard_map/all_to_all | solution.py:375
  29.6 0.8 shard_map.90
  30.4 14.9 %all-to-all-start.1 = ((f32[16,8,128]{2,1,0:T(8,128)}), f32[16,8,128]{2,1,0:T(8,128)S(1)}, u32[]{:S(2)}, u32[]{:S(2)}) async-start(f32[16,8,128]{2,1,0:T(8,128)} %get-tuple-element.45), calls=%async_computation.1 | async-start | bytes 131072 | tf_op jit(solution)/shard_map/all_to_all | solution.py:367
  45.4 2.2 %shard_map.89.local_ref = f32[1024,128]{1,0:T(8,128)S(1)} custom-call(bf16[1024,1024]{1,0:T(8,128)(2,1)} %bitcast.7, bf16[1024,128]{1,0:T(8,128)(2,1)S(1)} %get-tuple-element.43.sub_ref), custom_call_target="tpu_custom_call" | custom-call | flops 268435456 | bytes 2097152 | tf_op jit(solution)/shard_map/pallas_call | solution.py:45
  47.6 9.4 %all-to-all-done.1.parts_ref = f32[16,8,128]{2,1,0:T(8,128)S(1)} async-done(((f32[16,8,128]{2,1,0:T(8,128)}), f32[16,8,128]{2,1,0:T(8,128)S(1)}, u32[]{:S(2)}, u32[]{:S(2)}) %all-to-all-start.1) | async-done | bytes 65568 | tf_op jit(solution)/shard_map/all_to_all | solution.py:367
  57.4 4.6 %collective-permute-start.4 = (bf16[384,128]{1,0:T(8,128)(2,1)S(1)}, bf16[384,128]{1,0:T(8,128)(2,1)S(1)}, u32[]{:S(2)}, u32[]{:S(2)}) collective-permute-start(bf16[384,128]{1,0:T(8,128)(2,1)S(1)} %get-tuple-element.49), channel_id=1, source_target_pairs={{16,32},{48,64},{80,96},{112,128},{144,160},{176,192},{208,224},{2... | collective-permute-start | bytes 294920 | tf_op jit(solution)/shard_map/ppermute | solution.py:319
  62.1 1.9 %collective-permute-start.5 = (bf16[384,128]{1,0:T(8,128)(2,1)S(1)}, bf16[384,128]{1,0:T(8,128)(2,1)S(1)}, u32[]{:S(2)}, u32[]{:S(2)}) collective-permute-start(bf16[384,128]{1,0:T(8,128)(2,1)S(1)} %get-tuple-element.50), channel_id=1, source_target_pairs={{0,16},{32,48},{64,80},{96,112},{128,144},{160,176},{192,208},{224... | collective-permute-start | bytes 294920 | tf_op jit(solution)/shard_map/ppermute | solution.py:319
  64.3 0.9 collective-permute-done.5.inner_ref
  65.4 3.5 %collective-permute-start.6 = (bf16[384,128]{1,0:T(8,128)(2,1)S(1)}, bf16[384,128]{1,0:T(8,128)(2,1)S(1)}, u32[]{:S(2)}, u32[]{:S(2)}) collective-permute-start(bf16[384,128]{1,0:T(8,128)(2,1)S(1)} %get-tuple-element.52), channel_id=1, source_target_pairs={{0,1},{1,2},{2,3},{3,4},{4,5},{5,6},{6,7},{7,8},{8,9},{9,10},{10,1... | collective-permute-start | bytes 294920 | tf_op jit(solution)/shard_map/ppermute | solution.py:311
  68.9 1.9 %collective-permute-start.7 = (bf16[384,128]{1,0:T(8,128)(2,1)S(1)}, bf16[384,128]{1,0:T(8,128)(2,1)S(1)}, u32[]{:S(2)}, u32[]{:S(2)}) collective-permute-start(bf16[384,128]{1,0:T(8,128)(2,1)S(1)} %get-tuple-element.53), channel_id=1, source_target_pairs={{1,0},{2,1},{3,2},{4,3},{5,4},{6,5},{7,6},{8,7},{9,8},{10,9},{11,1... | collective-permute-start | bytes 294920 | tf_op jit(solution)/shard_map/ppermute | solution.py:311
  70.8 0.7 collective-permute-done.6.left_ref
  71.5 5.3 %collective-permute-done.7.right_ref = bf16[384,128]{1,0:T(8,128)(2,1)S(1)} collective-permute-done((bf16[384,128]{1,0:T(8,128)(2,1)S(1)}, bf16[384,128]{1,0:T(8,128)(2,1)S(1)}, u32[]{:S(2)}, u32[]{:S(2)}) %collective-permute-start.7) | collective-permute-done | bytes 98336 | tf_op jit(solution)/shard_map/ppermute | solution.py:311
  76.8 0.6 shard_map.93
  77.5 12.8 %all_to_all.21.column_ref = f32[32,8,128]{2,1,0:T(8,128)S(1)} all-to-all(f32[32,8,128]{2,1,0:T(8,128)S(1)} %get-tuple-element.58), channel_id=1, replica_groups=mesh['z'=16,'core'=2,'gy'=16] {'core','gy'}, dimensions={0} | all-to-all | bytes 262144 | tf_op jit(solution)/shard_map/all_to_all | solution.py:380
  90.3 0.8 shard_map.95
  91.1 4.1 %all-to-all-start.3 = ((f32[16,8,128]{2,1,0:T(8,128)}), f32[16,8,128]{2,1,0:T(8,128)S(1)}, u32[]{:S(2)}, u32[]{:S(2)}) async-start(f32[16,8,128]{2,1,0:T(8,128)} %shard_map.95), calls=%async_computation.3 | async-start | bytes 131072 | tf_op jit(solution)/shard_map/all_to_all | solution.py:367
  95.2 2.2 %shard_map.94.local_ref = f32[1024,128]{1,0:T(8,128)S(1)} custom-call(bf16[1024,1024]{1,0:T(8,128)(2,1)} %bitcast.8, bf16[1024,128]{1,0:T(8,128)(2,1)S(1)} %get-tuple-element.56.sub_ref), custom_call_target="tpu_custom_call" | custom-call | flops 268435456 | bytes 2097152 | tf_op jit(solution)/shard_map/pallas_call | solution.py:45
  97.4 9.4 %all-to-all-done.3.parts_ref = f32[16,8,128]{2,1,0:T(8,128)S(1)} async-done(((f32[16,8,128]{2,1,0:T(8,128)}), f32[16,8,128]{2,1,0:T(8,128)S(1)}, u32[]{:S(2)}, u32[]{:S(2)}) %all-to-all-start.3) | async-done | bytes 65568 | tf_op jit(solution)/shard_map/all_to_all | solution.py:367
  107.3 4.6 %collective-permute-start.8 = (bf16[240,128]{1,0:T(8,128)(2,1)S(1)}, bf16[240,128]{1,0:T(8,128)(2,1)S(1)}, u32[]{:S(2)}, u32[]{:S(2)}) collective-permute-start(bf16[240,128]{1,0:T(8,128)(2,1)S(1)} %get-tuple-element.60), channel_id=1, source_target_pairs={{16,32},{48,64},{80,96},{112,128},{144,160},{176,192},{208,224},{2... | collective-permute-start | bytes 184328 | tf_op jit(solution)/shard_map/ppermute | solution.py:319
  111.9 1.9 %collective-permute-start.9 = (bf16[240,128]{1,0:T(8,128)(2,1)S(1)}, bf16[240,128]{1,0:T(8,128)(2,1)S(1)}, u32[]{:S(2)}, u32[]{:S(2)}) collective-permute-start(bf16[240,128]{1,0:T(8,128)(2,1)S(1)} %get-tuple-element.61), channel_id=1, source_target_pairs={{0,16},{32,48},{64,80},{96,112},{128,144},{160,176},{192,208},{224... | collective-permute-start | bytes 184328 | tf_op jit(solution)/shard_map/ppermute | solution.py:319
  113.8 1.2 collective-permute-done.9.inner_ref
  115.1 3.5 %collective-permute-start.10 = (bf16[240,128]{1,0:T(8,128)(2,1)S(1)}, bf16[240,128]{1,0:T(8,128)(2,1)S(1)}, u32[]{:S(2)}, u32[]{:S(2)}) collective-permute-start(bf16[240,128]{1,0:T(8,128)(2,1)S(1)} %get-tuple-element.63), channel_id=1, source_target_pairs={{0,1},{1,2},{2,3},{3,4},{4,5},{5,6},{6,7},{7,8},{8,9},{9,10},{10,1... | collective-permute-start | bytes 184328 | tf_op jit(solution)/shard_map/ppermute | solution.py:311
  118.7 1.9 %collective-permute-start.11 = (bf16[240,128]{1,0:T(8,128)(2,1)S(1)}, bf16[240,128]{1,0:T(8,128)(2,1)S(1)}, u32[]{:S(2)}, u32[]{:S(2)}) collective-permute-start(bf16[240,128]{1,0:T(8,128)(2,1)S(1)} %get-tuple-element.64), channel_id=1, source_target_pairs={{1,0},{2,1},{3,2},{4,3},{5,4},{6,5},{7,6},{8,7},{9,8},{10,9},{11,1... | collective-permute-start | bytes 184328 | tf_op jit(solution)/shard_map/ppermute | solution.py:311
  120.6 5.1 %collective-permute-done.11.right_ref = bf16[240,128]{1,0:T(8,128)(2,1)S(1)} collective-permute-done((bf16[240,128]{1,0:T(8,128)(2,1)S(1)}, bf16[240,128]{1,0:T(8,128)(2,1)S(1)}, u32[]{:S(2)}, u32[]{:S(2)}) %collective-permute-start.11) | collective-permute-done | bytes 61472 | tf_op jit(solution)/shard_map/ppermute | solution.py:311
  125.7 1.1 shard_map.98
  (11 shorter events, 2.1 us)
Async XLA Ops:
  1.8 13.8 %collective-permute-start.1 = (f32[136,128]{1,0:T(8,128)S(1)}, f32[136,128]{1,0:T(8,128)S(1)}, u32[]{:S(2)}, u32[]{:S(2)}) collective-permute-start(f32[136,128]{1,0:T(8,128)S(1)} %get-tuple-element.40), channel_id=1, source_target_pairs={{16,32},{48,64},{80,96},{112,128},{144,160},{176,192},{208,224},{2... | collective-permute-start | bytes 208904 | tf_op jit(solution)/shard_map/ppermute | solution.py:319
  6.0 9.7 %collective-permute-start.2 = (f32[136,128]{1,0:T(8,128)S(1)}, f32[136,128]{1,0:T(8,128)S(1)}, u32[]{:S(2)}, u32[]{:S(2)}) collective-permute-start(f32[136,128]{1,0:T(8,128)S(1)} %get-tuple-element.41), channel_id=1, source_target_pairs={{0,1},{1,2},{2,3},{3,4},{4,5},{5,6},{6,7},{7,8},{8,9},{9,10},{10,1... | collective-permute-start | bytes 208904 | tf_op jit(solution)/shard_map/ppermute | solution.py:311
  9.1 7.2 %collective-permute-start.3 = (f32[136,128]{1,0:T(8,128)S(1)}, f32[136,128]{1,0:T(8,128)S(1)}, u32[]{:S(2)}, u32[]{:S(2)}) collective-permute-start(f32[136,128]{1,0:T(8,128)S(1)} %get-tuple-element.42), channel_id=1, source_target_pairs={{1,0},{2,1},{3,2},{4,3},{5,4},{6,5},{7,6},{8,7},{9,8},{10,9},{11,1... | collective-permute-start | bytes 208904 | tf_op jit(solution)/shard_map/ppermute | solution.py:311
  11.3 5.0 %collective-permute-start = (f32[136,128]{1,0:T(8,128)S(1)}, f32[136,128]{1,0:T(8,128)S(1)}, u32[]{:S(2)}, u32[]{:S(2)}) collective-permute-start(f32[136,128]{1,0:T(8,128)S(1)} %get-tuple-element.37.after_ref), channel_id=1, source_target_pairs={{0,16},{32,48},{64,80},{96,112},{128,144},{160,176},{192,208},{224... | collective-permute-start | bytes 208904 | tf_op jit(solution)/shard_map/ppermute | solution.py:319
  30.4 26.5 %all-to-all-start.1 = ((f32[16,8,128]{2,1,0:T(8,128)}), f32[16,8,128]{2,1,0:T(8,128)S(1)}, u32[]{:S(2)}, u32[]{:S(2)}) async-start(f32[16,8,128]{2,1,0:T(8,128)} %get-tuple-element.45), calls=%async_computation.1 | async-start | bytes 131072 | tf_op jit(solution)/shard_map/all_to_all | solution.py:367
  57.4 6.9 %collective-permute-start.4 = (bf16[384,128]{1,0:T(8,128)(2,1)S(1)}, bf16[384,128]{1,0:T(8,128)(2,1)S(1)}, u32[]{:S(2)}, u32[]{:S(2)}) collective-permute-start(bf16[384,128]{1,0:T(8,128)(2,1)S(1)} %get-tuple-element.49), channel_id=1, source_target_pairs={{16,32},{48,64},{80,96},{112,128},{144,160},{176,192},{208,224},{2... | collective-permute-start | bytes 294920 | tf_op jit(solution)/shard_map/ppermute | solution.py:319
  62.1 3.2 %collective-permute-start.5 = (bf16[384,128]{1,0:T(8,128)(2,1)S(1)}, bf16[384,128]{1,0:T(8,128)(2,1)S(1)}, u32[]{:S(2)}, u32[]{:S(2)}) collective-permute-start(bf16[384,128]{1,0:T(8,128)(2,1)S(1)} %get-tuple-element.50), channel_id=1, source_target_pairs={{0,16},{32,48},{64,80},{96,112},{128,144},{160,176},{192,208},{224... | collective-permute-start | bytes 294920 | tf_op jit(solution)/shard_map/ppermute | solution.py:319
  65.4 6.1 %collective-permute-start.6 = (bf16[384,128]{1,0:T(8,128)(2,1)S(1)}, bf16[384,128]{1,0:T(8,128)(2,1)S(1)}, u32[]{:S(2)}, u32[]{:S(2)}) collective-permute-start(bf16[384,128]{1,0:T(8,128)(2,1)S(1)} %get-tuple-element.52), channel_id=1, source_target_pairs={{0,1},{1,2},{2,3},{3,4},{4,5},{5,6},{6,7},{7,8},{8,9},{9,10},{10,1... | collective-permute-start | bytes 294920 | tf_op jit(solution)/shard_map/ppermute | solution.py:311
  68.9 7.9 %collective-permute-start.7 = (bf16[384,128]{1,0:T(8,128)(2,1)S(1)}, bf16[384,128]{1,0:T(8,128)(2,1)S(1)}, u32[]{:S(2)}, u32[]{:S(2)}) collective-permute-start(bf16[384,128]{1,0:T(8,128)(2,1)S(1)} %get-tuple-element.53), channel_id=1, source_target_pairs={{1,0},{2,1},{3,2},{4,3},{5,4},{6,5},{7,6},{8,7},{9,8},{10,9},{11,1... | collective-permute-start | bytes 294920 | tf_op jit(solution)/shard_map/ppermute | solution.py:311
  91.1 15.7 %all-to-all-start.3 = ((f32[16,8,128]{2,1,0:T(8,128)}), f32[16,8,128]{2,1,0:T(8,128)S(1)}, u32[]{:S(2)}, u32[]{:S(2)}) async-start(f32[16,8,128]{2,1,0:T(8,128)} %shard_map.95), calls=%async_computation.3 | async-start | bytes 131072 | tf_op jit(solution)/shard_map/all_to_all | solution.py:367
  107.3 6.5 %collective-permute-start.8 = (bf16[240,128]{1,0:T(8,128)(2,1)S(1)}, bf16[240,128]{1,0:T(8,128)(2,1)S(1)}, u32[]{:S(2)}, u32[]{:S(2)}) collective-permute-start(bf16[240,128]{1,0:T(8,128)(2,1)S(1)} %get-tuple-element.60), channel_id=1, source_target_pairs={{16,32},{48,64},{80,96},{112,128},{144,160},{176,192},{208,224},{2... | collective-permute-start | bytes 184328 | tf_op jit(solution)/shard_map/ppermute | solution.py:319
  111.9 3.1 %collective-permute-start.9 = (bf16[240,128]{1,0:T(8,128)(2,1)S(1)}, bf16[240,128]{1,0:T(8,128)(2,1)S(1)}, u32[]{:S(2)}, u32[]{:S(2)}) collective-permute-start(bf16[240,128]{1,0:T(8,128)(2,1)S(1)} %get-tuple-element.61), channel_id=1, source_target_pairs={{0,16},{32,48},{64,80},{96,112},{128,144},{160,176},{192,208},{224... | collective-permute-start | bytes 184328 | tf_op jit(solution)/shard_map/ppermute | solution.py:319
  115.1 5.5 %collective-permute-start.10 = (bf16[240,128]{1,0:T(8,128)(2,1)S(1)}, bf16[240,128]{1,0:T(8,128)(2,1)S(1)}, u32[]{:S(2)}, u32[]{:S(2)}) collective-permute-start(bf16[240,128]{1,0:T(8,128)(2,1)S(1)} %get-tuple-element.63), channel_id=1, source_target_pairs={{0,1},{1,2},{2,3},{3,4},{4,5},{5,6},{6,7},{7,8},{8,9},{9,10},{10,1... | collective-permute-start | bytes 184328 | tf_op jit(solution)/shard_map/ppermute | solution.py:311
  118.7 7.1 %collective-permute-start.11 = (bf16[240,128]{1,0:T(8,128)(2,1)S(1)}, bf16[240,128]{1,0:T(8,128)(2,1)S(1)}, u32[]{:S(2)}, u32[]{:S(2)}) collective-permute-start(bf16[240,128]{1,0:T(8,128)(2,1)S(1)} %get-tuple-element.64), channel_id=1, source_target_pairs={{1,0},{2,1},{3,2},{4,3},{5,4},{6,5},{7,6},{8,7},{9,8},{10,9},{11,1... | collective-permute-start | bytes 184328 | tf_op jit(solution)/shard_map/ppermute | solution.py:311
